TPU v7x, 256 devices: a whole 4x4x8 slice. The times are simulated.
256 devices in a mesh: dp: 8 (over x, core), ctx: 32 (over y, z).
Axes of the slice: x: 4, y: 4, z: 8, core: 2. Of those that a mesh axis runs over, the one named last changes fastest.
Arguments:
- queries: bfloat16 [32768, 4096], P(('dp', 'ctx')), may hold values from -128 to 128
- keys: bfloat16 [32768, 512], P(('dp', 'ctx')), may hold values from -8 to 8
- values: bfloat16 [32768, 512], P(('dp', 'ctx')), may hold values from -6 to 6
- output_gradient: bfloat16 [32768, 4096], P(('dp', 'ctx')), may hold values from -6 to 6
- doc_lengths: int32 [8, 3], replicated, may hold values from 1 to 4, 8 in all within a row
- dest_group: int32 [64], replicated, may hold values from 0 to 7, as said below
- dest_slot: int32 [64], replicated, may hold values from 0 to 7, as said below
Outputs:
- grad_q: bfloat16 [32768, 4096], P(('dp', 'ctx'))
- key_gradient: bfloat16 [32768, 512], P(('dp', 'ctx'))
- value_gradient: bfloat16 [32768, 512], P(('dp', 'ctx'))
Inputs may be any that keep to these rules, and one draw needn't show every extreme that they name: `dest_group`: every group receives exactly 8 blocks, and each group sends to each group either none or exactly 2 of its blocks. The pair of dest_group and dest_slot differs for every block, so every slot of every group is filled once. `doc_lengths`: each row sums to 8; its longest document has exactly 4 blocks.
All inputs are finite; a program needn't handle non-finite values.
Results may differ from a plain program's by a relative error of at most 0.035.
Values may be sent and summed in bfloat16 or wider, within the bound.
No kernel may reach another device: no remote copies, remote signals or barrier semaphores. Data moves between devices by JAX's collectives and lax.ppermute only.
A program may use at most 128 MiB of HBM per device.

v0:
```python
import jax
import jax.numpy as jnp
from jax import lax
from jax.sharding import PartitionSpec as P

QUERY_HEADS = 32
KEY_HEADS = 4
HEAD_SIZE = 128
GROUP_BLOCKS = 8


NEG = -1e30


def route_tables(dest_group, dest_slot, n_dp, cap, group):
    dest_all = dest_group.reshape(n_dp, GROUP_BLOCKS)
    slot_all = dest_slot.reshape(n_dp, GROUP_BLOCKS)
    index_blk = jnp.arange(GROUP_BLOCKS, dtype=jnp.int32)
    earlier = (dest_all[:, :, None] == dest_all[:, None, :]) & (
        index_blk[None, None, :] < index_blk[None, :, None]
    )
    rank_all = jnp.sum(earlier.astype(jnp.int32), axis=2)
    peers = jnp.arange(n_dp, dtype=jnp.int32)
    places = jnp.arange(cap, dtype=jnp.int32)
    dest_mine = dest_all[group]
    rank_mine = rank_all[group]
    send_match = (dest_mine[None, None, :] == peers[:, None, None]) & (
        rank_mine[None, None, :] == places[None, :, None]
    )
    send_src = jnp.sum(send_match.astype(jnp.int32) * index_blk[None, None, :], axis=2)
    send_valid = jnp.any(send_match, axis=2)
    arriving = dest_all == group
    recv_match = arriving[None] & (slot_all[None] == index_blk[:, None, None])
    recv_src = jnp.sum(
        recv_match.astype(jnp.int32) * (peers[:, None] * cap + rank_all)[None], axis=(1, 2)
    )
    back_match = arriving[:, None, :] & (rank_all[:, None, :] == places[None, :, None])
    back_src = jnp.sum(back_match.astype(jnp.int32) * slot_all[:, None, :], axis=2)
    back_valid = jnp.any(back_match, axis=2)
    home_source = dest_mine * cap + rank_mine
    return (
        send_src.reshape(-1),
        send_valid.reshape(-1),
        recv_src,
        back_src.reshape(-1),
        back_valid.reshape(-1),
        home_source,
    )


def pack_rows(blocks, source, valid):
    picked = jnp.take(blocks, source, axis=0)
    return jnp.where(valid[:, None, None], picked, jnp.zeros_like(picked))


def attend(q_tile, k_tile, v_tile, g_tile, q_pos, k_pos, seg, score_scale):
    nblk, heads, token_rows, width = q_tile.shape
    keys_n = k_tile.shape[2]
    causal = k_pos[None, :] <= q_pos[:, None]

    def per_slot(carry, slot):
        key_gradient_rows, value_gradient_rows = carry
        query_input = q_tile[slot]
        upstream_gradient = g_tile[slot]

        def scores(other):
            raw = (
                jnp.einsum(
                    "hrd,hkd->hrk", query_input, k_tile[other], preferred_element_type=jnp.float32
                )
                * score_scale
            )
            keep = causal | (other != slot)
            return jnp.where(keep[None], raw, NEG)

        def seen(other):
            return (seg[other] == seg[slot]) & (other <= slot)

        def stats_step(other, state):

            def stats_update(state):
                top, total = state
                score = scores(other)
                new_top = jnp.maximum(top, jnp.max(score, axis=-1))
                total = total * jnp.exp(top - new_top) + jnp.sum(
                    jnp.exp(score - new_top[..., None]), axis=-1
                )
                return (new_top, total)

            return lax.cond(seen(other), stats_update, lambda st: st, state)

        start_state = (
            jnp.full((heads, token_rows), NEG, jnp.float32),
            jnp.zeros((heads, token_rows), jnp.float32),
        )
        top, total = lax.fori_loop(0, nblk, stats_step, start_state)

        def probs(score):
            return jnp.exp(score - top[..., None]) / total[..., None]

        def out_step(other, acc):

            def out_update(acc):
                weights = probs(scores(other)).astype(jnp.bfloat16)
                return acc + jnp.einsum(
                    "hrk,hkd->hrd", weights, v_tile[other], preferred_element_type=jnp.float32
                )

            return lax.cond(seen(other), out_update, lambda a: a, acc)

        attended = lax.fori_loop(
            0, nblk, out_step, jnp.zeros((heads, token_rows, width), jnp.float32)
        ).astype(jnp.bfloat16)
        delta = jnp.sum(
            upstream_gradient.astype(jnp.float32) * attended.astype(jnp.float32), axis=-1
        )

        def grad_step(other, state):

            def grad_update(state):
                grad_query, key_gradient_rows, value_gradient_rows = state
                prob = probs(scores(other))
                dprob = jnp.einsum(
                    "hrd,hkd->hrk",
                    upstream_gradient,
                    v_tile[other],
                    preferred_element_type=jnp.float32,
                )
                dscore = (prob * (dprob - delta[..., None])).astype(jnp.bfloat16)
                grad_query = grad_query + jnp.einsum(
                    "hrk,hkd->hrd", dscore, k_tile[other], preferred_element_type=jnp.float32
                )
                key_term = jnp.einsum(
                    "hrk,hrd->hkd", dscore, query_input, preferred_element_type=jnp.float32
                )
                val_term = jnp.einsum(
                    "hrk,hrd->hkd",
                    prob.astype(jnp.bfloat16),
                    upstream_gradient,
                    preferred_element_type=jnp.float32,
                )
                return (
                    grad_query,
                    key_gradient_rows.at[other].add(key_term),
                    value_gradient_rows.at[other].add(val_term),
                )

            return lax.cond(seen(other), grad_update, lambda st: st, state)

        grad_query, key_gradient_rows, value_gradient_rows = lax.fori_loop(
            0,
            nblk,
            grad_step,
            (
                jnp.zeros((heads, token_rows, width), jnp.float32),
                key_gradient_rows,
                value_gradient_rows,
            ),
        )
        return (
            (key_gradient_rows, value_gradient_rows),
            (score_scale * grad_query).astype(jnp.bfloat16),
        )

    empty = jnp.zeros((nblk, heads, keys_n, width), jnp.float32)
    (key_gradient_rows, value_gradient_rows), grad_q = lax.scan(
        per_slot, (empty, empty), jnp.arange(nblk, dtype=jnp.int32)
    )
    return (grad_q, score_scale * key_gradient_rows, value_gradient_rows)


def shards(queries, keys, values, output_gradient, doc_lengths, dest_group, dest_slot):
    n_dp = lax.axis_size("dp")
    context_length = lax.axis_size("ctx")
    group = lax.axis_index("dp")
    column = lax.axis_index("ctx")
    block_rows = queries.shape[0] // GROUP_BLOCKS
    head_width = HEAD_SIZE
    per_key_head = QUERY_HEADS // KEY_HEADS
    cap = max(2, GROUP_BLOCKS // n_dp)
    score_scale = head_width ** (-0.5)
    send_src, send_valid, recv_src, back_src, back_valid, home_source = route_tables(
        dest_group, dest_slot, n_dp, cap, group
    )

    def to_blocks(input_array):
        return input_array.reshape(GROUP_BLOCKS, block_rows, input_array.shape[1])

    sent = tuple(
        (
            pack_rows(to_blocks(item), send_src, send_valid)
            for item in (queries, keys, values, output_gradient)
        )
    )
    q_recv, k_recv, v_recv, g_recv = (
        lax.all_to_all(sent[0], "dp", split_axis=0, concat_axis=0, tiled=True),
        lax.all_to_all(sent[1], "dp", split_axis=0, concat_axis=0, tiled=True),
        lax.all_to_all(sent[2], "dp", split_axis=0, concat_axis=0, tiled=True),
        lax.all_to_all(sent[3], "dp", split_axis=0, concat_axis=0, tiled=True),
    )
    q_att = jnp.take(q_recv, recv_src, axis=0)
    k_att = jnp.take(k_recv, recv_src, axis=0)
    v_att = jnp.take(v_recv, recv_src, axis=0)
    g_att = jnp.take(g_recv, recv_src, axis=0)
    ends = jnp.cumsum(doc_lengths[group])
    seg = jnp.sum(
        (ends[None, :] <= jnp.arange(GROUP_BLOCKS, dtype=jnp.int32)[:, None]).astype(jnp.int32),
        axis=1,
    )

    def query_tiles(input_array):
        return (
            input_array.reshape(GROUP_BLOCKS, block_rows, KEY_HEADS, per_key_head, head_width)
            .transpose(0, 2, 1, 3, 4)
            .reshape(GROUP_BLOCKS, KEY_HEADS, block_rows * per_key_head, head_width)
        )

    k_all, v_all = (
        lax.all_gather(k_att, "ctx", axis=0, tiled=True),
        lax.all_gather(v_att, "ctx", axis=0, tiled=True),
    )

    def key_tiles(input_array):
        return (
            input_array.reshape(context_length, GROUP_BLOCKS, block_rows, KEY_HEADS, head_width)
            .transpose(1, 3, 0, 2, 4)
            .reshape(GROUP_BLOCKS, KEY_HEADS, context_length * block_rows, head_width)
        )

    def key_rows(input_array):
        return (
            input_array.reshape(GROUP_BLOCKS, KEY_HEADS, context_length, block_rows, head_width)
            .transpose(2, 0, 3, 1, 4)
            .reshape(context_length * GROUP_BLOCKS, block_rows, KEY_HEADS * head_width)
        )

    q_pos = (
        column * block_rows + jnp.arange(block_rows * per_key_head, dtype=jnp.int32) // per_key_head
    )
    k_pos = jnp.arange(context_length * block_rows, dtype=jnp.int32)
    query_grad_tile, dk_tile, dv_tile = attend(
        query_tiles(q_att),
        key_tiles(k_all),
        key_tiles(v_all),
        query_tiles(g_att),
        q_pos,
        k_pos,
        seg,
        score_scale,
    )
    dq_att = (
        query_grad_tile.reshape(GROUP_BLOCKS, KEY_HEADS, block_rows, per_key_head, head_width)
        .transpose(0, 2, 1, 3, 4)
        .reshape(GROUP_BLOCKS, block_rows, QUERY_HEADS * head_width)
    )
    dk_sum, dv_sum = (
        lax.psum_scatter(key_rows(dk_tile), "ctx", scatter_dimension=0, tiled=True),
        lax.psum_scatter(key_rows(dv_tile), "ctx", scatter_dimension=0, tiled=True),
    )
    dk_att = dk_sum.astype(jnp.bfloat16)
    dv_att = dv_sum.astype(jnp.bfloat16)
    back_q = pack_rows(dq_att, back_src, back_valid)
    back_k = pack_rows(dk_att, back_src, back_valid)
    back_v = pack_rows(dv_att, back_src, back_valid)
    home_q, home_key_rows, home_value_rows = (
        lax.all_to_all(back_q, "dp", split_axis=0, concat_axis=0, tiled=True),
        lax.all_to_all(back_k, "dp", split_axis=0, concat_axis=0, tiled=True),
        lax.all_to_all(back_v, "dp", split_axis=0, concat_axis=0, tiled=True),
    )
    grad_q = jnp.take(home_q, home_source, axis=0).reshape(
        GROUP_BLOCKS * block_rows, QUERY_HEADS * head_width
    )
    key_gradient = jnp.take(home_key_rows, home_source, axis=0).reshape(
        GROUP_BLOCKS * block_rows, KEY_HEADS * head_width
    )
    value_gradient = jnp.take(home_value_rows, home_source, axis=0).reshape(
        GROUP_BLOCKS * block_rows, KEY_HEADS * head_width
    )
    return (grad_q, key_gradient, value_gradient)


def solution(mesh):
    placed = (
        P(("dp", "ctx"), None),
        P(("dp", "ctx"), None),
        P(("dp", "ctx"), None),
        P(("dp", "ctx"), None),
        P(),
        P(),
        P(),
    )
    return jax.shard_map(
        shards,
        mesh=mesh,
        in_specs=placed,
        out_specs=(P(("dp", "ctx"), None), P(("dp", "ctx"), None), P(("dp", "ctx"), None)),
        check_vma=False,
    )
```

profile of v0, /device:TPU:1, one launch (start us, length us, event | category | flops | bytes accessed | tf_op | source)
XLA Modules:
  0.0 1517.5 jit_solution(5829711938310554747)
XLA Ops:
  47.0 30.8 %all_to_all.35 = bf16[16,16,4096]{2,1,0:T(8,128)(2,1)} all-to-all(bf16[16,16,4096]{2,1,0:T(8,128)(2,1)S(1)} %get-tuple-element.1150), channel_id=1, replica_groups=mesh['dp'=8,'ctx'=32] {'dp'}, dimensions={0} | all-to-all | bytes 4194304 | tf_op jit(solution)/shard_map/all_to_all | solution.py:199
  85.0 23.7 %all-to-all-done = bf16[16,16,4096]{2,1,0:T(8,128)(2,1)S(1)} async-done(((bf16[16,16,4096]{2,1,0:T(8,128)(2,1)}), bf16[16,16,4096]{2,1,0:T(8,128)(2,1)S(1)}, u32[]{:S(2)}, u32[]{:S(2)}) %all-to-all-start) | async-done | bytes 2097184 | tf_op jit(solution)/shard_map/all_to_all | solution.py:196
  131.0 70.2 %all-gather.3.cloned.1.call-done = bf16[256,16,512]{2,1,0:T(8,128)(2,1)} async-done(((bf16[8,16,512]{2,1,0:T(8,128)(2,1)}), bf16[256,16,512]{2,1,0:T(8,128)(2,1)}) %all-gather.3.cloned.1.call-update) | async-done | bytes 4194320 | tf_op jit(solution)/shard_map/all_gather | solution.py:219
  221.7 771.7 %while.77 = (s32[]{:T(128)}, f32[8,4,512,128]{3,2,1,0:T(8,128)}, f32[8,4,512,128]{3,2,1,0:T(8,128)}, bf16[8,4,128,128]{3,2,1,0:T(8,128)(2,1)}, s32[8]{0:T(128)S(...) while((s32[]{:T(128)}, f32[8,4,512,128]{3,2,1,0:T(8,128)}, ...), condition=%wide.region_24.29_spmd.clone, body=%wide.region_7.28_spmd.clone.sunk | while | flops 543490624 | bytes 18399804 | solution.py:166
  224.7 20.6 %while.78 = (s32[]{:T(128)}, f32[4,128]{1,0:T(4,128)S(1)}, f32[4,128]{1,0:T(4,128)S(1)}, s32[8]{0:T(128)S(1)}, s32[1]{0:T(128)}, /*index=5*/s32[]{:T(128)}, pred...) while((s32[]{:T(128)}, f32[4,128]{1,0:T(4,128)S(1)}, ...), condition=%wide.region_13.17_spmd, body=%wide.region_8.16_spmd.sunk | while | flops 68486152 | bytes 2976035 | solution.py:96
  245.3 21.9 %while.79 = (s32[]{:T(128)}, f32[4,128,128]{2,1,0:T(8,128)S(1)}, s32[8]{0:T(128)S(1)}, s32[1]{0:T(128)}, s32[]{:T(128)}, /*index=5*/pred[128,512]{0,1:T(8,128)(4...) while((s32[]{:T(128)}, f32[4,128,128]{2,1,0:T(8,128)S(1)}, ...), condition=%wide.region_17.21_spmd, body=%wide.region_14.20_spmd.sunk | while | flops 135659520 | bytes 1905951 | solution.py:111
  267.4 31.0 %while.80 = (s32[]{:T(128)}, f32[4,128,128]{2,1,0:T(8,128)S(1)}, f32[8,4,512,128]{3,2,1,0:T(8,128)}, f32[8,4,512,128]{3,2,1,0:T(8,128)}, s32[8]{0:T(128)S(1)}, /...) while((s32[]{:T(128)}, f32[4,128,128]{2,1,0:T(8,128)S(1)}, ...), condition=%wide.region_23.27_spmd, body=%wide.region_19.26_spmd.sunk | while | flops 338821152 | bytes 11741096 | solution.py:150
  302.0 20.6 %while.78 = (s32[]{:T(128)}, f32[4,128]{1,0:T(4,128)S(1)}, f32[4,128]{1,0:T(4,128)S(1)}, s32[8]{0:T(128)S(1)}, s32[1]{0:T(128)}, /*index=5*/s32[]{:T(128)}, pred...) while((s32[]{:T(128)}, f32[4,128]{1,0:T(4,128)S(1)}, ...), condition=%wide.region_13.17_spmd, body=%wide.region_8.16_spmd.sunk | while | flops 68486152 | bytes 2976035 | solution.py:96
  322.7 21.9 %while.79 = (s32[]{:T(128)}, f32[4,128,128]{2,1,0:T(8,128)S(1)}, s32[8]{0:T(128)S(1)}, s32[1]{0:T(128)}, s32[]{:T(128)}, /*index=5*/pred[128,512]{0,1:T(8,128)(4...) while((s32[]{:T(128)}, f32[4,128,128]{2,1,0:T(8,128)S(1)}, ...), condition=%wide.region_17.21_spmd, body=%wide.region_14.20_spmd.sunk | while | flops 135659520 | bytes 1905951 | solution.py:111
  344.7 30.9 %while.80 = (s32[]{:T(128)}, f32[4,128,128]{2,1,0:T(8,128)S(1)}, f32[8,4,512,128]{3,2,1,0:T(8,128)}, f32[8,4,512,128]{3,2,1,0:T(8,128)}, s32[8]{0:T(128)S(1)}, /...) while((s32[]{:T(128)}, f32[4,128,128]{2,1,0:T(8,128)S(1)}, ...), condition=%wide.region_23.27_spmd, body=%wide.region_19.26_spmd.sunk | while | flops 338821152 | bytes 11741096 | solution.py:150
  379.3 22.8 %while.78 = (s32[]{:T(128)}, f32[4,128]{1,0:T(4,128)S(1)}, f32[4,128]{1,0:T(4,128)S(1)}, s32[8]{0:T(128)S(1)}, s32[1]{0:T(128)}, /*index=5*/s32[]{:T(128)}, pred...) while((s32[]{:T(128)}, f32[4,128]{1,0:T(4,128)S(1)}, ...), condition=%wide.region_13.17_spmd, body=%wide.region_8.16_spmd.sunk | while | flops 68486152 | bytes 2976035 | solution.py:96
  402.1 24.4 %while.79 = (s32[]{:T(128)}, f32[4,128,128]{2,1,0:T(8,128)S(1)}, s32[8]{0:T(128)S(1)}, s32[1]{0:T(128)}, s32[]{:T(128)}, /*index=5*/pred[128,512]{0,1:T(8,128)(4...) while((s32[]{:T(128)}, f32[4,128,128]{2,1,0:T(8,128)S(1)}, ...), condition=%wide.region_17.21_spmd, body=%wide.region_14.20_spmd.sunk | while | flops 135659520 | bytes 1905951 | solution.py:111
  426.7 43.2 %while.80 = (s32[]{:T(128)}, f32[4,128,128]{2,1,0:T(8,128)S(1)}, f32[8,4,512,128]{3,2,1,0:T(8,128)}, f32[8,4,512,128]{3,2,1,0:T(8,128)}, s32[8]{0:T(128)S(1)}, /...) while((s32[]{:T(128)}, f32[4,128,128]{2,1,0:T(8,128)S(1)}, ...), condition=%wide.region_23.27_spmd, body=%wide.region_19.26_spmd.sunk | while | flops 338821152 | bytes 11741096 | solution.py:150
  473.6 25.0 %while.78 = (s32[]{:T(128)}, f32[4,128]{1,0:T(4,128)S(1)}, f32[4,128]{1,0:T(4,128)S(1)}, s32[8]{0:T(128)S(1)}, s32[1]{0:T(128)}, /*index=5*/s32[]{:T(128)}, pred...) while((s32[]{:T(128)}, f32[4,128]{1,0:T(4,128)S(1)}, ...), condition=%wide.region_13.17_spmd, body=%wide.region_8.16_spmd.sunk | while | flops 68486152 | bytes 2976035 | solution.py:96
  498.6 27.0 %while.79 = (s32[]{:T(128)}, f32[4,128,128]{2,1,0:T(8,128)S(1)}, s32[8]{0:T(128)S(1)}, s32[1]{0:T(128)}, s32[]{:T(128)}, /*index=5*/pred[128,512]{0,1:T(8,128)(4...) while((s32[]{:T(128)}, f32[4,128,128]{2,1,0:T(8,128)S(1)}, ...), condition=%wide.region_17.21_spmd, body=%wide.region_14.20_spmd.sunk | while | flops 135659520 | bytes 1905951 | solution.py:111
  525.7 55.5 %while.80 = (s32[]{:T(128)}, f32[4,128,128]{2,1,0:T(8,128)S(1)}, f32[8,4,512,128]{3,2,1,0:T(8,128)}, f32[8,4,512,128]{3,2,1,0:T(8,128)}, s32[8]{0:T(128)S(1)}, /...) while((s32[]{:T(128)}, f32[4,128,128]{2,1,0:T(8,128)S(1)}, ...), condition=%wide.region_23.27_spmd, body=%wide.region_19.26_spmd.sunk | while | flops 338821152 | bytes 11741096 | solution.py:150
  584.9 20.6 %while.78 = (s32[]{:T(128)}, f32[4,128]{1,0:T(4,128)S(1)}, f32[4,128]{1,0:T(4,128)S(1)}, s32[8]{0:T(128)S(1)}, s32[1]{0:T(128)}, /*index=5*/s32[]{:T(128)}, pred...) while((s32[]{:T(128)}, f32[4,128]{1,0:T(4,128)S(1)}, ...), condition=%wide.region_13.17_spmd, body=%wide.region_8.16_spmd.sunk | while | flops 68486152 | bytes 2976035 | solution.py:96
  605.6 21.9 %while.79 = (s32[]{:T(128)}, f32[4,128,128]{2,1,0:T(8,128)S(1)}, s32[8]{0:T(128)S(1)}, s32[1]{0:T(128)}, s32[]{:T(128)}, /*index=5*/pred[128,512]{0,1:T(8,128)(4...) while((s32[]{:T(128)}, f32[4,128,128]{2,1,0:T(8,128)S(1)}, ...), condition=%wide.region_17.21_spmd, body=%wide.region_14.20_spmd.sunk | while | flops 135659520 | bytes 1905951 | solution.py:111
  627.7 31.0 %while.80 = (s32[]{:T(128)}, f32[4,128,128]{2,1,0:T(8,128)S(1)}, f32[8,4,512,128]{3,2,1,0:T(8,128)}, f32[8,4,512,128]{3,2,1,0:T(8,128)}, s32[8]{0:T(128)S(1)}, /...) while((s32[]{:T(128)}, f32[4,128,128]{2,1,0:T(8,128)S(1)}, ...), condition=%wide.region_23.27_spmd, body=%wide.region_19.26_spmd.sunk | while | flops 338821152 | bytes 11741096 | solution.py:150
  639.3 12.4 conditional.8
  662.2 22.8 %while.78 = (s32[]{:T(128)}, f32[4,128]{1,0:T(4,128)S(1)}, f32[4,128]{1,0:T(4,128)S(1)}, s32[8]{0:T(128)S(1)}, s32[1]{0:T(128)}, /*index=5*/s32[]{:T(128)}, pred...) while((s32[]{:T(128)}, f32[4,128]{1,0:T(4,128)S(1)}, ...), condition=%wide.region_13.17_spmd, body=%wide.region_8.16_spmd.sunk | while | flops 68486152 | bytes 2976035 | solution.py:96
  685.1 24.4 %while.79 = (s32[]{:T(128)}, f32[4,128,128]{2,1,0:T(8,128)S(1)}, s32[8]{0:T(128)S(1)}, s32[1]{0:T(128)}, s32[]{:T(128)}, /*index=5*/pred[128,512]{0,1:T(8,128)(4...) while((s32[]{:T(128)}, f32[4,128,128]{2,1,0:T(8,128)S(1)}, ...), condition=%wide.region_17.21_spmd, body=%wide.region_14.20_spmd.sunk | while | flops 135659520 | bytes 1905951 | solution.py:111
  709.7 43.3 %while.80 = (s32[]{:T(128)}, f32[4,128,128]{2,1,0:T(8,128)S(1)}, f32[8,4,512,128]{3,2,1,0:T(8,128)}, f32[8,4,512,128]{3,2,1,0:T(8,128)}, s32[8]{0:T(128)S(1)}, /...) while((s32[]{:T(128)}, f32[4,128,128]{2,1,0:T(8,128)S(1)}, ...), condition=%wide.region_23.27_spmd, body=%wide.region_19.26_spmd.sunk | while | flops 338821152 | bytes 11741096 | solution.py:150
  721.3 12.4 conditional.8
  756.6 25.0 %while.78 = (s32[]{:T(128)}, f32[4,128]{1,0:T(4,128)S(1)}, f32[4,128]{1,0:T(4,128)S(1)}, s32[8]{0:T(128)S(1)}, s32[1]{0:T(128)}, /*index=5*/s32[]{:T(128)}, pred...) while((s32[]{:T(128)}, f32[4,128]{1,0:T(4,128)S(1)}, ...), condition=%wide.region_13.17_spmd, body=%wide.region_8.16_spmd.sunk | while | flops 68486152 | bytes 2976035 | solution.py:96
  781.6 27.0 %while.79 = (s32[]{:T(128)}, f32[4,128,128]{2,1,0:T(8,128)S(1)}, s32[8]{0:T(128)S(1)}, s32[1]{0:T(128)}, s32[]{:T(128)}, /*index=5*/pred[128,512]{0,1:T(8,128)(4...) while((s32[]{:T(128)}, f32[4,128,128]{2,1,0:T(8,128)S(1)}, ...), condition=%wide.region_17.21_spmd, body=%wide.region_14.20_spmd.sunk | while | flops 135659520 | bytes 1905951 | solution.py:111
  808.8 55.6 %while.80 = (s32[]{:T(128)}, f32[4,128,128]{2,1,0:T(8,128)S(1)}, f32[8,4,512,128]{3,2,1,0:T(8,128)}, f32[8,4,512,128]{3,2,1,0:T(8,128)}, s32[8]{0:T(128)S(1)}, /...) while((s32[]{:T(128)}, f32[4,128,128]{2,1,0:T(8,128)S(1)}, ...), condition=%wide.region_23.27_spmd, body=%wide.region_19.26_spmd.sunk | while | flops 338821152 | bytes 11741096 | solution.py:150
  868.0 27.2 %while.78 = (s32[]{:T(128)}, f32[4,128]{1,0:T(4,128)S(1)}, f32[4,128]{1,0:T(4,128)S(1)}, s32[8]{0:T(128)S(1)}, s32[1]{0:T(128)}, /*index=5*/s32[]{:T(128)}, pred...) while((s32[]{:T(128)}, f32[4,128]{1,0:T(4,128)S(1)}, ...), condition=%wide.region_13.17_spmd, body=%wide.region_8.16_spmd.sunk | while | flops 68486152 | bytes 2976035 | solution.py:96
  895.2 29.5 %while.79 = (s32[]{:T(128)}, f32[4,128,128]{2,1,0:T(8,128)S(1)}, s32[8]{0:T(128)S(1)}, s32[1]{0:T(128)}, s32[]{:T(128)}, /*index=5*/pred[128,512]{0,1:T(8,128)(4...) while((s32[]{:T(128)}, f32[4,128,128]{2,1,0:T(8,128)S(1)}, ...), condition=%wide.region_17.21_spmd, body=%wide.region_14.20_spmd.sunk | while | flops 135659520 | bytes 1905951 | solution.py:111
  924.9 67.9 %while.80 = (s32[]{:T(128)}, f32[4,128,128]{2,1,0:T(8,128)S(1)}, f32[8,4,512,128]{3,2,1,0:T(8,128)}, f32[8,4,512,128]{3,2,1,0:T(8,128)}, s32[8]{0:T(128)S(1)}, /...) while((s32[]{:T(128)}, f32[4,128,128]{2,1,0:T(8,128)S(1)}, ...), condition=%wide.region_23.27_spmd, body=%wide.region_19.26_spmd.sunk | while | flops 338821152 | bytes 11741096 | solution.py:150
  1057.6 189.5 %reduce-scatter.3.cloned.1.call-done = f32[8,16,512]{2,1,0:T(8,128)} async-done(((f32[256,16,512]{2,1,0:T(8,128)}), f32[8,16,512]{2,1,0:T(8,128)}) %reduce-scatter.3.cloned.1.call-update) | async-done | bytes 262160 | tf_op jit(solution)/shard_map/reduce_scatter | solution.py:257
  1248.6 230.6 %reduce-scatter.5.cloned.1.call-done = f32[8,16,512]{2,1,0:T(8,128)} async-done(((f32[256,16,512]{2,1,0:T(8,128)}), f32[8,16,512]{2,1,0:T(8,128)}) %reduce-scatter.5.cloned.1.call-update) | async-done | bytes 262160 | tf_op jit(solution)/shard_map/reduce_scatter | solution.py:258
  (838 shorter events, 843.1 us)
Async XLA Ops:
  7.2 32.5 %copy-start = (bf16[128,4096]{1,0:T(8,128)(2,1)S(1)}, bf16[128,4096]{1,0:T(8,128)(2,1)}, u32[]{:S(2)}) copy-start(bf16[128,4096]{1,0:T(8,128)(2,1)} %param.36) | copy-start | bytes 3145732
  8.3 22.7 %copy-start.3 = (s32[8,8]{1,0:T(8,128)}, s32[8,8]{1,0:T(8,128)S(1)}, u32[]{:S(2)}) copy-start(s32[8,8]{1,0:T(8,128)S(1)} %convert_reduce_fusion) | copy-start | bytes 772
  13.5 13.1 all-to-all-start.3
  20.1 6.5 copy-start.7
  20.9 5.7 copy-start.5
  26.6 10.9 all-to-all-start.1
  31.0 87.9 %all-gather.5.cloned.1.call-start = ((), (), s32[]{:S(2)}) async-start(), calls=%async_computation.10 | async-start | bytes 4325376 | tf_op jit(solution)/shard_map/all_gather | solution.py:220
  38.9 162.3 %all-gather.3.cloned.1.call-start = ((), (), s32[]{:S(2)}) async-start(), calls=%async_computation.9 | async-start | bytes 4325376 | tf_op jit(solution)/shard_map/all_gather | solution.py:219
  47.0 35.4 %copy-start.10 = (s32[8,3]{0,1:T(4,128)S(1)}, s32[8,3]{0,1:T(4,128)}, u32[]{:S(2)}) copy-start(s32[8,3]{0,1:T(4,128)} %param.37) | copy-start | bytes 292
  77.8 30.9 %all-to-all-start = ((bf16[16,16,4096]{2,1,0:T(8,128)(2,1)}), bf16[16,16,4096]{2,1,0:T(8,128)(2,1)S(1)}, u32[]{:S(2)}, u32[]{:S(2)}) async-start(bf16[16,16,4096]{2,1,0:T(8,128)(2,1)} %get-tuple-element.1151), calls=%async_computation | async-start | bytes 4194304 | tf_op jit(solution)/shard_map/all_to_all | solution.py:196
  82.3 1164.7 %reduce-scatter.3.cloned.1.call-start = ((), (), s32[]{:S(2)}) async-start(), calls=%async_computation.11 | async-start | bytes 8650752 | tf_op jit(solution)/shard_map/reduce_scatter | solution.py:257
  1023.5 455.7 %reduce-scatter.5.cloned.1.call-start = ((), (), s32[]{:S(2)}) async-start(), calls=%async_computation.12 | async-start | bytes 8650752 | tf_op jit(solution)/shard_map/reduce_scatter | solution.py:258
  1046.1 0.7 copy-start.4
  1046.1 0.7 copy-start.8
  1046.1 1.0 copy-start.6
  1046.1 1.4 copy-start.2
  1050.5 452.6 %copy-start.9 = (pred[8]{0:T(512)(128)(4,1)S(1)}, pred[8]{0:T(512)(128)(4,1)}, u32[]{:S(2)}) copy-start(pred[8]{0:T(512)(128)(4,1)} %get-tuple-element.1140) | copy-start | bytes 28
  1050.5 432.8 %all-to-all-start.4 = ((bf16[16,16,4096]{2,1,0:T(8,128)(2,1)}), bf16[16,16,4096]{2,1,0:T(8,128)(2,1)S(1)}, u32[]{:S(2)}, u32[]{:S(2)}) async-start(bf16[16,16,4096]{2,1,0:T(8,128)(2,1)} %select_select_fusion), calls=%async_computation.4 | async-start | bytes 4194304 | tf_op jit(solution)/shard_map/all_to_all | solution.py:266
  1248.1 262.9 %copy-start.1 = (bf16[128,4096]{1,0:T(8,128)(2,1)S(1)}, bf16[128,4096]{1,0:T(8,128)(2,1)}, u32[]{:S(2)}) copy-start(bf16[128,4096]{1,0:T(8,128)(2,1)} %param.36) | copy-start | bytes 3145732
  1483.3 15.4 %all-to-all-start.6 = ((bf16[16,16,512]{2,1,0:T(8,128)(2,1)}), bf16[16,16,512]{2,1,0:T(8,128)(2,1)S(1)}, u32[]{:S(2)}, u32[]{:S(2)}) async-start(bf16[16,16,512]{2,1,0:T(8,128)(2,1)} %get-tuple-element.1146), calls=%async_computation.8 | async-start | bytes 524288 | tf_op jit(solution)/shard_map/all_to_all | solution.py:268
  1498.7 10.9 all-to-all-start.5
Sparse Core Ops, SparseCore 0:
  39.0 79.8 all-gather.4
  122.1 79.0 all-gather.2
  1023.7 223.3 reduce-scatter.2
  1251.5 227.6 reduce-scatter.4
where the time goes:
time: 1530 us; the launch traced here: 1520 us
  waiting for transfers between devices  540 us (35%)
  loops' own time  383 us (25%)
  matrix products  232 us (15%)
  local copies, waits for them, and re-layouts  221 us (14%)
  other arithmetic  60.9 us (4%)
  starting transfers between devices  36.1 us (2%)
  blocking collectives  30.8 us (2%)
    reduce_scatter x1, waiting for transfers between devices, shards(): lax.psum_scatter(key_rows(dv_tile), 'ctx', scatter_dimension=0, tiled=True)  231 us
    reduce_scatter x1, waiting for transfers between devices, shards(): lax.psum_scatter(key_rows(dk_tile), 'ctx', scatter_dimension=0, tiled=True)  189 us
    dynamic_slice x200, local copies, waits for them, and re-layouts, seen(): return (seg[other] == seg[slot]) & (other <= slot)  116 us
    another operation x8, loops' own time, per_slot(): lax.fori_loop(0, nblk, out_step, jnp.zeros((heads, token_rows, width), jn...  115 us
    another operation x8, loops' own time, per_slot(): top, total = lax.fori_loop(0, nblk, stats_step, start_state)  111 us
    another operation x8, loops' own time, per_slot(): lax.fori_loop(0, nblk, grad_step, (jnp.zeros((heads, token_rows, width),...  111 us
    all_gather x1, waiting for transfers between devices, shards(): lax.all_gather(k_att, 'ctx', axis=0, tiled=True)  70.2 us
    dot_general x17, matrix products, grad_update(): jnp.einsum('hrk,hrd->hkd', prob.astype(jnp.bfloat16), upstream_gradient,...  52.4 us
  transfers between devices with their start and end apart: 10, of which 9 were waited for; matrix products, arithmetic and copies ran while one was open for 4% of the time, Pallas kernels for 0%

commit v1 on v0

v1 whole, which is shorter than its diff:
```python
import math

import jax
import jax.numpy as jnp
from jax import lax
from jax.experimental import pallas as pl
from jax.experimental.pallas import tpu as pltpu
from jax.sharding import Mesh, PartitionSpec as P

QUERY_HEADS = 32
KEY_HEADS = 4
HEAD = 128
SLOTS = 8
BLOCK = 512
PER_KEY = QUERY_HEADS // KEY_HEADS
WIDE = PER_KEY * HEAD
BR = 16
CAP = 2
N_DP = 8
N_Y = 4
N_Z = 8
HALF = BLOCK // 2
SPAN = SLOTS // 2
NEG = -1.0e30
SCALE = HEAD ** -0.5
EXP_SCALE = SCALE / math.log(2.0)
F32 = jnp.float32
BF16 = jnp.bfloat16
MIB = 1024 * 1024


def tables(doc_lengths, dest_group, dest_slot):
    me = lax.axis_index("dp")
    blocks = jnp.arange(SLOTS, dtype=jnp.int32)
    dest = dest_group.reshape(N_DP, SLOTS)
    slot = dest_slot.reshape(N_DP, SLOTS)
    earlier = (dest[:, :, None] == dest[:, None, :]) & (blocks[None, :] < blocks[:, None])[None]
    rank = jnp.sum(earlier.astype(jnp.int32), axis=2)
    mine = blocks == me
    hit = ((dest == me)[None] & (slot[None] == blocks[:, None, None])).astype(jnp.int32)
    from_group = jnp.sum(hit * blocks[None, :, None], axis=(1, 2))
    from_rank = jnp.sum(hit * rank[None], axis=(1, 2))
    lengths = jnp.sum(jnp.where(mine[:, None], doc_lengths, 0), axis=0)
    docs = jnp.arange(lengths.shape[0], dtype=jnp.int32)
    ends = jnp.sum(jnp.where(docs[None, :] <= docs[:, None], lengths[None, :], 0), axis=1)
    first = jnp.max(jnp.where(ends[None, :] <= blocks[:, None], ends[None, :], 0), axis=1)
    place = jnp.full((SLOTS,), lax.axis_index("z"), jnp.int32)
    return jnp.stack([from_group, from_rank, first, place]).astype(jnp.int32)


def params(mib):
    return pltpu.CompilerParams(vmem_limit_bytes=mib * MIB)


def to_source(s, t):
    return (t[0, s], 0, t[1, s], 0, 0)


def whole(space):
    return pl.BlockSpec(memory_space=space)


def route(dest):
    base = lax.axis_index("dp") * SLOTS
    groups = [dest[base + j] for j in range(SLOTS)]
    ranks = []
    for j in range(SLOTS):
        rank = jnp.int32(0)
        for i in range(j):
            rank = rank + jnp.where(groups[i] == groups[j], 1, 0).astype(jnp.int32)
        ranks.append(rank)
    return list(zip(groups, ranks))


def run(copies):
    for copy in copies:
        copy.start()
    for copy in copies:
        copy.wait()


def pack_pair_body(dest, k, v, out, stage, sem):
    copies = []
    for j, (group, rank) in enumerate(route(dest)):
        rows = slice(j * BR, (j + 1) * BR)
        for h in range(KEY_HEADS):
            cols = slice(h * HEAD, (h + 1) * HEAD)
            stage[j, h, :, :HEAD] = k[rows, cols]
            stage[j, h, :, HEAD:] = v[rows, cols]
        copies.append(pltpu.make_async_copy(stage.at[j], out.at[group, :, rank], sem.at[j]))
    run(copies)


def pack_pair(dest, k, v):
    return pl.pallas_call(
        pack_pair_body,
        in_specs=[whole(pltpu.SMEM), whole(pltpu.VMEM), whole(pltpu.VMEM)],
        out_specs=whole(pl.ANY),
        out_shape=jax.ShapeDtypeStruct((N_DP, KEY_HEADS, CAP, BR, 2 * HEAD), BF16),
        scratch_shapes=[
            pltpu.VMEM((SLOTS, KEY_HEADS, BR, 2 * HEAD), BF16),
            pltpu.SemaphoreType.DMA((SLOTS,)),
        ],
        name="pack_pair",
    )(dest, k, v)


def pack_wide_body(dest, q, g, out, sem):
    copies = []
    for j, (group, rank) in enumerate(route(dest)):
        for h in range(KEY_HEADS):
            for n, x in enumerate((q, g)):
                copies.append(pltpu.make_async_copy(
                    x.at[pl.ds(j * BR, BR), pl.ds(h * WIDE, WIDE)],
                    out.at[group, h, rank, :, pl.ds(n * WIDE, WIDE)],
                    sem.at[j, h, n]))
    run(copies)


def pack_wide(dest, q, g):
    return pl.pallas_call(
        pack_wide_body,
        in_specs=[whole(pltpu.SMEM), whole(pltpu.VMEM), whole(pltpu.VMEM)],
        out_specs=whole(pl.ANY),
        out_shape=jax.ShapeDtypeStruct((N_DP, KEY_HEADS, CAP, BR, 2 * WIDE), BF16),
        scratch_shapes=[pltpu.SemaphoreType.DMA((SLOTS, KEY_HEADS, 2))],
        name="pack_wide",
    )(dest, q, g)


def pick_body(t, x, out, sem):
    run([pltpu.make_async_copy(x.at[t[0, s], :, t[1, s]], out.at[s], sem.at[s])
         for s in range(SLOTS)])


def pick_pair(table, x):
    return pl.pallas_call(
        pick_body,
        in_specs=[whole(pltpu.SMEM), whole(pl.ANY)],
        out_specs=whole(pltpu.VMEM),
        out_shape=jax.ShapeDtypeStruct((SLOTS, N_Y, BR, 2 * HEAD), BF16),
        scratch_shapes=[pltpu.SemaphoreType.DMA((SLOTS,))],
        name="pick_pair",
    )(table, x)


def place_body(t, x, out, sem):
    run([pltpu.make_async_copy(x.at[s], out.at[t[0, s], :, t[1, s]], sem.at[s])
         for s in range(SLOTS)])


def place_pair(table, x):
    return pl.pallas_call(
        place_body,
        in_specs=[whole(pltpu.SMEM), whole(pltpu.VMEM)],
        out_specs=whole(pl.ANY),
        out_shape=jax.ShapeDtypeStruct((N_DP, N_Y, CAP, BR, 2 * HEAD), BF16),
        scratch_shapes=[pltpu.SemaphoreType.DMA((SLOTS,))],
        name="place_pair",
    )(table, x)


def home_wide_body(dest, x, out, sem):
    copies = []
    for j, (group, rank) in enumerate(route(dest)):
        for h in range(KEY_HEADS):
            copies.append(pltpu.make_async_copy(
                x.at[group, h, rank],
                out.at[pl.ds(j * BR, BR), pl.ds(h * WIDE, WIDE)],
                sem.at[j, h]))
    run(copies)


def home_wide(dest, x):
    return pl.pallas_call(
        home_wide_body,
        in_specs=[whole(pltpu.SMEM), whole(pl.ANY)],
        out_specs=whole(pltpu.VMEM),
        out_shape=jax.ShapeDtypeStruct((SLOTS * BR, QUERY_HEADS * HEAD), BF16),
        scratch_shapes=[pltpu.SemaphoreType.DMA((SLOTS, KEY_HEADS))],
        name="home_wide",
    )(dest, x)


def home_pair_body(dest, x, k, v, stage, sem):
    copies = []
    for j, (group, rank) in enumerate(route(dest)):
        copies.append(pltpu.make_async_copy(x.at[group, :, rank], stage.at[j], sem.at[j]))
    run(copies)
    for j in range(SLOTS):
        rows = slice(j * BR, (j + 1) * BR)
        for h in range(KEY_HEADS):
            cols = slice(h * HEAD, (h + 1) * HEAD)
            k[rows, cols] = stage[j, h, :, :HEAD]
            v[rows, cols] = stage[j, h, :, HEAD:]


def home_pair(dest, x):
    out = jax.ShapeDtypeStruct((SLOTS * BR, KEY_HEADS * HEAD), BF16)
    return pl.pallas_call(
        home_pair_body,
        in_specs=[whole(pltpu.SMEM), whole(pl.ANY)],
        out_specs=[whole(pltpu.VMEM), whole(pltpu.VMEM)],
        out_shape=[out, out],
        scratch_shapes=[
            pltpu.VMEM((SLOTS, KEY_HEADS, BR, 2 * HEAD), BF16),
            pltpu.SemaphoreType.DMA((SLOTS,)),
        ],
        name="home_pair",
    )(dest, x)


def dot_nt(a, b):
    return lax.dot_general(a, b, (((1,), (1,)), ((), ())), preferred_element_type=F32)


def dot_nn(a, b):
    return lax.dot_general(a, b, (((1,), (0,)), ((), ())), preferred_element_type=F32)


def fold_max(x):
    return jnp.max(x.reshape(x.shape[0] // 8, 8, x.shape[1]), axis=0)


def fold_sum(x):
    return jnp.sum(x.reshape(x.shape[0] // 8, 8, x.shape[1]), axis=0)


def attend_body(t, qg_ref, kv_ref, dq_ref, dkv_ref,
                ks, vs, kt, qm, gm, bias, sc, dp, acc_k, acc_v, dqt):
    s = pl.program_id(0)
    first = t[2, s]

    @pl.when(s == 0)
    def _():
        def lay(o, carry):
            for y in range(N_Y):
                rows = pl.ds(y * HEAD, HEAD)
                ks[o, rows] = kv_ref[:, o, y, :, :HEAD].reshape(HEAD, HEAD)
                vs[o, rows] = kv_ref[:, o, y, :, HEAD:].reshape(HEAD, HEAD)
            kt[o] = ks[o].T
            return carry

        lax.fori_loop(0, SLOTS, lay, 0)
        key = lax.broadcasted_iota(jnp.int32, (HALF, HALF), 0)
        lane = lax.broadcasted_iota(jnp.int32, (HALF, HALF), 1)
        query = (lane // HEAD) * HEAD + t[3, 0] * BR + lane % BR
        bias[...] = jnp.where(key <= query, 0.0, NEG).astype(F32)

    for y in range(N_Y):
        for h in range(PER_KEY):
            rows = pl.ds(y * HEAD + h * BR, BR)
            qm[rows, :] = qg_ref[0, y, 0, :, h * HEAD:(h + 1) * HEAD]
            gm[rows, :] = qg_ref[0, y, 0, :, WIDE + h * HEAD:WIDE + (h + 1) * HEAD]

    count = s - first
    own = SPAN - 1
    lo, hi = slice(0, HALF), slice(HALF, BLOCK)
    parts = ((lo, lo, True), (lo, hi, False), (hi, hi, True))

    top = {}
    for keys, rows, masked in parts:
        x = dot_nt(ks[s, keys], qm[rows])
        if masked:
            x = x + bias[...]
        sc[own, keys, rows] = x
        x = fold_max(x)
        top[rows.start] = jnp.maximum(top[rows.start], x) if rows.start in top else x
    top = jnp.concatenate([top[0], top[HALF]], axis=1)

    def score_step(i, top):
        x = dot_nt(ks[first + i], qm[...])
        sc[i] = x
        return jnp.maximum(top, fold_max(x))

    top = lax.fori_loop(0, count, score_step, top)
    top = jnp.max(top, axis=0, keepdims=True)

    total, moment = {}, {}
    for keys, rows, masked in parts:
        d = dot_nt(vs[s, keys], gm[rows])
        e = jnp.exp2((sc[own, keys, rows] - top[:, rows]) * EXP_SCALE)
        sc[own, keys, rows] = e
        dp[own, keys, rows] = d
        a, b = fold_sum(e), fold_sum(e * d)
        if rows.start in total:
            a, b = a + total[rows.start], b + moment[rows.start]
        total[rows.start], moment[rows.start] = a, b

    def exp_step(i, state):
        total, moment = state
        d = dot_nt(vs[first + i], gm[...])
        e = jnp.exp2((sc[i] - top) * EXP_SCALE)
        sc[i] = e
        dp[i] = d
        return total + fold_sum(e), moment + fold_sum(e * d)

    total, moment = lax.fori_loop(
        0, count, exp_step,
        (jnp.concatenate([total[0], total[HALF]], axis=1),
         jnp.concatenate([moment[0], moment[HALF]], axis=1)))
    inverse = 1.0 / jnp.sum(total, axis=0, keepdims=True)
    delta = jnp.sum(moment, axis=0, keepdims=True) * inverse

    for n, (keys, rows, masked) in enumerate(parts):
        p = sc[own, keys, rows] * inverse[:, rows]
        w = p.astype(BF16)
        ds = (p * (dp[own, keys, rows] - delta[:, rows])).astype(BF16)
        val_term = dot_nn(w, gm[rows])
        key_term = dot_nn(ds, qm[rows])
        qry_term = dot_nn(kt[s, :, keys], ds)
        if n == 1:
            acc_v[s, keys] += val_term
            acc_k[s, keys] += key_term
        else:
            acc_v[s, keys] = val_term
            acc_k[s, keys] = key_term
        if n == 2:
            dqt[:, rows] += qry_term
        else:
            dqt[:, rows] = qry_term

    def grad_step(i, carry):
        o = first + i
        p = sc[i] * inverse
        w = p.astype(BF16)
        ds = (p * (dp[i] - delta)).astype(BF16)
        acc_v[o] += dot_nn(w, gm[...])
        acc_k[o] += dot_nn(ds, qm[...])
        dqt[...] += dot_nn(kt[o], ds)
        return carry

    lax.fori_loop(0, count, grad_step, 0)

    dq = (dqt[...].T * SCALE).astype(BF16)
    for y in range(N_Y):
        for h in range(PER_KEY):
            at = y * HEAD + h * BR
            dq_ref[0, y, 0, :, h * HEAD:(h + 1) * HEAD] = dq[at:at + BR]

    @pl.when(s == SLOTS - 1)
    def _():
        def emit(o, carry):
            for y in range(N_Y):
                rows = pl.ds(y * HEAD, HEAD)
                dkv_ref[:, o, y, :, :HEAD] = (
                    (acc_k[o, rows] * SCALE).astype(BF16).reshape(N_Z, BR, HEAD))
                dkv_ref[:, o, y, :, HEAD:] = acc_v[o, rows].astype(BF16).reshape(N_Z, BR, HEAD)
            return carry

        lax.fori_loop(0, SLOTS, emit, 0)


def attend(table, qg, kv):
    both = pl.BlockSpec((1, N_Y, 1, BR, 2 * WIDE), to_source)
    wide = pl.BlockSpec((1, N_Y, 1, BR, WIDE), to_source)
    pair = pl.BlockSpec((N_Z, SLOTS, N_Y, BR, 2 * HEAD), lambda s, t: (0, 0, 0, 0, 0))
    return pl.pallas_call(
        attend_body,
        grid_spec=pltpu.PrefetchScalarGridSpec(
            num_scalar_prefetch=1,
            grid=(SLOTS,),
            in_specs=[both, pair],
            out_specs=[wide, pair],
            scratch_shapes=[
                pltpu.VMEM((SLOTS, BLOCK, HEAD), BF16),
                pltpu.VMEM((SLOTS, BLOCK, HEAD), BF16),
                pltpu.VMEM((SLOTS, HEAD, BLOCK), BF16),
                pltpu.VMEM((BLOCK, HEAD), BF16),
                pltpu.VMEM((BLOCK, HEAD), BF16),
                pltpu.VMEM((HALF, HALF), F32),
                pltpu.VMEM((SPAN, BLOCK, BLOCK), F32),
                pltpu.VMEM((SPAN, BLOCK, BLOCK), F32),
                pltpu.VMEM((SLOTS, BLOCK, HEAD), F32),
                pltpu.VMEM((SLOTS, BLOCK, HEAD), F32),
                pltpu.VMEM((HEAD, BLOCK), F32),
            ],
        ),
        out_shape=[
            jax.ShapeDtypeStruct((N_DP, N_Y, CAP, BR, WIDE), BF16),
            jax.ShapeDtypeStruct((N_Z, SLOTS, N_Y, BR, 2 * HEAD), BF16),
        ],
        compiler_params=params(48),
        name="attend",
    )(table, qg, kv)


def swap(x):
    flat = x.reshape((N_DP * N_Y,) + x.shape[2:])
    return lax.all_to_all(flat, ("dp", "y"), 0, 0, tiled=True).reshape(x.shape)


def shards(queries, keys, values, output_gradient, doc_lengths, dest_group, dest_slot):
    packed = pack_pair(dest_group, keys, values)
    doc_lengths, dest_slot, late, packed = lax.optimization_barrier(
        (doc_lengths, dest_slot, dest_group, packed))
    arrived = swap(packed)
    wide = pack_wide(late, queries, output_gradient)
    table = tables(doc_lengths, late, dest_slot)
    kv = lax.all_gather(pick_pair(table, arrived), "z", axis=0, tiled=False)
    dq, dkv = attend(table, swap(wide), kv)
    dkv = lax.psum_scatter(dkv, "z", scatter_dimension=0, tiled=False)
    grad_q = home_wide(dest_group, swap(dq))
    key_gradient, value_gradient = home_pair(dest_group, swap(place_pair(table, dkv)))
    return grad_q, key_gradient, value_gradient


def solution(mesh):
    grid = Mesh(mesh.devices.reshape(N_DP, N_Y, N_Z), ("dp", "y", "z"))
    rows = P(("dp", "y", "z"), None)
    return jax.shard_map(
        shards,
        mesh=grid,
        in_specs=(rows, rows, rows, rows, P(), P(), P()),
        out_specs=(rows, rows, rows),
        check_vma=False,
    )
```

time: 1530 us -> 187 us (0.12)
  waiting for transfers between devices: 540 us -> 93.9 us
  loops' own time: 383 us -> 0 us
  matrix products: 232 us -> 0 us
  local copies, waits for them, and re-layouts: 221 us -> 3.14 us
  other arithmetic: 60.9 us -> 2.34 us
  Pallas kernels: 0 us -> 38.3 us
  blocking collectives: 30.8 us -> 0 us
    reduce_scatter x2 -> x1, waiting for transfers between devices: 420 us -> 33.5 us  [shards(): dkv = lax.psum_scatter(dkv, 'z', scatter_dimension=0, tiled=False)]
    another operation x217 -> x0, loops' own time: 383 us -> none  [the longest x8 115 us: per_slot(): lax.fori_loop(0, nblk, out_step, jnp.zeros((heads, token_rows, width), jn...]
    dot_general x119 -> x0, matrix products: 232 us -> none  [the longest x17 52.4 us: grad_update(): jnp.einsum('hrk,hrd->hkd', prob.astype(jnp.bfloat16), upstream_gradient,...]
    dynamic_slice x209 -> x0, local copies, waits for them, and re-layouts: 121 us -> none  [the longest x200 116 us: seen(): return (seg[other] == seg[slot]) & (other <= slot)]
    all_gather x2 -> x1, waiting for transfers between devices: 76.2 us -> 0.01 us  [shards(): kv = lax.all_gather(pick_pair(table, arrived), 'z', axis=0, tiled=False)]
    reshape x11 -> x1, local copies, waits for them, and re-layouts: 60.5 us -> 0.73 us  [tables(): dest = dest_group.reshape(N_DP, SLOTS)]
    pallas_call x0 -> x7, Pallas kernels: none -> 38.3 us  [the longest x1 23.4 us: attend(): pl.pallas_call(attend_body, grid_spec=pltpu.PrefetchScalarGridSpec(num_sc...]
    all_to_all x1 -> x0, blocking collectives: 30.8 us -> none  [shards(): lax.all_to_all(sent[3], 'dp', split_axis=0, concat_axis=0, tiled=True)]
  transfers between devices with their start and end apart: 10 -> 6, of which waited for: 9 -> 4; matrix products, arithmetic and copies ran while one was open for 4% -> 2% of each run, Pallas kernels for 0% -> 6%
where the time goes in v1:
time: 187 us; the launch traced here: 186 us
  waiting for transfers between devices  93.9 us (50%)
  Pallas kernels  38.3 us (20%)
  starting transfers between devices  34.5 us (18%)
  between operations  14.2 us (8%)
  local copies, waits for them, and re-layouts  3.14 us (2%)
  other arithmetic  2.34 us (1%)
    all_to_all x4, waiting for transfers between devices, swap(): return lax.all_to_all(flat, ('dp', 'y'), 0, 0, tiled=True).reshape(x.shape)  60.3 us
    all_to_all x4, starting transfers between devices, swap(): return lax.all_to_all(flat, ('dp', 'y'), 0, 0, tiled=True).reshape(x.shape)  34.4 us
    reduce_scatter x1, waiting for transfers between devices, shards(): dkv = lax.psum_scatter(dkv, 'z', scatter_dimension=0, tiled=False)  33.5 us
    pallas_call x1, Pallas kernels, attend(): pl.pallas_call(attend_body, grid_spec=pltpu.PrefetchScalarGridSpec(num_sc...  23.4 us
  transfers between devices with their start and end apart: 6, of which 4 were waited for; matrix products, arithmetic and copies ran while one was open for 2% of the time, Pallas kernels for 6%

profile of v1, /device:TPU:1, one launch (start us, length us, event | category | flops | bytes accessed | tf_op | source)
XLA Modules:
  0.0 186.3 jit_solution(1387045349640944388)
XLA Ops:
  7.2 1.8 pack_pair.1
  9.0 8.6 %all-to-all-start.1 = ((bf16[32,2,16,256]{3,2,1,0:T(8,128)(2,1)}), bf16[32,2,16,256]{3,2,1,0:T(8,128)(2,1)S(1)}, u32[]{:S(2)}, u32[]{:S(2)}) async-start(bf16[32,2,16,256]{3,2,1,0:T(8,128)(2,1)} %bitcast.18), calls=%async_computation.1 | async-start | bytes 1048576 | tf_op jit(solution)/shard_map/all_to_all | solution.py:390
  17.6 0.7 reshape.60
  18.3 0.8 select_reduce_fusion.4
  19.1 3.5 %pack_wide.1 = bf16[8,4,2,16,2048]{4,3,2,1,0:T(8,128)(2,1)} custom-call(s32[64]{0:T(128)} %dest.6, bf16[128,4096]{1,0:T(8,128)(2,1)} %q.1, bf16[128,4096]{1,0:T(8,128)(2,1)} %g.1), custom_call_target="tpu_custom_call" | custom-call | tf_op jit(solution)/shard_map/pack_wide/pallas_call | solution.py:121
  22.7 0.1 select_reduce_fusion.3
  22.8 0.3 convert_reduce_fusion
  23.1 5.5 %all-to-all-done.1 = bf16[32,2,16,256]{3,2,1,0:T(8,128)(2,1)S(1)} async-done(((bf16[32,2,16,256]{3,2,1,0:T(8,128)(2,1)}), bf16[32,2,16,256]{3,2,1,0:T(8,128)(2,1)S(1)}, u32[]{:S(2)}, u32[]{:S(2)}) %all-to-all-start.1) | async-done | bytes 524320 | tf_op jit(solution)/shard_map/all_to_all | solution.py:390
  28.6 0.8 copy-done.2
  29.4 5.4 %all-to-all-start = ((bf16[32,2,16,2048]{3,2,1,0:T(8,128)(2,1)}), bf16[32,2,16,2048]{3,2,1,0:T(8,128)(2,1)}, u32[]{:S(2)}, u32[]{:S(2)}) async-start(bf16[32,2,16,2048]{3,2,1,0:T(8,128)(2,1)} %bitcast.14), calls=%async_computation | async-start | bytes 8388608 | tf_op jit(solution)/shard_map/all_to_all | solution.py:390
  34.8 0.0 all-gather.3.cloned.1.call-start
  34.9 0.1 select_reduce_fusion.2
  35.0 0.1 eq.50
  35.1 0.1 pad.3.clone
  35.1 0.4 select_reduce_fusion.1
  35.5 0.7 add_add_fusion.t
  36.2 2.4 %pick_pair.1 = bf16[8,4,16,256]{3,2,1,0:T(8,128)(2,1)} custom-call(s32[4,8]{1,0:T(4,128)} %add_add_fusion.t, bf16[8,4,2,16,256]{4,3,2,1,0:T(8,128)(2,1)} %bitcast.17), custom_call_target="tpu_custom_call" | custom-call | tf_op jit(solution)/shard_map/pick_pair/pallas_call | solution.py:137
  38.5 0.0 all-gather.3.cloned.1.call-update
  38.6 0.0 reduce-scatter.2.cloned.1.call-start
  38.6 46.8 %all-to-all-done = bf16[32,2,16,2048]{3,2,1,0:T(8,128)(2,1)} async-done(((bf16[32,2,16,2048]{3,2,1,0:T(8,128)(2,1)}), bf16[32,2,16,2048]{3,2,1,0:T(8,128)(2,1)}, u32[]{:S(2)}, u32[]{:S(2)}) %all-to-all-start) | async-done | bytes 4194336 | tf_op jit(solution)/shard_map/all_to_all | solution.py:390
  85.5 0.7 copy-done
  86.1 23.4 %attend.1 = (bf16[8,4,2,16,1024]{4,3,2,1,0:T(8,128)(2,1)}, bf16[8,8,4,16,256]{4,3,2,1,0:T(8,128)(2,1)}) custom-call(s32[4,8]{1,0:T(4,128)S(1)} %copy-done, bf16[8,4,2,16,2048]{4,3,2,1,0:T(8,128)(2,1)} %bitcast.4.qg_ref, bf16[8,8,4,16,256]{4,3,2,1,0:T(8,128)(2,1)} %bitcast.16), custom_call_target="tpu_custom_call" | custom-call | tf_op jit(solution)/shard_map/attend/pallas_call | solution.py:358
  109.5 0.0 reduce-scatter.2.cloned.1.call-update
  109.6 9.0 %all-to-all-start.2 = ((bf16[32,2,16,1024]{3,2,1,0:T(8,128)(2,1)}), bf16[32,2,16,1024]{3,2,1,0:T(8,128)(2,1)S(1)}, u32[]{:S(2)}, u32[]{:S(2)}) async-start(bf16[32,2,16,1024]{3,2,1,0:T(8,128)(2,1)} %bitcast.8), calls=%async_computation.2 | async-start | bytes 4194304 | tf_op jit(solution)/shard_map/all_to_all | solution.py:390
  118.6 33.5 %reduce-scatter.2.cloned.1.call-done = bf16[1,8,4,16,256]{4,3,2,1,0:T(8,128)(2,1)} async-done(((bf16[8,8,4,16,256]{4,3,2,1,0:T(8,128)(2,1)}), bf16[1,8,4,16,256]{4,3,2,1,0:T(8,128)(2,1)}) %reduce-scatter.2.cloned.1.call-update) | async-done | bytes 262160 | tf_op jit(solution)/shard_map/reduce_scatter | solution.py:402
  152.1 1.7 place_pair.1
  153.8 0.0 all-to-all-done.2
  153.8 11.4 %all-to-all-start.3 = ((bf16[32,2,16,256]{3,2,1,0:T(8,128)(2,1)}), bf16[32,2,16,256]{3,2,1,0:T(8,128)(2,1)S(1)}, u32[]{:S(2)}, u32[]{:S(2)}) async-start(bf16[32,2,16,256]{3,2,1,0:T(8,128)(2,1)} %bitcast.19), calls=%async_computation.4 | async-start | bytes 1048576 | tf_op jit(solution)/shard_map/all_to_all | solution.py:390
  165.3 3.1 %home_wide.1 = bf16[128,4096]{1,0:T(8,128)(2,1)} custom-call(s32[64]{0:T(128)} %dest.6, bf16[8,4,2,16,1024]{4,3,2,1,0:T(8,128)(2,1)} %bitcast.15), custom_call_target="tpu_custom_call" | custom-call | tf_op jit(solution)/shard_map/home_wide/pallas_call | solution.py:175
  168.4 7.9 %all-to-all-done.3 = bf16[32,2,16,256]{3,2,1,0:T(8,128)(2,1)S(1)} async-done(((bf16[32,2,16,256]{3,2,1,0:T(8,128)(2,1)}), bf16[32,2,16,256]{3,2,1,0:T(8,128)(2,1)S(1)}, u32[]{:S(2)}, u32[]{:S(2)}) %all-to-all-start.3) | async-done | bytes 524320 | tf_op jit(solution)/shard_map/all_to_all | solution.py:390
  176.3 0.8 copy-done.3
  177.1 2.4 %home_pair.1 = (bf16[128,512]{1,0:T(8,128)(2,1)}, bf16[128,512]{1,0:T(8,128)(2,1)}) custom-call(s32[64]{0:T(128)} %dest.6, bf16[8,4,2,16,256]{4,3,2,1,0:T(8,128)(2,1)} %bitcast.20), custom_call_target="tpu_custom_call" | custom-call | tf_op jit(solution)/shard_map/home_pair/pallas_call | solution.py:200
  (11 shorter events, 0.0 us)
Async XLA Ops:
  9.0 19.6 %all-to-all-start.1 = ((bf16[32,2,16,256]{3,2,1,0:T(8,128)(2,1)}), bf16[32,2,16,256]{3,2,1,0:T(8,128)(2,1)S(1)}, u32[]{:S(2)}, u32[]{:S(2)}) async-start(bf16[32,2,16,256]{3,2,1,0:T(8,128)(2,1)} %bitcast.18), calls=%async_computation.1 | async-start | bytes 1048576 | tf_op jit(solution)/shard_map/all_to_all | solution.py:390
  28.6 0.8 copy-start.2
  28.6 6.4 %copy-start.4 = (s32[64]{0:T(128)S(1)}, s32[64]{0:T(128)}, u32[]{:S(2)}) copy-start(s32[64]{0:T(128)} %param.13) | copy-start | bytes 772
  29.4 56.0 %all-to-all-start = ((bf16[32,2,16,2048]{3,2,1,0:T(8,128)(2,1)}), bf16[32,2,16,2048]{3,2,1,0:T(8,128)(2,1)}, u32[]{:S(2)}, u32[]{:S(2)}) async-start(bf16[32,2,16,2048]{3,2,1,0:T(8,128)(2,1)} %bitcast.14), calls=%async_computation | async-start | bytes 8388608 | tf_op jit(solution)/shard_map/all_to_all | solution.py:390
  34.8 50.6 %all-gather.3.cloned.1.call-start = ((), (), s32[]{:S(2)}) async-start(), calls=%async_computation.6 | async-start | bytes 2359296 | tf_op jit(solution)/shard_map/all_gather | solution.py:400
  38.6 113.5 %reduce-scatter.2.cloned.1.call-start = ((), (), s32[]{:S(2)}) async-start(), calls=%async_computation.5 | async-start | bytes 2359296 | tf_op jit(solution)/shard_map/reduce_scatter | solution.py:402
  85.5 0.7 copy-start
  109.6 44.3 %all-to-all-start.2 = ((bf16[32,2,16,1024]{3,2,1,0:T(8,128)(2,1)}), bf16[32,2,16,1024]{3,2,1,0:T(8,128)(2,1)S(1)}, u32[]{:S(2)}, u32[]{:S(2)}) async-start(bf16[32,2,16,1024]{3,2,1,0:T(8,128)(2,1)} %bitcast.8), calls=%async_computation.2 | async-start | bytes 4194304 | tf_op jit(solution)/shard_map/all_to_all | solution.py:390
  153.8 11.4 %copy-start.1 = (bf16[32,2,16,1024]{3,2,1,0:T(8,128)(2,1)}, bf16[32,2,16,1024]{3,2,1,0:T(8,128)(2,1)S(1)}, u32[]{:S(2)}) copy-start(bf16[32,2,16,1024]{3,2,1,0:T(8,128)(2,1)S(1)} %all-to-all-done.2) | copy-start | bytes 6291460
  153.8 22.4 %all-to-all-start.3 = ((bf16[32,2,16,256]{3,2,1,0:T(8,128)(2,1)}), bf16[32,2,16,256]{3,2,1,0:T(8,128)(2,1)S(1)}, u32[]{:S(2)}, u32[]{:S(2)}) async-start(bf16[32,2,16,256]{3,2,1,0:T(8,128)(2,1)} %bitcast.19), calls=%async_computation.4 | async-start | bytes 1048576 | tf_op jit(solution)/shard_map/all_to_all | solution.py:390
  176.3 0.8 copy-start.3
Sparse Core Ops, SparseCore 0:
  38.7 40.0 all-gather.2
  109.7 42.3 reduce-scatter.1

commit v2 on v1

v2 whole, which is shorter than its diff:
```python
import math

import jax
import jax.numpy as jnp
from jax import lax
from jax.experimental import pallas as pl
from jax.experimental.pallas import tpu as pltpu
from jax.sharding import Mesh, PartitionSpec as P

QUERY_HEADS = 32
KEY_HEADS = 4
HEAD = 128
SLOTS = 8
BLOCK = 512
PER_KEY = QUERY_HEADS // KEY_HEADS
WIDE = PER_KEY * HEAD
SOON = 2 * HEAD
LATER = WIDE - SOON
BR = 16
CAP = 2
N_DP = 8
N_Y = 4
N_Z = 8
HALF = BLOCK // 2
CHUNK = (SLOTS, N_Y, BR, HEAD)
SPAN = SLOTS // 2
NEG = -1.0e30
TILE = 256
SCALE = HEAD ** -0.5
EXP_SCALE = SCALE / math.log(2.0)
F32 = jnp.float32
BF16 = jnp.bfloat16
MIB = 1024 * 1024


def tables(doc_lengths, dest_group, dest_slot):
    me = lax.axis_index("dp")
    blocks = jnp.arange(SLOTS, dtype=jnp.int32)
    dest = dest_group.reshape(N_DP, SLOTS)
    slot = dest_slot.reshape(N_DP, SLOTS)
    earlier = (dest[:, :, None] == dest[:, None, :]) & (blocks[None, :] < blocks[:, None])[None]
    rank = jnp.sum(earlier.astype(jnp.int32), axis=2)
    mine = blocks == me
    hit = ((dest == me)[None] & (slot[None] == blocks[:, None, None])).astype(jnp.int32)
    from_group = jnp.sum(hit * blocks[None, :, None], axis=(1, 2))
    from_rank = jnp.sum(hit * rank[None], axis=(1, 2))
    lengths = jnp.sum(jnp.where(mine[:, None], doc_lengths, 0), axis=0)
    docs = jnp.arange(lengths.shape[0], dtype=jnp.int32)
    ends = jnp.sum(jnp.where(docs[None, :] <= docs[:, None], lengths[None, :], 0), axis=1)
    first = jnp.max(jnp.where(ends[None, :] <= blocks[:, None], ends[None, :], 0), axis=1)
    place = jnp.full((SLOTS,), lax.axis_index("z"), jnp.int32)
    return jnp.stack([from_group, from_rank, first, place]).astype(jnp.int32)


def params(mib):
    return pltpu.CompilerParams(vmem_limit_bytes=mib * MIB)


def to_source(s, t):
    return (t[0, s], 0, t[1, s], 0, 0)


def whole(space):
    return pl.BlockSpec(memory_space=space)


def route(dest):
    base = lax.axis_index("dp") * SLOTS
    groups = [dest[base + j] for j in range(SLOTS)]
    ranks = []
    for j in range(SLOTS):
        rank = jnp.int32(0)
        for i in range(j):
            rank = rank + jnp.where(groups[i] == groups[j], 1, 0).astype(jnp.int32)
        ranks.append(rank)
    return list(zip(groups, ranks))


def run(copies):
    for copy in copies:
        copy.start()
    for copy in copies:
        copy.wait()


def pack_first_body(dest, k, v, q, g, out, part, stage, get, put):
    gets = [pltpu.make_async_copy(x.at[:, pl.ds(h * WIDE + LATER, SOON)], part.at[n, h],
                                  get.at[n, h])
            for n, x in enumerate((q, g)) for h in range(KEY_HEADS)]
    run(gets)
    puts = []
    for j, (group, rank) in enumerate(route(dest)):
        rows = slice(j * BR, (j + 1) * BR)
        for h in range(KEY_HEADS):
            cols = slice(h * HEAD, (h + 1) * HEAD)
            stage[j, h, :, :HEAD] = k[rows, cols]
            stage[j, h, :, HEAD:2 * HEAD] = v[rows, cols]
            stage[j, h, :, 2 * HEAD:2 * HEAD + SOON] = part[0, h, rows]
            stage[j, h, :, 2 * HEAD + SOON:] = part[1, h, rows]
        puts.append(pltpu.make_async_copy(stage.at[j], out.at[group, :, rank], put.at[j]))
        puts[-1].start()
    for copy in puts:
        copy.wait()


def pack_first(dest, k, v, q, g):
    width = 2 * HEAD + 2 * SOON
    return pl.pallas_call(
        pack_first_body,
        in_specs=[whole(pltpu.SMEM), whole(pltpu.VMEM), whole(pltpu.VMEM), whole(pl.ANY),
                  whole(pl.ANY)],
        out_specs=whole(pl.ANY),
        out_shape=jax.ShapeDtypeStruct((N_DP, KEY_HEADS, CAP, BR, width), BF16),
        scratch_shapes=[
            pltpu.VMEM((2, KEY_HEADS, SLOTS * BR, SOON), BF16),
            pltpu.VMEM((SLOTS, KEY_HEADS, BR, width), BF16),
            pltpu.SemaphoreType.DMA((2, KEY_HEADS)),
            pltpu.SemaphoreType.DMA((SLOTS,)),
        ],
        name="pack_first",
    )(dest, k, v, q, g)


def pack_rest_body(dest, q, g, out, sem):
    copies = []
    for j, (group, rank) in enumerate(route(dest)):
        for h in range(KEY_HEADS):
            for n, x in enumerate((q, g)):
                copies.append(pltpu.make_async_copy(
                    x.at[pl.ds(j * BR, BR), pl.ds(h * WIDE, LATER)],
                    out.at[group, h, rank, :, pl.ds(n * LATER, LATER)],
                    sem.at[j, h, n]))
    run(copies)


def pack_rest(dest, q, g):
    return pl.pallas_call(
        pack_rest_body,
        in_specs=[whole(pltpu.SMEM), whole(pltpu.VMEM), whole(pltpu.VMEM)],
        out_specs=whole(pl.ANY),
        out_shape=jax.ShapeDtypeStruct((N_DP, KEY_HEADS, CAP, BR, 2 * LATER), BF16),
        scratch_shapes=[pltpu.SemaphoreType.DMA((SLOTS, KEY_HEADS, 2))],
        name="pack_rest",
    )(dest, q, g)


def pick_body(t, x, k, v, stage, get, put):
    run([pltpu.make_async_copy(x.at[t[0, s], :, t[1, s], :, pl.ds(n * HEAD, HEAD)],
                               stage.at[n, s], get.at[n, s])
         for s in range(SLOTS) for n in range(2)])
    run([pltpu.make_async_copy(stage.at[n], out, put.at[n]) for n, out in enumerate((k, v))])


def pick_pair(table, x):
    out = jax.ShapeDtypeStruct(CHUNK, BF16)
    return pl.pallas_call(
        pick_body,
        in_specs=[whole(pltpu.SMEM), whole(pl.ANY)],
        out_specs=[whole(pltpu.HBM), whole(pltpu.HBM)],
        out_shape=[out, out],
        scratch_shapes=[
            pltpu.VMEM((2,) + CHUNK, BF16),
            pltpu.SemaphoreType.DMA((2, SLOTS)),
            pltpu.SemaphoreType.DMA((2,)),
        ],
        name="pick_pair",
    )(table, x)


def place_body(t, ka, kb, kc, va, vb, vc, out, stage, sem):
    copies = []
    for s in range(SLOTS):
        for n, (a, b, c) in enumerate(((ka, kb, kc), (va, vb, vc))):
            total = a[s].astype(F32) + b[s].astype(F32) + c[s].astype(F32)
            stage[s, :, :, n * HEAD:(n + 1) * HEAD] = total.astype(BF16)
        copies.append(pltpu.make_async_copy(stage.at[s], out.at[t[0, s], :, t[1, s]], sem.at[s]))
    run(copies)


def place_pair(table, dk, dv):
    return pl.pallas_call(
        place_body,
        in_specs=[whole(pltpu.SMEM)] + [whole(pltpu.VMEM)] * 6,
        out_specs=whole(pl.ANY),
        out_shape=jax.ShapeDtypeStruct((N_DP, N_Y, CAP, BR, 2 * HEAD), BF16),
        scratch_shapes=[
            pltpu.VMEM((SLOTS, N_Y, BR, 2 * HEAD), BF16),
            pltpu.SemaphoreType.DMA((SLOTS,)),
        ],
        name="place_pair",
    )(table, *dk, *dv)


def home_wide_body(dest, x, out, sem):
    copies = []
    for j, (group, rank) in enumerate(route(dest)):
        for h in range(KEY_HEADS):
            copies.append(pltpu.make_async_copy(
                x.at[group, h, rank],
                out.at[pl.ds(j * BR, BR), pl.ds(h * WIDE, WIDE)],
                sem.at[j, h]))
    run(copies)


def home_wide(dest, x):
    return pl.pallas_call(
        home_wide_body,
        in_specs=[whole(pltpu.SMEM), whole(pl.ANY)],
        out_specs=whole(pltpu.VMEM),
        out_shape=jax.ShapeDtypeStruct((SLOTS * BR, QUERY_HEADS * HEAD), BF16),
        scratch_shapes=[pltpu.SemaphoreType.DMA((SLOTS, KEY_HEADS))],
        name="home_wide",
    )(dest, x)


def home_pair_body(dest, x, k, v, stage, sem):
    copies = []
    for j, (group, rank) in enumerate(route(dest)):
        copies.append(pltpu.make_async_copy(x.at[group, :, rank], stage.at[j], sem.at[j]))
    run(copies)
    for j in range(SLOTS):
        rows = slice(j * BR, (j + 1) * BR)
        for h in range(KEY_HEADS):
            cols = slice(h * HEAD, (h + 1) * HEAD)
            k[rows, cols] = stage[j, h, :, :HEAD]
            v[rows, cols] = stage[j, h, :, HEAD:]


def home_pair(dest, x):
    out = jax.ShapeDtypeStruct((SLOTS * BR, KEY_HEADS * HEAD), BF16)
    return pl.pallas_call(
        home_pair_body,
        in_specs=[whole(pltpu.SMEM), whole(pl.ANY)],
        out_specs=[whole(pltpu.VMEM), whole(pltpu.VMEM)],
        out_shape=[out, out],
        scratch_shapes=[
            pltpu.VMEM((SLOTS, KEY_HEADS, BR, 2 * HEAD), BF16),
            pltpu.SemaphoreType.DMA((SLOTS,)),
        ],
        name="home_pair",
    )(dest, x)


def dot_nt(a, b):
    return lax.dot_general(a, b, (((1,), (1,)), ((), ())), preferred_element_type=F32)


def dot_nn(a, b):
    return lax.dot_general(a, b, (((1,), (0,)), ((), ())), preferred_element_type=F32)


def fold_max(x):
    return jnp.max(x.reshape(x.shape[0] // 8, 8, x.shape[1]), axis=0)


def fold_sum(x):
    return jnp.sum(x.reshape(x.shape[0] // 8, 8, x.shape[1]), axis=0)


def attend_body(t, soon_hbm, rest_hbm, *refs):
    ins, refs = refs[:2 * N_Z], refs[2 * N_Z:]
    dq_hbm, outs, refs = refs[0], refs[1:1 + 2 * N_Z], refs[1 + 2 * N_Z:]
    (soon_buf, rest_buf, kv_buf, dq_buf, dkv_buf, ks, vs, kt, qm, gm, bias, sc, dp, acc_k, acc_v,
     dqt, qg_in, kv_in, dq_out, dkv_out) = refs
    bands = (pl.ds(SPAN, SPAN), pl.ds(0, SPAN))
    z = t[3, 0]
    spots = [pl.multiple_of((z + r) % N_Z * BR, BR) for r in range(N_Z)]

    def qg_copies(s):
        return (
            pltpu.make_async_copy(
                soon_hbm.at[t[0, s], :, t[1, s], :, pl.ds(2 * HEAD, 2 * SOON)], soon_buf.at[s],
                qg_in.at[0, s]),
            pltpu.make_async_copy(
                rest_hbm.at[t[0, s], :, t[1, s]], rest_buf.at[s], qg_in.at[1, s]))

    def kv_copies(n):
        return [pltpu.make_async_copy(ins[i].at[bands[n]], kv_buf.at[i, bands[n]], kv_in.at[n, i])
                for i in range(2 * N_Z)]

    def dkv_copies(n):
        return [pltpu.make_async_copy(dkv_buf.at[i, bands[n]], outs[i].at[bands[n]],
                                      dkv_out.at[n, i])
                for i in range(2 * N_Z)]

    def dq_copy(s):
        return pltpu.make_async_copy(dq_buf.at[s], dq_hbm.at[t[0, s], :, t[1, s]], dq_out.at[s])

    for n in range(2):
        for copy in qg_copies(SLOTS - 1 - n * SPAN):
            copy.start()
        for copy in kv_copies(n):
            copy.start()
        for s in range(1, SPAN):
            for copy in qg_copies(SLOTS - 1 - n * SPAN - s):
                copy.start()

    key = lax.broadcasted_iota(jnp.int32, (HALF, HALF), 0)
    lane = lax.broadcasted_iota(jnp.int32, (HALF, HALF), 1)
    query = (lane // HEAD) * HEAD + t[3, 0] * BR + lane % BR
    bias[...] = jnp.where(key <= query, 0.0, NEG).astype(F32)
    halves = (slice(0, HALF), slice(HALF, BLOCK))
    own = SPAN - 1

    def lay(n, ready):
        o = ready - 1

        @pl.when(o == SPAN - 1)
        def _():
            for copy in kv_copies(1):
                copy.wait()

        for y in range(N_Y):
            for r in range(N_Z):
                rows = pl.ds(y * HEAD + spots[r], BR)
                ks[o, rows] = kv_buf[r, o, y]
                vs[o, rows] = kv_buf[N_Z + r, o, y]
        kt[o] = ks[o].T
        acc_k[o] = jnp.zeros((BLOCK, HEAD), F32)
        acc_v[o] = jnp.zeros((BLOCK, HEAD), F32)
        return o

    def step(n, ready):
        s = SLOTS - 1 - n
        first = t[2, s]
        ready = lax.fori_loop(0, ready - first, lay, ready)
        for copy in qg_copies(s):
            copy.wait()
        for y in range(N_Y):
            for h in range(PER_KEY):
                rows = pl.ds(y * HEAD + h * BR, BR)
                late = h * HEAD < LATER
                buf, span = (rest_buf, LATER) if late else (soon_buf, SOON)
                at = h * HEAD if late else h * HEAD - LATER
                qm[rows, :] = buf[s, y, :, at:at + HEAD]
                gm[rows, :] = buf[s, y, :, span + at:span + at + HEAD]
        count = s - first

        def score_tile(o, at, keys, rows, masked):
            top = None
            for k0 in range(keys.start, keys.stop, TILE):
                part = slice(k0, k0 + TILE)
                x = dot_nt(ks[o, part], qm[rows])
                if masked:
                    x = x + bias[k0 - keys.start:k0 - keys.start + TILE]
                sc[at, part, rows] = x
                x = fold_max(x)
                top = x if top is None else jnp.maximum(top, x)
            return top

        low, high = halves
        tops = (score_tile(s, own, low, low, True),
                jnp.maximum(score_tile(s, own, low, high, False),
                            score_tile(s, own, high, high, True)))

        def score_step(i, tops):
            full = slice(0, BLOCK)
            return tuple(jnp.maximum(top, score_tile(first + i, i, full, rows, False))
                         for top, rows in zip(tops, halves))

        tops = lax.fori_loop(0, count, score_step, tops)
        tops = [jnp.max(top, axis=0, keepdims=True) for top in tops]

        def exp_tile(o, at, keys, rows, top):
            total = moment = None
            for k0 in range(keys.start, keys.stop, TILE):
                part = slice(k0, k0 + TILE)
                d = dot_nt(vs[o, part], gm[rows])
                e = jnp.exp2((sc[at, part, rows] - top) * EXP_SCALE)
                sc[at, part, rows] = e
                dp[at, part, rows] = d
                a, b = fold_sum(e), fold_sum(e * d)
                total = a if total is None else total + a
                moment = b if moment is None else moment + b
            return total, moment

        def add(x, y):
            return tuple(a + b for a, b in zip(x, y))

        sums = (exp_tile(s, own, low, low, tops[0]),
                add(exp_tile(s, own, low, high, tops[1]), exp_tile(s, own, high, high, tops[1])))

        def exp_step(i, sums):
            full = slice(0, BLOCK)
            return tuple(add(old, exp_tile(first + i, i, full, rows, top))
                         for old, rows, top in zip(sums, halves, tops))

        sums = lax.fori_loop(0, count, exp_step, sums)
        inverse, delta = [], []
        for total, moment in sums:
            inverse.append(1.0 / jnp.sum(total, axis=0, keepdims=True))
            delta.append(jnp.sum(moment, axis=0, keepdims=True) * inverse[-1])
        inverse = jnp.concatenate(inverse, axis=1)
        delta = jnp.concatenate(delta, axis=1)

        def grad_tile(o, at, keys, rows, fresh):
            for k0 in range(keys.start, keys.stop, TILE):
                part = slice(k0, k0 + TILE)
                p = sc[at, part, rows] * inverse[:, rows]
                w = p.astype(BF16)
                ds = (p * (dp[at, part, rows] - delta[:, rows])).astype(BF16)
                acc_v[o, part] += dot_nn(w, gm[rows])
                acc_k[o, part] += dot_nn(ds, qm[rows])
                term = dot_nn(kt[o, :, part], ds)
                if fresh and k0 == keys.start:
                    dqt[:, rows] = term
                else:
                    dqt[:, rows] += term

        grad_tile(s, own, low, slice(0, BLOCK), True)
        grad_tile(s, own, high, high, False)

        def grad_step(i, carry):
            grad_tile(first + i, i, slice(0, BLOCK), slice(0, BLOCK), False)
            return carry

        lax.fori_loop(0, count, grad_step, 0)

        dq = (dqt[...] * SCALE).T.astype(BF16)
        for y in range(N_Y):
            for h in range(PER_KEY):
                at = y * HEAD + h * BR
                dq_buf[s, y, :, h * HEAD:(h + 1) * HEAD] = dq[at:at + BR]
            for r in range(N_Z):
                rows = pl.ds(y * HEAD + spots[r], BR)
                dkv_buf[r, s, y] = (acc_k[s, rows] * SCALE).astype(BF16)
                dkv_buf[N_Z + r, s, y] = acc_v[s, rows].astype(BF16)
        dq_copy(s).start()

        @pl.when(s == SPAN)
        def _():
            for copy in dkv_copies(0):
                copy.start()

        return ready

    for copy in kv_copies(0):
        copy.wait()
    lax.fori_loop(0, SLOTS, step, SLOTS)
    for copy in dkv_copies(1):
        copy.start()
    for n in range(2):
        for copy in dkv_copies(n):
            copy.wait()
    for s in reversed(range(SLOTS)):
        dq_copy(s).wait()


def attend(table, soon, rest, kv):
    out = pl.pallas_call(
        attend_body,
        in_specs=[whole(pltpu.SMEM), whole(pl.ANY), whole(pl.ANY)]
        + [whole(pltpu.HBM)] * (2 * N_Z),
        out_specs=[whole(pl.ANY)] + [whole(pltpu.HBM)] * (2 * N_Z),
        scratch_shapes=[
            pltpu.VMEM((SLOTS, N_Y, BR, 2 * SOON), BF16),
            pltpu.VMEM((SLOTS, N_Y, BR, 2 * LATER), BF16),
            pltpu.VMEM((2 * N_Z,) + CHUNK, BF16),
            pltpu.VMEM((SLOTS, N_Y, BR, WIDE), BF16),
            pltpu.VMEM((2 * N_Z,) + CHUNK, BF16),
            pltpu.VMEM((SLOTS, BLOCK, HEAD), BF16),
            pltpu.VMEM((SLOTS, BLOCK, HEAD), BF16),
            pltpu.VMEM((SLOTS, HEAD, BLOCK), BF16),
            pltpu.VMEM((BLOCK, HEAD), BF16),
            pltpu.VMEM((BLOCK, HEAD), BF16),
            pltpu.VMEM((HALF, HALF), F32),
            pltpu.VMEM((SPAN, BLOCK, BLOCK), F32),
            pltpu.VMEM((SPAN, BLOCK, BLOCK), F32),
            pltpu.VMEM((SLOTS, BLOCK, HEAD), F32),
            pltpu.VMEM((SLOTS, BLOCK, HEAD), F32),
            pltpu.VMEM((HEAD, BLOCK), F32),
            pltpu.SemaphoreType.DMA((2, SLOTS)),
            pltpu.SemaphoreType.DMA((2, 2 * N_Z)),
            pltpu.SemaphoreType.DMA((SLOTS,)),
            pltpu.SemaphoreType.DMA((2, 2 * N_Z)),
        ],
        out_shape=[jax.ShapeDtypeStruct((N_DP, N_Y, CAP, BR, WIDE), BF16)]
        + [jax.ShapeDtypeStruct(CHUNK, BF16)] * (2 * N_Z),
        compiler_params=params(63),
        name="attend",
    )(table, soon, rest, *kv)
    return out[0], out[1:1 + N_Z], out[1 + N_Z:]


def hop(x, step):
    return lax.ppermute(x, "z", [(i, (i + step) % N_Z) for i in range(N_Z)])


def spread(x):
    out = [x] * N_Z
    left = right = x
    for r in range(1, N_Z // 2 + 1):
        left = hop(left, -1)
        out[r] = left
        if r < N_Z // 2:
            right = hop(right, 1)
            out[N_Z - r] = right
    return out


def collect(chunks):
    half = N_Z // 2
    left, right = hop(chunks[half], -1), hop(chunks[half - 1], 1)
    for n in range(1, half):
        left = hop(plus(left, chunks[half + n]), -1)
        if n < half - 1:
            right = hop(plus(right, chunks[half - 1 - n]), 1)
    return left, right, chunks[0]


def plus(a, b):
    return (a.astype(F32) + b.astype(F32)).astype(BF16)


def swap(x):
    flat = x.reshape((N_DP * N_Y,) + x.shape[2:])
    return lax.all_to_all(flat, ("dp", "y"), 0, 0, tiled=True).reshape(x.shape)


def shards(queries, keys, values, output_gradient, doc_lengths, dest_group, dest_slot):
    packed = pack_first(dest_group, keys, values, queries, output_gradient)
    doc_lengths, dest_slot, late, packed = lax.optimization_barrier(
        (doc_lengths, dest_slot, dest_group, packed))
    arrived = swap(packed)
    rest = pack_rest(late, queries, output_gradient)
    table = tables(doc_lengths, late, dest_slot)
    k, v = pick_pair(table, arrived)
    dq, dk, dv = attend(table, arrived, swap(rest), spread(k) + spread(v))
    dq, pair = lax.optimization_barrier((swap(dq), place_pair(table, collect(dk), collect(dv))))
    grad_q = home_wide(dest_group, dq)
    key_gradient, value_gradient = home_pair(dest_group, swap(pair))
    return grad_q, key_gradient, value_gradient


def solution(mesh):
    grid = Mesh(mesh.devices.reshape(N_DP, N_Y, N_Z), ("dp", "y", "z"))
    rows = P(("dp", "y", "z"), None)
    return jax.shard_map(
        shards,
        mesh=grid,
        in_specs=(rows, rows, rows, rows, P(), P(), P()),
        out_specs=(rows, rows, rows),
        check_vma=False,
    )
```

time: 187 us -> 170 us (0.909)
  waiting for transfers between devices: 93.9 us -> 37.5 us
  starting transfers between devices: 34.5 us -> 83.5 us
  between operations: 14.2 us -> 1.36 us
  Pallas kernels: 38.3 us -> 40.9 us
    ppermute x0 -> x28, starting transfers between devices: none -> 51 us  [hop(): return lax.ppermute(x, 'z', [(i, (i + step) % N_Z) for i in range(N_Z)])]
    reduce_scatter x1 -> x0, waiting for transfers between devices: 33.5 us -> none  [shards(): dkv = lax.psum_scatter(dkv, 'z', scatter_dimension=0, tiled=False)]
    all_to_all x4, waiting for transfers between devices: 60.3 us -> 29.9 us  [swap(): return lax.all_to_all(flat, ('dp', 'y'), 0, 0, tiled=True).reshape(x.shape)]
    ppermute x0 -> x28, waiting for transfers between devices: none -> 7.59 us  [hop(): return lax.ppermute(x, 'z', [(i, (i + step) % N_Z) for i in range(N_Z)])]
    pallas_call x4, Pallas kernels: 30.4 us -> 32.9 us  [the longest x1 24.4 us: attend(): pl.pallas_call(attend_body, in_specs=[whole(pltpu.SMEM), whole(pl.ANY), w...]
    all_to_all x4, starting transfers between devices: 34.4 us -> 32.4 us  [swap(): return lax.all_to_all(flat, ('dp', 'y'), 0, 0, tiled=True).reshape(x.shape)]
    unnamed x10 -> x72, local copies, waits for them, and re-layouts: 2.26 us -> 4.09 us
  transfers between devices with their start and end apart: 6 -> 32, of which waited for: 4 -> 12; matrix products, arithmetic and copies ran while one was open for 2% -> 1% of each run, Pallas kernels for 6% -> 6%
where the time goes in v2:
time: 170 us
  starting transfers between devices  83.5 us (49%)
  Pallas kernels  40.9 us (24%)
  waiting for transfers between devices  37.5 us (22%)
  local copies, waits for them, and re-layouts  4.32 us (3%)
  other arithmetic  2.06 us (1%)
    ppermute x28, starting transfers between devices, hop(): return lax.ppermute(x, 'z', [(i, (i + step) % N_Z) for i in range(N_Z)])  51 us
    all_to_all x4, starting transfers between devices, swap(): return lax.all_to_all(flat, ('dp', 'y'), 0, 0, tiled=True).reshape(x.shape)  32.4 us
    all_to_all x4, waiting for transfers between devices, swap(): return lax.all_to_all(flat, ('dp', 'y'), 0, 0, tiled=True).reshape(x.shape)  29.9 us
    pallas_call x1, Pallas kernels, attend(): pl.pallas_call(attend_body, in_specs=[whole(pltpu.SMEM), whole(pl.ANY), w...  24.4 us
    ppermute x28, waiting for transfers between devices, hop(): return lax.ppermute(x, 'z', [(i, (i + step) % N_Z) for i in range(N_Z)])  7.59 us
    unnamed x72, local copies, waits for them, and re-layouts  4.09 us
  transfers between devices with their start and end apart: 32, of which 12 were waited for; matrix products, arithmetic and copies ran while one was open for 1% of the time, Pallas kernels for 6%

profile of v2, /device:TPU:1, one launch (start us, length us, event | category | flops | bytes accessed | tf_op | source)
XLA Modules:
  0.0 169.6 jit_solution(10114583098706036660)
XLA Ops:
  0.6 3.1 %pack_first.1 = bf16[8,4,2,16,768]{4,3,2,1,0:T(8,128)(2,1)} custom-call(s32[64]{0:T(128)} %dest.6, bf16[128,512]{1,0:T(8,128)(2,1)} %k.1, bf16[128,512]{1,0:T(8,128)(2,1)} %v.1, bf16[128,4096]{1,0:T(8,128)(2,1)} %q.3, bf16[128,4096]{1,0:T(8,128)(2,1)} %g.3), custom_call_target="tpu_custom_call" | custom-call | tf_op jit(solution)/shard_map/pack_first/pallas_call | solution.py:108
  3.8 8.6 %all-to-all-start = ((bf16[32,2,16,768]{3,2,1,0:T(8,128)(2,1)}), bf16[32,2,16,768]{3,2,1,0:T(8,128)(2,1)S(1)}, u32[]{:S(2)}, u32[]{:S(2)}) async-start(bf16[32,2,16,768]{3,2,1,0:T(8,128)(2,1)} %bitcast.16), calls=%async_computation | async-start | bytes 3145728 | tf_op jit(solution)/shard_map/all_to_all | solution.py:517
  12.4 3.3 %pack_rest.1 = bf16[8,4,2,16,1536]{4,3,2,1,0:T(8,128)(2,1)} custom-call(s32[64]{0:T(128)} %dest.6, bf16[128,4096]{1,0:T(8,128)(2,1)} %q.3, bf16[128,4096]{1,0:T(8,128)(2,1)} %g.3), custom_call_target="tpu_custom_call" | custom-call | tf_op jit(solution)/shard_map/pack_rest/pallas_call | solution.py:137
  15.7 18.2 %all-to-all-done = bf16[32,2,16,768]{3,2,1,0:T(8,128)(2,1)S(1)} async-done(((bf16[32,2,16,768]{3,2,1,0:T(8,128)(2,1)}), bf16[32,2,16,768]{3,2,1,0:T(8,128)(2,1)S(1)}, u32[]{:S(2)}, u32[]{:S(2)}) %all-to-all-start) | async-done | bytes 1572896 | tf_op jit(solution)/shard_map/all_to_all | solution.py:517
  33.9 1.2 copy-done
  35.1 5.9 %all-to-all-start.1 = ((bf16[32,2,16,1536]{3,2,1,0:T(8,128)(2,1)}), bf16[32,2,16,1536]{3,2,1,0:T(8,128)(2,1)}, u32[]{:S(2)}, u32[]{:S(2)}) async-start(bf16[32,2,16,1536]{3,2,1,0:T(8,128)(2,1)} %bitcast.14), calls=%async_computation.1 | async-start | bytes 6291456 | tf_op jit(solution)/shard_map/all_to_all | solution.py:517
  43.0 2.5 %pick_pair.1 = (bf16[8,4,16,128]{3,2,1,0:T(8,128)(2,1)}, bf16[8,4,16,128]{3,2,1,0:T(8,128)(2,1)}) custom-call(s32[4,8]{1,0:T(4,128)} %add_add_fusion.t, bf16[8,4,2,16,768]{4,3,2,1,0:T(8,128)(2,1)} %bitcast.12), custom_call_target="tpu_custom_call" | custom-call | tf_op jit(solution)/shard_map/pick_pair/pallas_call | solution.py:156
  45.4 5.7 %collective-permute-start = (bf16[8,4,16,128]{3,2,1,0:T(8,128)(2,1)}, bf16[8,4,16,128]{3,2,1,0:T(8,128)(2,1)S(1)}, u32[]{:S(2)}, u32[]{:S(2)}) collective-permute-start(bf16[8,4,16,128]{3,2,1,0:T(8,128)(2,1)} %get-tuple-element.34.refs_0_), channel_id=1, source_target_pairs={{0,7},{1,0},{2,1},{3,2},{4,3},{5,4},{6,5},{7,6},{8,15},{9,8},{10,9... | collective-permute-start | bytes 393224 | tf_op jit(solution)/shard_map/ppermute | solution.py:486
  52.6 1.3 collective-permute-done.refs_1_
  53.9 3.4 %collective-permute-start.1 = (bf16[8,4,16,128]{3,2,1,0:T(8,128)(2,1)S(1)}, bf16[8,4,16,128]{3,2,1,0:T(8,128)(2,1)S(1)}, u32[]{:S(2)}, u32[]{:S(2)}) collective-permute-start(bf16[8,4,16,128]{3,2,1,0:T(8,128)(2,1)S(1)} %collective-permute-done.refs_1_), channel_id=1, source_target_pairs={{0,7},{1,0},{2,1},{3,2},{4,3},{5,4},{6,5},{7,6},{8,15},{9,8},{10,9... | collective-permute-start | bytes 393224 | tf_op jit(solution)/shard_map/ppermute | solution.py:486
  57.3 2.8 %collective-permute-start.8 = (bf16[8,4,16,128]{3,2,1,0:T(8,128)(2,1)S(1)}, bf16[8,4,16,128]{3,2,1,0:T(8,128)(2,1)S(1)}, u32[]{:S(2)}, u32[]{:S(2)}) collective-permute-start(bf16[8,4,16,128]{3,2,1,0:T(8,128)(2,1)S(1)} %collective-permute-done.7.refs_9_), channel_id=1, source_target_pairs={{0,7},{1,0},{2,1},{3,2},{4,3},{5,4},{6,5},{7,6},{8,15},{9,8},{10,9... | collective-permute-start | bytes 393224 | tf_op jit(solution)/shard_map/ppermute | solution.py:486
  60.3 2.6 %collective-permute-start.2 = (bf16[8,4,16,128]{3,2,1,0:T(8,128)(2,1)S(1)}, bf16[8,4,16,128]{3,2,1,0:T(8,128)(2,1)S(1)}, u32[]{:S(2)}, u32[]{:S(2)}) collective-permute-start(bf16[8,4,16,128]{3,2,1,0:T(8,128)(2,1)S(1)} %collective-permute-done.1.refs_2_), channel_id=1, source_target_pairs={{0,7},{1,0},{2,1},{3,2},{4,3},{5,4},{6,5},{7,6},{8,15},{9,8},{10,9... | collective-permute-start | bytes 393224 | tf_op jit(solution)/shard_map/ppermute | solution.py:486
  63.3 3.5 %collective-permute-start.9 = (bf16[8,4,16,128]{3,2,1,0:T(8,128)(2,1)S(1)}, bf16[8,4,16,128]{3,2,1,0:T(8,128)(2,1)S(1)}, u32[]{:S(2)}, u32[]{:S(2)}) collective-permute-start(bf16[8,4,16,128]{3,2,1,0:T(8,128)(2,1)S(1)} %collective-permute-done.8.refs_10_), channel_id=1, source_target_pairs={{0,7},{1,0},{2,1},{3,2},{4,3},{5,4},{6,5},{7,6},{8,15},{9,8},{10,9... | collective-permute-start | bytes 393224 | tf_op jit(solution)/shard_map/ppermute | solution.py:486
  67.9 2.7 %collective-permute-start.3 = (bf16[8,4,16,128]{3,2,1,0:T(8,128)(2,1)S(1)}, bf16[8,4,16,128]{3,2,1,0:T(8,128)(2,1)S(1)}, u32[]{:S(2)}, u32[]{:S(2)}) collective-permute-start(bf16[8,4,16,128]{3,2,1,0:T(8,128)(2,1)S(1)} %collective-permute-done.2.refs_3_), channel_id=1, source_target_pairs={{0,7},{1,0},{2,1},{3,2},{4,3},{5,4},{6,5},{7,6},{8,15},{9,8},{10,9... | collective-permute-start | bytes 393224 | tf_op jit(solution)/shard_map/ppermute | solution.py:486
  70.5 3.0 %collective-permute-start.10 = (bf16[8,4,16,128]{3,2,1,0:T(8,128)(2,1)S(1)}, bf16[8,4,16,128]{3,2,1,0:T(8,128)(2,1)}, u32[]{:S(2)}, u32[]{:S(2)}) collective-permute-start(bf16[8,4,16,128]{3,2,1,0:T(8,128)(2,1)S(1)} %collective-permute-done.9.refs_11_), channel_id=1, source_target_pairs={{0,7},{1,0},{2,1},{3,2},{4,3},{5,4},{6,5},{7,6},{8,15},{9,8},{10,9... | collective-permute-start | bytes 393224 | tf_op jit(solution)/shard_map/ppermute | solution.py:486
  76.0 3.8 %all-to-all-done.1 = bf16[32,2,16,1536]{3,2,1,0:T(8,128)(2,1)} async-done(((bf16[32,2,16,1536]{3,2,1,0:T(8,128)(2,1)}), bf16[32,2,16,1536]{3,2,1,0:T(8,128)(2,1)}, u32[]{:S(2)}, u32[]{:S(2)}) %all-to-all-start.1) | async-done | bytes 3145760 | tf_op jit(solution)/shard_map/all_to_all | solution.py:517
  79.9 24.4 %attend.1 = (bf16[8,4,2,16,1024]{4,3,2,1,0:T(8,128)(2,1)}, bf16[8,4,16,128]{3,2,1,0:T(8,128)(2,1)}, bf16[8,4,16,128]{3,2,1,0:T(8,128)(2,1)}, bf16[8,4,16,128]{3,...) custom-call(s32[4,8]{1,0:T(4,128)} %add_add_fusion.t, ...), custom_call_target="tpu_custom_call" | custom-call | tf_op jit(solution)/shard_map/attend/pallas_call | solution.py:450
  104.3 5.7 %collective-permute-start.14 = (bf16[8,4,16,128]{3,2,1,0:T(8,128)(2,1)}, bf16[8,4,16,128]{3,2,1,0:T(8,128)(2,1)S(1)}, u32[]{:S(2)}, u32[]{:S(2)}) collective-permute-start(bf16[8,4,16,128]{3,2,1,0:T(8,128)(2,1)} %get-tuple-element.37), channel_id=1, source_target_pairs={{0,7},{1,0},{2,1},{3,2},{4,3},{5,4},{6,5},{7,6},{8,15},{9,8},{10,9... | collective-permute-start | bytes 393224 | tf_op jit(solution)/shard_map/ppermute | solution.py:486
  110.1 7.2 %all-to-all-start.2 = ((bf16[32,2,16,1024]{3,2,1,0:T(8,128)(2,1)}), bf16[32,2,16,1024]{3,2,1,0:T(8,128)(2,1)S(1)}, u32[]{:S(2)}, u32[]{:S(2)}) async-start(bf16[32,2,16,1024]{3,2,1,0:T(8,128)(2,1)} %bitcast.18), calls=%async_computation.2 | async-start | bytes 4194304 | tf_op jit(solution)/shard_map/all_to_all | solution.py:517
  117.5 2.7 %collective-permute-start.21 = (bf16[8,4,16,128]{3,2,1,0:T(8,128)(2,1)S(1)}, bf16[8,4,16,128]{3,2,1,0:T(8,128)(2,1)S(1)}, u32[]{:S(2)}, u32[]{:S(2)}) collective-permute-start(bf16[8,4,16,128]{3,2,1,0:T(8,128)(2,1)S(1)} %copy-done.34), channel_id=1, source_target_pairs={{0,7},{1,0},{2,1},{3,2},{4,3},{5,4},{6,5},{7,6},{8,15},{9,8},{10,9... | collective-permute-start | bytes 393224 | tf_op jit(solution)/shard_map/ppermute | solution.py:486
  120.2 2.7 %collective-permute-start.15 = (bf16[8,4,16,128]{3,2,1,0:T(8,128)(2,1)S(1)}, bf16[8,4,16,128]{3,2,1,0:T(8,128)(2,1)S(1)}, u32[]{:S(2)}, u32[]{:S(2)}) collective-permute-start(bf16[8,4,16,128]{3,2,1,0:T(8,128)(2,1)S(1)} %add_convert_fusion.9), channel_id=1, source_target_pairs={{0,7},{1,0},{2,1},{3,2},{4,3},{5,4},{6,5},{7,6},{8,15},{9,8},{10,9... | collective-permute-start | bytes 393224 | tf_op jit(solution)/shard_map/ppermute | solution.py:486
  123.7 2.7 %collective-permute-start.22 = (bf16[8,4,16,128]{3,2,1,0:T(8,128)(2,1)S(1)}, bf16[8,4,16,128]{3,2,1,0:T(8,128)(2,1)S(1)}, u32[]{:S(2)}, u32[]{:S(2)}) collective-permute-start(bf16[8,4,16,128]{3,2,1,0:T(8,128)(2,1)S(1)} %add_convert_fusion.4), channel_id=1, source_target_pairs={{0,7},{1,0},{2,1},{3,2},{4,3},{5,4},{6,5},{7,6},{8,15},{9,8},{10,9... | collective-permute-start | bytes 393224 | tf_op jit(solution)/shard_map/ppermute | solution.py:486
  126.7 2.7 %collective-permute-start.16 = (bf16[8,4,16,128]{3,2,1,0:T(8,128)(2,1)S(1)}, bf16[8,4,16,128]{3,2,1,0:T(8,128)(2,1)S(1)}, u32[]{:S(2)}, u32[]{:S(2)}) collective-permute-start(bf16[8,4,16,128]{3,2,1,0:T(8,128)(2,1)S(1)} %add_convert_fusion.8), channel_id=1, source_target_pairs={{0,7},{1,0},{2,1},{3,2},{4,3},{5,4},{6,5},{7,6},{8,15},{9,8},{10,9... | collective-permute-start | bytes 393224 | tf_op jit(solution)/shard_map/ppermute | solution.py:486
  129.6 2.9 %collective-permute-start.23 = (bf16[8,4,16,128]{3,2,1,0:T(8,128)(2,1)S(1)}, bf16[8,4,16,128]{3,2,1,0:T(8,128)(2,1)S(1)}, u32[]{:S(2)}, u32[]{:S(2)}) collective-permute-start(bf16[8,4,16,128]{3,2,1,0:T(8,128)(2,1)S(1)} %add_convert_fusion.3), channel_id=1, source_target_pairs={{0,7},{1,0},{2,1},{3,2},{4,3},{5,4},{6,5},{7,6},{8,15},{9,8},{10,9... | collective-permute-start | bytes 393224 | tf_op jit(solution)/shard_map/ppermute | solution.py:486
  132.8 2.7 %collective-permute-start.17 = (bf16[8,4,16,128]{3,2,1,0:T(8,128)(2,1)S(1)}, bf16[8,4,16,128]{3,2,1,0:T(8,128)(2,1)S(1)}, u32[]{:S(2)}, u32[]{:S(2)}) collective-permute-start(bf16[8,4,16,128]{3,2,1,0:T(8,128)(2,1)S(1)} %add_convert_fusion.7), channel_id=1, source_target_pairs={{0,7},{1,0},{2,1},{3,2},{4,3},{5,4},{6,5},{7,6},{8,15},{9,8},{10,9... | collective-permute-start | bytes 393224 | tf_op jit(solution)/shard_map/ppermute | solution.py:486
  135.5 3.1 %collective-permute-start.24 = (bf16[8,4,16,128]{3,2,1,0:T(8,128)(2,1)S(1)}, bf16[8,4,16,128]{3,2,1,0:T(8,128)(2,1)S(1)}, u32[]{:S(2)}, u32[]{:S(2)}) collective-permute-start(bf16[8,4,16,128]{3,2,1,0:T(8,128)(2,1)S(1)} %add_convert_fusion.2), channel_id=1, source_target_pairs={{0,7},{1,0},{2,1},{3,2},{4,3},{5,4},{6,5},{7,6},{8,15},{9,8},{10,9... | collective-permute-start | bytes 393224 | tf_op jit(solution)/shard_map/ppermute | solution.py:486
  138.9 2.8 %collective-permute-done.24.va = bf16[8,4,16,128]{3,2,1,0:T(8,128)(2,1)S(1)} collective-permute-done((bf16[8,4,16,128]{3,2,1,0:T(8,128)(2,1)S(1)}, bf16[8,4,16,128]{3,2,1,0:T(8,128)(2,1)S(1)}, u32[]{:S(2)}, u32[]{:S(2)}) %collective-permute-start.24) | collective-permute-done | bytes 131104 | tf_op jit(solution)/shard_map/ppermute | solution.py:486
  142.4 2.1 %place_pair.1 = bf16[8,4,2,16,256]{4,3,2,1,0:T(8,128)(2,1)} custom-call(s32[4,8]{1,0:T(4,128)} %add_add_fusion.t, bf16[8,4,16,128]{3,2,1,0:T(8,128)(2,1)} %copy-done.28, bf16[8,4,16,128]{3,2,1,0:T(8,128)(2,1)} %copy-done.23, bf16[8,4,16,128]{3,2,1,0:T(8,128)(2,1)} %get-tuple-element.44.kc, bf16[8,4,16,128]{3,2,1,0:T(8,128)(2,1)} %copy-done.29, ...), custom_call_target="tpu_custom_call" | custom-call | tf_op jit(solution)/shard_map/place_pair/pallas_call | solution.py:181
  144.5 10.7 %all-to-all-start.3 = ((bf16[32,2,16,256]{3,2,1,0:T(8,128)(2,1)}), bf16[32,2,16,256]{3,2,1,0:T(8,128)(2,1)S(1)}, u32[]{:S(2)}, u32[]{:S(2)}) async-start(bf16[32,2,16,256]{3,2,1,0:T(8,128)(2,1)} %bitcast.17), calls=%async_computation.3 | async-start | bytes 1048576 | tf_op jit(solution)/shard_map/all_to_all | solution.py:517
  155.2 3.1 %home_wide.1 = bf16[128,4096]{1,0:T(8,128)(2,1)} custom-call(s32[64]{0:T(128)} %dest.6, bf16[8,4,2,16,1024]{4,3,2,1,0:T(8,128)(2,1)} %bitcast.15), custom_call_target="tpu_custom_call" | custom-call | tf_op jit(solution)/shard_map/home_wide/pallas_call | solution.py:206
  158.3 7.9 %all-to-all-done.3 = bf16[32,2,16,256]{3,2,1,0:T(8,128)(2,1)S(1)} async-done(((bf16[32,2,16,256]{3,2,1,0:T(8,128)(2,1)}), bf16[32,2,16,256]{3,2,1,0:T(8,128)(2,1)S(1)}, u32[]{:S(2)}, u32[]{:S(2)}) %all-to-all-start.3) | async-done | bytes 524320 | tf_op jit(solution)/shard_map/all_to_all | solution.py:517
  167.0 2.4 %home_pair.1 = (bf16[128,512]{1,0:T(8,128)(2,1)}, bf16[128,512]{1,0:T(8,128)(2,1)}) custom-call(s32[64]{0:T(128)} %dest.6, bf16[8,4,2,16,256]{4,3,2,1,0:T(8,128)(2,1)} %bitcast.19), custom_call_target="tpu_custom_call" | custom-call | tf_op jit(solution)/shard_map/home_pair/pallas_call | solution.py:231
  (133 shorter events, 10.6 us)
Async XLA Ops:
  3.8 30.1 %all-to-all-start = ((bf16[32,2,16,768]{3,2,1,0:T(8,128)(2,1)}), bf16[32,2,16,768]{3,2,1,0:T(8,128)(2,1)S(1)}, u32[]{:S(2)}, u32[]{:S(2)}) async-start(bf16[32,2,16,768]{3,2,1,0:T(8,128)(2,1)} %bitcast.16), calls=%async_computation | async-start | bytes 3145728 | tf_op jit(solution)/shard_map/all_to_all | solution.py:517
  35.1 44.7 %all-to-all-start.1 = ((bf16[32,2,16,1536]{3,2,1,0:T(8,128)(2,1)}), bf16[32,2,16,1536]{3,2,1,0:T(8,128)(2,1)}, u32[]{:S(2)}, u32[]{:S(2)}) async-start(bf16[32,2,16,1536]{3,2,1,0:T(8,128)(2,1)} %bitcast.14), calls=%async_computation.1 | async-start | bytes 6291456 | tf_op jit(solution)/shard_map/all_to_all | solution.py:517
  45.4 8.5 %collective-permute-start = (bf16[8,4,16,128]{3,2,1,0:T(8,128)(2,1)}, bf16[8,4,16,128]{3,2,1,0:T(8,128)(2,1)S(1)}, u32[]{:S(2)}, u32[]{:S(2)}) collective-permute-start(bf16[8,4,16,128]{3,2,1,0:T(8,128)(2,1)} %get-tuple-element.34.refs_0_), channel_id=1, source_target_pairs={{0,7},{1,0},{2,1},{3,2},{4,3},{5,4},{6,5},{7,6},{8,15},{9,8},{10,9... | collective-permute-start | bytes 393224 | tf_op jit(solution)/shard_map/ppermute | solution.py:486
  51.1 6.2 %collective-permute-start.7 = (bf16[8,4,16,128]{3,2,1,0:T(8,128)(2,1)}, bf16[8,4,16,128]{3,2,1,0:T(8,128)(2,1)S(1)}, u32[]{:S(2)}, u32[]{:S(2)}) collective-permute-start(bf16[8,4,16,128]{3,2,1,0:T(8,128)(2,1)} %get-tuple-element.35.refs_8_), channel_id=1, source_target_pairs={{0,7},{1,0},{2,1},{3,2},{4,3},{5,4},{6,5},{7,6},{8,15},{9,8},{10,9... | collective-permute-start | bytes 393224 | tf_op jit(solution)/shard_map/ppermute | solution.py:486
  51.8 8.3 %collective-permute-start.4 = (bf16[8,4,16,128]{3,2,1,0:T(8,128)(2,1)}, bf16[8,4,16,128]{3,2,1,0:T(8,128)(2,1)S(1)}, u32[]{:S(2)}, u32[]{:S(2)}) collective-permute-start(bf16[8,4,16,128]{3,2,1,0:T(8,128)(2,1)} %get-tuple-element.34.refs_0_), channel_id=1, source_target_pairs={{0,1},{1,2},{2,3},{3,4},{4,5},{5,6},{6,7},{7,0},{8,9},{9,10},{10,1... | collective-permute-start | bytes 393224 | tf_op jit(solution)/shard_map/ppermute | solution.py:486
  52.6 7.6 %collective-permute-start.11 = (bf16[8,4,16,128]{3,2,1,0:T(8,128)(2,1)}, bf16[8,4,16,128]{3,2,1,0:T(8,128)(2,1)S(1)}, u32[]{:S(2)}, u32[]{:S(2)}) collective-permute-start(bf16[8,4,16,128]{3,2,1,0:T(8,128)(2,1)} %get-tuple-element.35.refs_8_), channel_id=1, source_target_pairs={{0,1},{1,2},{2,3},{3,4},{4,5},{5,6},{6,7},{7,0},{8,9},{9,10},{10,1... | collective-permute-start | bytes 393224 | tf_op jit(solution)/shard_map/ppermute | solution.py:486
  53.9 6.3 %collective-permute-start.1 = (bf16[8,4,16,128]{3,2,1,0:T(8,128)(2,1)S(1)}, bf16[8,4,16,128]{3,2,1,0:T(8,128)(2,1)S(1)}, u32[]{:S(2)}, u32[]{:S(2)}) collective-permute-start(bf16[8,4,16,128]{3,2,1,0:T(8,128)(2,1)S(1)} %collective-permute-done.refs_1_), channel_id=1, source_target_pairs={{0,7},{1,0},{2,1},{3,2},{4,3},{5,4},{6,5},{7,6},{8,15},{9,8},{10,9... | collective-permute-start | bytes 393224 | tf_op jit(solution)/shard_map/ppermute | solution.py:486
  57.3 6.0 %collective-permute-start.8 = (bf16[8,4,16,128]{3,2,1,0:T(8,128)(2,1)S(1)}, bf16[8,4,16,128]{3,2,1,0:T(8,128)(2,1)S(1)}, u32[]{:S(2)}, u32[]{:S(2)}) collective-permute-start(bf16[8,4,16,128]{3,2,1,0:T(8,128)(2,1)S(1)} %collective-permute-done.7.refs_9_), channel_id=1, source_target_pairs={{0,7},{1,0},{2,1},{3,2},{4,3},{5,4},{6,5},{7,6},{8,15},{9,8},{10,9... | collective-permute-start | bytes 393224 | tf_op jit(solution)/shard_map/ppermute | solution.py:486
  60.1 6.7 %collective-permute-start.5 = (bf16[8,4,16,128]{3,2,1,0:T(8,128)(2,1)S(1)}, bf16[8,4,16,128]{3,2,1,0:T(8,128)(2,1)S(1)}, u32[]{:S(2)}, u32[]{:S(2)}) collective-permute-start(bf16[8,4,16,128]{3,2,1,0:T(8,128)(2,1)S(1)} %collective-permute-done.4.refs_7_), channel_id=1, source_target_pairs={{0,1},{1,2},{2,3},{3,4},{4,5},{5,6},{6,7},{7,0},{8,9},{9,10},{10,1... | collective-permute-start | bytes 393224 | tf_op jit(solution)/shard_map/ppermute | solution.py:486
  60.2 7.6 %collective-permute-start.12 = (bf16[8,4,16,128]{3,2,1,0:T(8,128)(2,1)S(1)}, bf16[8,4,16,128]{3,2,1,0:T(8,128)(2,1)S(1)}, u32[]{:S(2)}, u32[]{:S(2)}) collective-permute-start(bf16[8,4,16,128]{3,2,1,0:T(8,128)(2,1)S(1)} %collective-permute-done.11.refs_15_), channel_id=1, source_target_pairs={{0,1},{1,2},{2,3},{3,4},{4,5},{5,6},{6,7},{7,0},{8,9},{9,10},{10,1... | collective-permute-start | bytes 393224 | tf_op jit(solution)/shard_map/ppermute | solution.py:486
  60.3 7.6 %collective-permute-start.2 = (bf16[8,4,16,128]{3,2,1,0:T(8,128)(2,1)S(1)}, bf16[8,4,16,128]{3,2,1,0:T(8,128)(2,1)S(1)}, u32[]{:S(2)}, u32[]{:S(2)}) collective-permute-start(bf16[8,4,16,128]{3,2,1,0:T(8,128)(2,1)S(1)} %collective-permute-done.1.refs_2_), channel_id=1, source_target_pairs={{0,7},{1,0},{2,1},{3,2},{4,3},{5,4},{6,5},{7,6},{8,15},{9,8},{10,9... | collective-permute-start | bytes 393224 | tf_op jit(solution)/shard_map/ppermute | solution.py:486
  63.3 7.2 %collective-permute-start.9 = (bf16[8,4,16,128]{3,2,1,0:T(8,128)(2,1)S(1)}, bf16[8,4,16,128]{3,2,1,0:T(8,128)(2,1)S(1)}, u32[]{:S(2)}, u32[]{:S(2)}) collective-permute-start(bf16[8,4,16,128]{3,2,1,0:T(8,128)(2,1)S(1)} %collective-permute-done.8.refs_10_), channel_id=1, source_target_pairs={{0,7},{1,0},{2,1},{3,2},{4,3},{5,4},{6,5},{7,6},{8,15},{9,8},{10,9... | collective-permute-start | bytes 393224 | tf_op jit(solution)/shard_map/ppermute | solution.py:486
  66.9 6.7 %collective-permute-start.6 = (bf16[8,4,16,128]{3,2,1,0:T(8,128)(2,1)S(1)}, bf16[8,4,16,128]{3,2,1,0:T(8,128)(2,1)S(1)}, u32[]{:S(2)}, u32[]{:S(2)}) collective-permute-start(bf16[8,4,16,128]{3,2,1,0:T(8,128)(2,1)S(1)} %collective-permute-done.5.refs_6_), channel_id=1, source_target_pairs={{0,1},{1,2},{2,3},{3,4},{4,5},{5,6},{6,7},{7,0},{8,9},{9,10},{10,1... | collective-permute-start | bytes 393224 | tf_op jit(solution)/shard_map/ppermute | solution.py:486
  67.8 5.9 %collective-permute-start.13 = (bf16[8,4,16,128]{3,2,1,0:T(8,128)(2,1)S(1)}, bf16[8,4,16,128]{3,2,1,0:T(8,128)(2,1)S(1)}, u32[]{:S(2)}, u32[]{:S(2)}) collective-permute-start(bf16[8,4,16,128]{3,2,1,0:T(8,128)(2,1)S(1)} %collective-permute-done.12.refs_14_), channel_id=1, source_target_pairs={{0,1},{1,2},{2,3},{3,4},{4,5},{5,6},{6,7},{7,0},{8,9},{9,10},{10,1... | collective-permute-start | bytes 393224 | tf_op jit(solution)/shard_map/ppermute | solution.py:486
  67.9 5.9 %collective-permute-start.3 = (bf16[8,4,16,128]{3,2,1,0:T(8,128)(2,1)S(1)}, bf16[8,4,16,128]{3,2,1,0:T(8,128)(2,1)S(1)}, u32[]{:S(2)}, u32[]{:S(2)}) collective-permute-start(bf16[8,4,16,128]{3,2,1,0:T(8,128)(2,1)S(1)} %collective-permute-done.2.refs_3_), channel_id=1, source_target_pairs={{0,7},{1,0},{2,1},{3,2},{4,3},{5,4},{6,5},{7,6},{8,15},{9,8},{10,9... | collective-permute-start | bytes 393224 | tf_op jit(solution)/shard_map/ppermute | solution.py:486
  70.5 5.5 %collective-permute-start.10 = (bf16[8,4,16,128]{3,2,1,0:T(8,128)(2,1)S(1)}, bf16[8,4,16,128]{3,2,1,0:T(8,128)(2,1)}, u32[]{:S(2)}, u32[]{:S(2)}) collective-permute-start(bf16[8,4,16,128]{3,2,1,0:T(8,128)(2,1)S(1)} %collective-permute-done.9.refs_11_), channel_id=1, source_target_pairs={{0,7},{1,0},{2,1},{3,2},{4,3},{5,4},{6,5},{7,6},{8,15},{9,8},{10,9... | collective-permute-start | bytes 393224 | tf_op jit(solution)/shard_map/ppermute | solution.py:486
  104.3 15.8 %collective-permute-start.14 = (bf16[8,4,16,128]{3,2,1,0:T(8,128)(2,1)}, bf16[8,4,16,128]{3,2,1,0:T(8,128)(2,1)S(1)}, u32[]{:S(2)}, u32[]{:S(2)}) collective-permute-start(bf16[8,4,16,128]{3,2,1,0:T(8,128)(2,1)} %get-tuple-element.37), channel_id=1, source_target_pairs={{0,7},{1,0},{2,1},{3,2},{4,3},{5,4},{6,5},{7,6},{8,15},{9,8},{10,9... | collective-permute-start | bytes 393224 | tf_op jit(solution)/shard_map/ppermute | solution.py:486
  110.1 34.4 %all-to-all-start.2 = ((bf16[32,2,16,1024]{3,2,1,0:T(8,128)(2,1)}), bf16[32,2,16,1024]{3,2,1,0:T(8,128)(2,1)S(1)}, u32[]{:S(2)}, u32[]{:S(2)}) async-start(bf16[32,2,16,1024]{3,2,1,0:T(8,128)(2,1)} %bitcast.18), calls=%async_computation.2 | async-start | bytes 4194304 | tf_op jit(solution)/shard_map/all_to_all | solution.py:517
  117.4 6.2 %collective-permute-start.18 = (bf16[8,4,16,128]{3,2,1,0:T(8,128)(2,1)S(1)}, bf16[8,4,16,128]{3,2,1,0:T(8,128)(2,1)S(1)}, u32[]{:S(2)}, u32[]{:S(2)}) collective-permute-start(bf16[8,4,16,128]{3,2,1,0:T(8,128)(2,1)S(1)} %copy-done.35), channel_id=1, source_target_pairs={{0,1},{1,2},{2,3},{3,4},{4,5},{5,6},{6,7},{7,0},{8,9},{9,10},{10,1... | collective-permute-start | bytes 393224 | tf_op jit(solution)/shard_map/ppermute | solution.py:486
  117.5 6.2 %collective-permute-start.21 = (bf16[8,4,16,128]{3,2,1,0:T(8,128)(2,1)S(1)}, bf16[8,4,16,128]{3,2,1,0:T(8,128)(2,1)S(1)}, u32[]{:S(2)}, u32[]{:S(2)}) collective-permute-start(bf16[8,4,16,128]{3,2,1,0:T(8,128)(2,1)S(1)} %copy-done.34), channel_id=1, source_target_pairs={{0,7},{1,0},{2,1},{3,2},{4,3},{5,4},{6,5},{7,6},{8,15},{9,8},{10,9... | collective-permute-start | bytes 393224 | tf_op jit(solution)/shard_map/ppermute | solution.py:486
  120.1 6.3 %collective-permute-start.25 = (bf16[8,4,16,128]{3,2,1,0:T(8,128)(2,1)S(1)}, bf16[8,4,16,128]{3,2,1,0:T(8,128)(2,1)S(1)}, u32[]{:S(2)}, u32[]{:S(2)}) collective-permute-start(bf16[8,4,16,128]{3,2,1,0:T(8,128)(2,1)S(1)} %copy-done.33), channel_id=1, source_target_pairs={{0,1},{1,2},{2,3},{3,4},{4,5},{5,6},{6,7},{7,0},{8,9},{9,10},{10,1... | collective-permute-start | bytes 393224 | tf_op jit(solution)/shard_map/ppermute | solution.py:486
  120.2 6.4 %collective-permute-start.15 = (bf16[8,4,16,128]{3,2,1,0:T(8,128)(2,1)S(1)}, bf16[8,4,16,128]{3,2,1,0:T(8,128)(2,1)S(1)}, u32[]{:S(2)}, u32[]{:S(2)}) collective-permute-start(bf16[8,4,16,128]{3,2,1,0:T(8,128)(2,1)S(1)} %add_convert_fusion.9), channel_id=1, source_target_pairs={{0,7},{1,0},{2,1},{3,2},{4,3},{5,4},{6,5},{7,6},{8,15},{9,8},{10,9... | collective-permute-start | bytes 393224 | tf_op jit(solution)/shard_map/ppermute | solution.py:486
  123.6 5.8 %collective-permute-start.19 = (bf16[8,4,16,128]{3,2,1,0:T(8,128)(2,1)S(1)}, bf16[8,4,16,128]{3,2,1,0:T(8,128)(2,1)S(1)}, u32[]{:S(2)}, u32[]{:S(2)}) collective-permute-start(bf16[8,4,16,128]{3,2,1,0:T(8,128)(2,1)S(1)} %add_convert_fusion.6), channel_id=1, source_target_pairs={{0,1},{1,2},{2,3},{3,4},{4,5},{5,6},{6,7},{7,0},{8,9},{9,10},{10,1... | collective-permute-start | bytes 393224 | tf_op jit(solution)/shard_map/ppermute | solution.py:486
  123.7 5.8 %collective-permute-start.22 = (bf16[8,4,16,128]{3,2,1,0:T(8,128)(2,1)S(1)}, bf16[8,4,16,128]{3,2,1,0:T(8,128)(2,1)S(1)}, u32[]{:S(2)}, u32[]{:S(2)}) collective-permute-start(bf16[8,4,16,128]{3,2,1,0:T(8,128)(2,1)S(1)} %add_convert_fusion.4), channel_id=1, source_target_pairs={{0,7},{1,0},{2,1},{3,2},{4,3},{5,4},{6,5},{7,6},{8,15},{9,8},{10,9... | collective-permute-start | bytes 393224 | tf_op jit(solution)/shard_map/ppermute | solution.py:486
  126.5 6.0 %collective-permute-start.26 = (bf16[8,4,16,128]{3,2,1,0:T(8,128)(2,1)S(1)}, bf16[8,4,16,128]{3,2,1,0:T(8,128)(2,1)S(1)}, u32[]{:S(2)}, u32[]{:S(2)}) collective-permute-start(bf16[8,4,16,128]{3,2,1,0:T(8,128)(2,1)S(1)} %add_convert_fusion.1), channel_id=1, source_target_pairs={{0,1},{1,2},{2,3},{3,4},{4,5},{5,6},{6,7},{7,0},{8,9},{9,10},{10,1... | collective-permute-start | bytes 393224 | tf_op jit(solution)/shard_map/ppermute | solution.py:486
  126.7 6.0 %collective-permute-start.16 = (bf16[8,4,16,128]{3,2,1,0:T(8,128)(2,1)S(1)}, bf16[8,4,16,128]{3,2,1,0:T(8,128)(2,1)S(1)}, u32[]{:S(2)}, u32[]{:S(2)}) collective-permute-start(bf16[8,4,16,128]{3,2,1,0:T(8,128)(2,1)S(1)} %add_convert_fusion.8), channel_id=1, source_target_pairs={{0,7},{1,0},{2,1},{3,2},{4,3},{5,4},{6,5},{7,6},{8,15},{9,8},{10,9... | collective-permute-start | bytes 393224 | tf_op jit(solution)/shard_map/ppermute | solution.py:486
  129.4 9.2 %collective-permute-start.20 = (bf16[8,4,16,128]{3,2,1,0:T(8,128)(2,1)S(1)}, bf16[8,4,16,128]{3,2,1,0:T(8,128)(2,1)S(1)}, u32[]{:S(2)}, u32[]{:S(2)}) collective-permute-start(bf16[8,4,16,128]{3,2,1,0:T(8,128)(2,1)S(1)} %add_convert_fusion.5), channel_id=1, source_target_pairs={{0,1},{1,2},{2,3},{3,4},{4,5},{5,6},{6,7},{7,0},{8,9},{9,10},{10,1... | collective-permute-start | bytes 393224 | tf_op jit(solution)/shard_map/ppermute | solution.py:486
  129.6 5.9 %collective-permute-start.23 = (bf16[8,4,16,128]{3,2,1,0:T(8,128)(2,1)S(1)}, bf16[8,4,16,128]{3,2,1,0:T(8,128)(2,1)S(1)}, u32[]{:S(2)}, u32[]{:S(2)}) collective-permute-start(bf16[8,4,16,128]{3,2,1,0:T(8,128)(2,1)S(1)} %add_convert_fusion.3), channel_id=1, source_target_pairs={{0,7},{1,0},{2,1},{3,2},{4,3},{5,4},{6,5},{7,6},{8,15},{9,8},{10,9... | collective-permute-start | bytes 393224 | tf_op jit(solution)/shard_map/ppermute | solution.py:486
  132.6 6.3 %collective-permute-start.27 = (bf16[8,4,16,128]{3,2,1,0:T(8,128)(2,1)S(1)}, bf16[8,4,16,128]{3,2,1,0:T(8,128)(2,1)S(1)}, u32[]{:S(2)}, u32[]{:S(2)}) collective-permute-start(bf16[8,4,16,128]{3,2,1,0:T(8,128)(2,1)S(1)} %add_convert_fusion), channel_id=1, source_target_pairs={{0,1},{1,2},{2,3},{3,4},{4,5},{5,6},{6,7},{7,0},{8,9},{9,10},{10,1... | collective-permute-start | bytes 393224 | tf_op jit(solution)/shard_map/ppermute | solution.py:486
  132.8 6.2 %collective-permute-start.17 = (bf16[8,4,16,128]{3,2,1,0:T(8,128)(2,1)S(1)}, bf16[8,4,16,128]{3,2,1,0:T(8,128)(2,1)S(1)}, u32[]{:S(2)}, u32[]{:S(2)}) collective-permute-start(bf16[8,4,16,128]{3,2,1,0:T(8,128)(2,1)S(1)} %add_convert_fusion.7), channel_id=1, source_target_pairs={{0,7},{1,0},{2,1},{3,2},{4,3},{5,4},{6,5},{7,6},{8,15},{9,8},{10,9... | collective-permute-start | bytes 393224 | tf_op jit(solution)/shard_map/ppermute | solution.py:486
  135.5 6.2 %collective-permute-start.24 = (bf16[8,4,16,128]{3,2,1,0:T(8,128)(2,1)S(1)}, bf16[8,4,16,128]{3,2,1,0:T(8,128)(2,1)S(1)}, u32[]{:S(2)}, u32[]{:S(2)}) collective-permute-start(bf16[8,4,16,128]{3,2,1,0:T(8,128)(2,1)S(1)} %add_convert_fusion.2), channel_id=1, source_target_pairs={{0,7},{1,0},{2,1},{3,2},{4,3},{5,4},{6,5},{7,6},{8,15},{9,8},{10,9... | collective-permute-start | bytes 393224 | tf_op jit(solution)/shard_map/ppermute | solution.py:486
  144.5 21.7 %all-to-all-start.3 = ((bf16[32,2,16,256]{3,2,1,0:T(8,128)(2,1)}), bf16[32,2,16,256]{3,2,1,0:T(8,128)(2,1)S(1)}, u32[]{:S(2)}, u32[]{:S(2)}) async-start(bf16[32,2,16,256]{3,2,1,0:T(8,128)(2,1)} %bitcast.17), calls=%async_computation.3 | async-start | bytes 1048576 | tf_op jit(solution)/shard_map/all_to_all | solution.py:517
  (36 other events, 373.1 us)

commit v3 on v2

--- a/solution.py
+++ b/solution.py
@@ -1,3 +1,4 @@
+import functools
 import math
 
 import jax
@@ -144,49 +145,48 @@
     )(dest, q, g)
 
 
-def pick_body(t, x, k, v, stage, get, put):
-    run([pltpu.make_async_copy(x.at[t[0, s], :, t[1, s], :, pl.ds(n * HEAD, HEAD)],
-                               stage.at[n, s], get.at[n, s])
-         for s in range(SLOTS) for n in range(2)])
-    run([pltpu.make_async_copy(stage.at[n], out, put.at[n]) for n, out in enumerate((k, v))])
-
-
-def pick_pair(table, x):
+def pick_body(t, x, k, v, soon, pair_stage, soon_stage, sem):
+    for s in range(SLOTS):
+        for y in range(N_Y):
+            rows = x[t[0, s], y, t[1, s]]
+            pair_stage[0, s, y] = rows[:, :HEAD]
+            pair_stage[1, s, y] = rows[:, HEAD:2 * HEAD]
+            soon_stage[s, y] = rows[:, 2 * HEAD:]
+    run([pltpu.make_async_copy(pair_stage.at[0], k, sem.at[0]),
+         pltpu.make_async_copy(pair_stage.at[1], v, sem.at[1]),
+         pltpu.make_async_copy(soon_stage, soon, sem.at[2])])
+
+
+def pick_first(table, x):
     out = jax.ShapeDtypeStruct(CHUNK, BF16)
+    late = (SLOTS, N_Y, BR, 2 * SOON)
     return pl.pallas_call(
         pick_body,
-        in_specs=[whole(pltpu.SMEM), whole(pl.ANY)],
-        out_specs=[whole(pltpu.HBM), whole(pltpu.HBM)],
-        out_shape=[out, out],
+        in_specs=[whole(pltpu.SMEM), whole(pltpu.VMEM)],
+        out_specs=[whole(pltpu.HBM)] * 3,
+        out_shape=[out, out, jax.ShapeDtypeStruct(late, BF16)],
         scratch_shapes=[
             pltpu.VMEM((2,) + CHUNK, BF16),
-            pltpu.SemaphoreType.DMA((2, SLOTS)),
-            pltpu.SemaphoreType.DMA((2,)),
+            pltpu.VMEM(late, BF16),
+            pltpu.SemaphoreType.DMA((3,)),
         ],
-        name="pick_pair",
+        name="pick_first",
     )(table, x)
 
 
-def place_body(t, ka, kb, kc, va, vb, vc, out, stage, sem):
-    copies = []
+def place_body(t, ka, kb, kc, va, vb, vc, out):
     for s in range(SLOTS):
         for n, (a, b, c) in enumerate(((ka, kb, kc), (va, vb, vc))):
             total = a[s].astype(F32) + b[s].astype(F32) + c[s].astype(F32)
-            stage[s, :, :, n * HEAD:(n + 1) * HEAD] = total.astype(BF16)
-        copies.append(pltpu.make_async_copy(stage.at[s], out.at[t[0, s], :, t[1, s]], sem.at[s]))
-    run(copies)
+            out[t[0, s], :, t[1, s], :, n * HEAD:(n + 1) * HEAD] = total.astype(BF16)
 
 
 def place_pair(table, dk, dv):
     return pl.pallas_call(
         place_body,
         in_specs=[whole(pltpu.SMEM)] + [whole(pltpu.VMEM)] * 6,
-        out_specs=whole(pl.ANY),
+        out_specs=whole(pltpu.VMEM),
         out_shape=jax.ShapeDtypeStruct((N_DP, N_Y, CAP, BR, 2 * HEAD), BF16),
-        scratch_shapes=[
-            pltpu.VMEM((SLOTS, N_Y, BR, 2 * HEAD), BF16),
-            pltpu.SemaphoreType.DMA((SLOTS,)),
-        ],
         name="place_pair",
     )(table, *dk, *dv)
 
@@ -213,30 +213,23 @@
     )(dest, x)
 
 
-def home_pair_body(dest, x, k, v, stage, sem):
-    copies = []
+def home_pair_body(dest, x, k, v):
     for j, (group, rank) in enumerate(route(dest)):
-        copies.append(pltpu.make_async_copy(x.at[group, :, rank], stage.at[j], sem.at[j]))
-    run(copies)
-    for j in range(SLOTS):
         rows = slice(j * BR, (j + 1) * BR)
         for h in range(KEY_HEADS):
             cols = slice(h * HEAD, (h + 1) * HEAD)
-            k[rows, cols] = stage[j, h, :, :HEAD]
-            v[rows, cols] = stage[j, h, :, HEAD:]
+            part = x[group, h, rank]
+            k[rows, cols] = part[:, :HEAD]
+            v[rows, cols] = part[:, HEAD:]
 
 
 def home_pair(dest, x):
     out = jax.ShapeDtypeStruct((SLOTS * BR, KEY_HEADS * HEAD), BF16)
     return pl.pallas_call(
         home_pair_body,
-        in_specs=[whole(pltpu.SMEM), whole(pl.ANY)],
+        in_specs=[whole(pltpu.SMEM), whole(pltpu.VMEM)],
         out_specs=[whole(pltpu.VMEM), whole(pltpu.VMEM)],
         out_shape=[out, out],
-        scratch_shapes=[
-            pltpu.VMEM((SLOTS, KEY_HEADS, BR, 2 * HEAD), BF16),
-            pltpu.SemaphoreType.DMA((SLOTS,)),
-        ],
         name="home_pair",
     )(dest, x)
 
@@ -269,8 +262,7 @@
     def qg_copies(s):
         return (
             pltpu.make_async_copy(
-                soon_hbm.at[t[0, s], :, t[1, s], :, pl.ds(2 * HEAD, 2 * SOON)], soon_buf.at[s],
-                qg_in.at[0, s]),
+                soon_hbm.at[s], soon_buf.at[s], qg_in.at[0, s]),
             pltpu.make_async_copy(
                 rest_hbm.at[t[0, s], :, t[1, s]], rest_buf.at[s], qg_in.at[1, s]))
 
@@ -319,6 +311,88 @@
         acc_k[o] = jnp.zeros((BLOCK, HEAD), F32)
         acc_v[o] = jnp.zeros((BLOCK, HEAD), F32)
         return o
+
+    def work(s, first, count):
+        low, high = halves
+        full = slice(0, BLOCK)
+        blocks = [(first + i, i) for i in range(count)]
+
+        def score_tile(o, at, keys, rows, masked):
+            top = None
+            for k0 in range(keys.start, keys.stop, TILE):
+                part = slice(k0, k0 + TILE)
+                x = dot_nt(ks[o, part], qm[rows])
+                if masked:
+                    x = x + bias[k0 - keys.start:k0 - keys.start + TILE]
+                sc[at, part, rows] = x
+                x = fold_max(x)
+                top = x if top is None else jnp.maximum(top, x)
+            return top
+
+        tops = [score_tile(s, own, low, low, True),
+                jnp.maximum(score_tile(s, own, low, high, False),
+                            score_tile(s, own, high, high, True))]
+        for o, i in blocks:
+            tops = [jnp.maximum(top, score_tile(o, i, full, rows, False))
+                    for top, rows in zip(tops, halves)]
+        tops = [jnp.max(top, axis=0, keepdims=True) for top in tops]
+
+        def exp_tile(o, at, keys, rows, top):
+            total = moment = None
+            for k0 in range(keys.start, keys.stop, TILE):
+                part = slice(k0, k0 + TILE)
+                d = dot_nt(vs[o, part], gm[rows])
+                e = jnp.exp2((sc[at, part, rows] - top) * EXP_SCALE)
+                sc[at, part, rows] = e
+                dp[at, part, rows] = d
+                a, b = fold_sum(e), fold_sum(e * d)
+                total = a if total is None else total + a
+                moment = b if moment is None else moment + b
+            return total, moment
+
+        def add(x, y):
+            return tuple(a + b for a, b in zip(x, y))
+
+        sums = [exp_tile(s, own, low, low, tops[0]),
+                add(exp_tile(s, own, low, high, tops[1]), exp_tile(s, own, high, high, tops[1]))]
+        for o, i in blocks:
+            sums = [add(old, exp_tile(o, i, full, rows, top))
+                    for old, rows, top in zip(sums, halves, tops)]
+        inverse, delta = [], []
+        for total, moment in sums:
+            inverse.append(1.0 / jnp.sum(total, axis=0, keepdims=True))
+            delta.append(jnp.sum(moment, axis=0, keepdims=True) * inverse[-1])
+        inverse = jnp.concatenate(inverse, axis=1)
+        delta = jnp.concatenate(delta, axis=1)
+
+        def grad_tile(o, at, keys, rows, fresh):
+            for k0 in range(keys.start, keys.stop, TILE):
+                part = slice(k0, k0 + TILE)
+                p = sc[at, part, rows] * inverse[:, rows]
+                w = p.astype(BF16)
+                ds = (p * (dp[at, part, rows] - delta[:, rows])).astype(BF16)
+                acc_v[o, part] += dot_nn(w, gm[rows])
+                acc_k[o, part] += dot_nn(ds, qm[rows])
+                term = dot_nn(kt[o, :, part], ds)
+                if fresh and k0 == keys.start:
+                    dqt[:, rows] = term
+                else:
+                    dqt[:, rows] += term
+
+        grad_tile(s, own, low, full, True)
+        grad_tile(s, own, high, high, False)
+        for y in range(N_Y):
+            for r in range(N_Z):
+                rows = pl.ds(y * HEAD + spots[r], BR)
+                dkv_buf[r, s, y] = (acc_k[s, rows] * SCALE).astype(BF16)
+                dkv_buf[N_Z + r, s, y] = acc_v[s, rows].astype(BF16)
+        for o, i in blocks:
+            grad_tile(o, i, full, full, False)
+        dq = (dqt[...] * SCALE).T.astype(BF16)
+        for y in range(N_Y):
+            for h in range(PER_KEY):
+                at = y * HEAD + h * BR
+                dq_buf[s, y, :, h * HEAD:(h + 1) * HEAD] = dq[at:at + BR]
 
     def step(n, ready):
         s = SLOTS - 1 - n
@@ -334,97 +408,9 @@
                 at = h * HEAD if late else h * HEAD - LATER
                 qm[rows, :] = buf[s, y, :, at:at + HEAD]
                 gm[rows, :] = buf[s, y, :, span + at:span + at + HEAD]
-        count = s - first
-
-        def score_tile(o, at, keys, rows, masked):
-            top = None
-            for k0 in range(keys.start, keys.stop, TILE):
-                part = slice(k0, k0 + TILE)
-                x = dot_nt(ks[o, part], qm[rows])
-                if masked:
-                    x = x + bias[k0 - keys.start:k0 - keys.start + TILE]
-                sc[at, part, rows] = x
-                x = fold_max(x)
-                top = x if top is None else jnp.maximum(top, x)
-            return top
-
-        low, high = halves
-        tops = (score_tile(s, own, low, low, True),
-                jnp.maximum(score_tile(s, own, low, high, False),
-                            score_tile(s, own, high, high, True)))
-
-        def score_step(i, tops):
-            full = slice(0, BLOCK)
-            return tuple(jnp.maximum(top, score_tile(first + i, i, full, rows, False))
-                         for top, rows in zip(tops, halves))
-
-        tops = lax.fori_loop(0, count, score_step, tops)
-        tops = [jnp.max(top, axis=0, keepdims=True) for top in tops]
-
-        def exp_tile(o, at, keys, rows, top):
-            total = moment = None
-            for k0 in range(keys.start, keys.stop, TILE):
-                part = slice(k0, k0 + TILE)
-                d = dot_nt(vs[o, part], gm[rows])
-                e = jnp.exp2((sc[at, part, rows] - top) * EXP_SCALE)
-                sc[at, part, rows] = e
-                dp[at, part, rows] = d
-                a, b = fold_sum(e), fold_sum(e * d)
-                total = a if total is None else total + a
-                moment = b if moment is None else moment + b
-            return total, moment
-
-        def add(x, y):
-            return tuple(a + b for a, b in zip(x, y))
-
-        sums = (exp_tile(s, own, low, low, tops[0]),
-                add(exp_tile(s, own, low, high, tops[1]), exp_tile(s, own, high, high, tops[1])))
-
-        def exp_step(i, sums):
-            full = slice(0, BLOCK)
-            return tuple(add(old, exp_tile(first + i, i, full, rows, top))
-                         for old, rows, top in zip(sums, halves, tops))
-
-        sums = lax.fori_loop(0, count, exp_step, sums)
-        inverse, delta = [], []
-        for total, moment in sums:
-            inverse.append(1.0 / jnp.sum(total, axis=0, keepdims=True))
-            delta.append(jnp.sum(moment, axis=0, keepdims=True) * inverse[-1])
-        inverse = jnp.concatenate(inverse, axis=1)
-        delta = jnp.concatenate(delta, axis=1)
-
-        def grad_tile(o, at, keys, rows, fresh):
-            for k0 in range(keys.start, keys.stop, TILE):
-                part = slice(k0, k0 + TILE)
-                p = sc[at, part, rows] * inverse[:, rows]
-                w = p.astype(BF16)
-                ds = (p * (dp[at, part, rows] - delta[:, rows])).astype(BF16)
-                acc_v[o, part] += dot_nn(w, gm[rows])
-                acc_k[o, part] += dot_nn(ds, qm[rows])
-                term = dot_nn(kt[o, :, part], ds)
-                if fresh and k0 == keys.start:
-                    dqt[:, rows] = term
-                else:
-                    dqt[:, rows] += term
-
-        grad_tile(s, own, low, slice(0, BLOCK), True)
-        grad_tile(s, own, high, high, False)
-
-        def grad_step(i, carry):
-            grad_tile(first + i, i, slice(0, BLOCK), slice(0, BLOCK), False)
-            return carry
-
-        lax.fori_loop(0, count, grad_step, 0)
-
-        dq = (dqt[...] * SCALE).T.astype(BF16)
-        for y in range(N_Y):
-            for h in range(PER_KEY):
-                at = y * HEAD + h * BR
-                dq_buf[s, y, :, h * HEAD:(h + 1) * HEAD] = dq[at:at + BR]
-            for r in range(N_Z):
-                rows = pl.ds(y * HEAD + spots[r], BR)
-                dkv_buf[r, s, y] = (acc_k[s, rows] * SCALE).astype(BF16)
-                dkv_buf[N_Z + r, s, y] = acc_v[s, rows].astype(BF16)
+        for count in range(SPAN):
+            pl.when(s - first == count)(functools.partial(work, s, first, count))
+
         dq_copy(s).start()
 
         @pl.when(s == SPAN)
@@ -524,8 +510,8 @@
     arrived = swap(packed)
     rest = pack_rest(late, queries, output_gradient)
     table = tables(doc_lengths, late, dest_slot)
-    k, v = pick_pair(table, arrived)
-    dq, dk, dv = attend(table, arrived, swap(rest), spread(k) + spread(v))
+    k, v, soon = pick_first(table, arrived)
+    dq, dk, dv = attend(table, soon, swap(rest), spread(k) + spread(v))
     dq, pair = lax.optimization_barrier((swap(dq), place_pair(table, collect(dk), collect(dv))))
     grad_q = home_wide(dest_group, dq)
     key_gradient, value_gradient = home_pair(dest_group, swap(pair))

time: 170 us -> 166 us (0.976)
  Pallas kernels: 40.9 us -> 36.4 us
    pallas_call x1, Pallas kernels: 24.4 us -> 20.6 us  [attend(): pl.pallas_call(attend_body, in_specs=[whole(pltpu.SMEM), whole(pl.ANY), w...]
  transfers between devices with their start and end apart: 32 -> 32, of which waited for: 12 -> 12; matrix products, arithmetic and copies ran while one was open for 1% -> 1% of each run, Pallas kernels for 6% -> 7%
where the time goes in v3:
time: 166 us; the launch traced here: 165 us
  starting transfers between devices  83.3 us (50%)
  waiting for transfers between devices  37.6 us (23%)
  Pallas kernels  36.4 us (22%)
  local copies, waits for them, and re-layouts  4.31 us (3%)
  other arithmetic  2.01 us (1%)
    ppermute x28, starting transfers between devices, hop(): return lax.ppermute(x, 'z', [(i, (i + step) % N_Z) for i in range(N_Z)])  51 us
    all_to_all x4, starting transfers between devices, swap(): return lax.all_to_all(flat, ('dp', 'y'), 0, 0, tiled=True).reshape(x.shape)  32.3 us
    all_to_all x4, waiting for transfers between devices, swap(): return lax.all_to_all(flat, ('dp', 'y'), 0, 0, tiled=True).reshape(x.shape)  30.1 us
    pallas_call x1, Pallas kernels, attend(): pl.pallas_call(attend_body, in_specs=[whole(pltpu.SMEM), whole(pl.ANY), w...  20.6 us
    ppermute x28, waiting for transfers between devices, hop(): return lax.ppermute(x, 'z', [(i, (i + step) % N_Z) for i in range(N_Z)])  7.55 us
    unnamed x72, local copies, waits for them, and re-layouts  4.08 us
  transfers between devices with their start and end apart: 32, of which 12 were waited for; matrix products, arithmetic and copies ran while one was open for 1% of the time, Pallas kernels for 7%

profile of v3, /device:TPU:1, one launch (start us, length us, event | category | flops | bytes accessed | tf_op | source)
XLA Modules:
  0.0 164.8 jit_solution(15174597836993271238)
XLA Ops:
  0.6 3.1 %pack_first.1 = bf16[8,4,2,16,768]{4,3,2,1,0:T(8,128)(2,1)} custom-call(s32[64]{0:T(128)} %dest.6, bf16[128,512]{1,0:T(8,128)(2,1)} %k.1, bf16[128,512]{1,0:T(8,128)(2,1)} %v.1, bf16[128,4096]{1,0:T(8,128)(2,1)} %q.3, bf16[128,4096]{1,0:T(8,128)(2,1)} %g.3), custom_call_target="tpu_custom_call" | custom-call | tf_op jit(solution)/shard_map/pack_first/pallas_call | solution.py:109
  3.8 8.6 %all-to-all-start = ((bf16[32,2,16,768]{3,2,1,0:T(8,128)(2,1)}), bf16[32,2,16,768]{3,2,1,0:T(8,128)(2,1)S(1)}, u32[]{:S(2)}, u32[]{:S(2)}) async-start(bf16[32,2,16,768]{3,2,1,0:T(8,128)(2,1)} %bitcast.15), calls=%async_computation | async-start | bytes 3145728 | tf_op jit(solution)/shard_map/all_to_all | solution.py:503
  12.4 3.3 %pack_rest.1 = bf16[8,4,2,16,1536]{4,3,2,1,0:T(8,128)(2,1)} custom-call(s32[64]{0:T(128)} %dest.6, bf16[128,4096]{1,0:T(8,128)(2,1)} %q.3, bf16[128,4096]{1,0:T(8,128)(2,1)} %g.3), custom_call_target="tpu_custom_call" | custom-call | tf_op jit(solution)/shard_map/pack_rest/pallas_call | solution.py:138
  15.7 18.2 %all-to-all-done = bf16[32,2,16,768]{3,2,1,0:T(8,128)(2,1)S(1)} async-done(((bf16[32,2,16,768]{3,2,1,0:T(8,128)(2,1)}), bf16[32,2,16,768]{3,2,1,0:T(8,128)(2,1)S(1)}, u32[]{:S(2)}, u32[]{:S(2)}) %all-to-all-start) | async-done | bytes 1572896 | tf_op jit(solution)/shard_map/all_to_all | solution.py:503
  33.9 1.2 copy-done.1
  35.1 5.9 %all-to-all-start.1 = ((bf16[32,2,16,1536]{3,2,1,0:T(8,128)(2,1)}), bf16[32,2,16,1536]{3,2,1,0:T(8,128)(2,1)}, u32[]{:S(2)}, u32[]{:S(2)}) async-start(bf16[32,2,16,1536]{3,2,1,0:T(8,128)(2,1)} %bitcast.12), calls=%async_computation.1 | async-start | bytes 6291456 | tf_op jit(solution)/shard_map/all_to_all | solution.py:503
  42.9 2.4 %pick_first.1 = (bf16[8,4,16,128]{3,2,1,0:T(8,128)(2,1)}, bf16[8,4,16,128]{3,2,1,0:T(8,128)(2,1)}, bf16[8,4,16,512]{3,2,1,0:T(8,128)(2,1)}) custom-call(s32[4,8]{1,0:T(4,128)} %add_add_fusion.t, bf16[8,4,2,16,768]{4,3,2,1,0:T(8,128)(2,1)} %bitcast.14), custom_call_target="tpu_custom_call" | custom-call | tf_op jit(solution)/shard_map/pick_first/pallas_call | solution.py:163
  45.3 5.7 %collective-permute-start = (bf16[8,4,16,128]{3,2,1,0:T(8,128)(2,1)}, bf16[8,4,16,128]{3,2,1,0:T(8,128)(2,1)S(1)}, u32[]{:S(2)}, u32[]{:S(2)}) collective-permute-start(bf16[8,4,16,128]{3,2,1,0:T(8,128)(2,1)} %get-tuple-element.36.refs_0_), channel_id=1, source_target_pairs={{0,7},{1,0},{2,1},{3,2},{4,3},{5,4},{6,5},{7,6},{8,15},{9,8},{10,9... | collective-permute-start | bytes 393224 | tf_op jit(solution)/shard_map/ppermute | solution.py:472
  52.5 1.3 collective-permute-done.refs_1_
  53.8 3.4 %collective-permute-start.1 = (bf16[8,4,16,128]{3,2,1,0:T(8,128)(2,1)S(1)}, bf16[8,4,16,128]{3,2,1,0:T(8,128)(2,1)S(1)}, u32[]{:S(2)}, u32[]{:S(2)}) collective-permute-start(bf16[8,4,16,128]{3,2,1,0:T(8,128)(2,1)S(1)} %collective-permute-done.refs_1_), channel_id=1, source_target_pairs={{0,7},{1,0},{2,1},{3,2},{4,3},{5,4},{6,5},{7,6},{8,15},{9,8},{10,9... | collective-permute-start | bytes 393224 | tf_op jit(solution)/shard_map/ppermute | solution.py:472
  57.2 2.8 %collective-permute-start.8 = (bf16[8,4,16,128]{3,2,1,0:T(8,128)(2,1)S(1)}, bf16[8,4,16,128]{3,2,1,0:T(8,128)(2,1)S(1)}, u32[]{:S(2)}, u32[]{:S(2)}) collective-permute-start(bf16[8,4,16,128]{3,2,1,0:T(8,128)(2,1)S(1)} %collective-permute-done.7.refs_9_), channel_id=1, source_target_pairs={{0,7},{1,0},{2,1},{3,2},{4,3},{5,4},{6,5},{7,6},{8,15},{9,8},{10,9... | collective-permute-start | bytes 393224 | tf_op jit(solution)/shard_map/ppermute | solution.py:472
  60.1 2.6 %collective-permute-start.2 = (bf16[8,4,16,128]{3,2,1,0:T(8,128)(2,1)S(1)}, bf16[8,4,16,128]{3,2,1,0:T(8,128)(2,1)S(1)}, u32[]{:S(2)}, u32[]{:S(2)}) collective-permute-start(bf16[8,4,16,128]{3,2,1,0:T(8,128)(2,1)S(1)} %collective-permute-done.1.refs_2_), channel_id=1, source_target_pairs={{0,7},{1,0},{2,1},{3,2},{4,3},{5,4},{6,5},{7,6},{8,15},{9,8},{10,9... | collective-permute-start | bytes 393224 | tf_op jit(solution)/shard_map/ppermute | solution.py:472
  63.2 3.5 %collective-permute-start.9 = (bf16[8,4,16,128]{3,2,1,0:T(8,128)(2,1)S(1)}, bf16[8,4,16,128]{3,2,1,0:T(8,128)(2,1)S(1)}, u32[]{:S(2)}, u32[]{:S(2)}) collective-permute-start(bf16[8,4,16,128]{3,2,1,0:T(8,128)(2,1)S(1)} %collective-permute-done.8.refs_10_), channel_id=1, source_target_pairs={{0,7},{1,0},{2,1},{3,2},{4,3},{5,4},{6,5},{7,6},{8,15},{9,8},{10,9... | collective-permute-start | bytes 393224 | tf_op jit(solution)/shard_map/ppermute | solution.py:472
  67.7 2.7 %collective-permute-start.3 = (bf16[8,4,16,128]{3,2,1,0:T(8,128)(2,1)S(1)}, bf16[8,4,16,128]{3,2,1,0:T(8,128)(2,1)S(1)}, u32[]{:S(2)}, u32[]{:S(2)}) collective-permute-start(bf16[8,4,16,128]{3,2,1,0:T(8,128)(2,1)S(1)} %collective-permute-done.2.refs_3_), channel_id=1, source_target_pairs={{0,7},{1,0},{2,1},{3,2},{4,3},{5,4},{6,5},{7,6},{8,15},{9,8},{10,9... | collective-permute-start | bytes 393224 | tf_op jit(solution)/shard_map/ppermute | solution.py:472
  70.4 3.0 %collective-permute-start.10 = (bf16[8,4,16,128]{3,2,1,0:T(8,128)(2,1)S(1)}, bf16[8,4,16,128]{3,2,1,0:T(8,128)(2,1)}, u32[]{:S(2)}, u32[]{:S(2)}) collective-permute-start(bf16[8,4,16,128]{3,2,1,0:T(8,128)(2,1)S(1)} %collective-permute-done.9.refs_11_), channel_id=1, source_target_pairs={{0,7},{1,0},{2,1},{3,2},{4,3},{5,4},{6,5},{7,6},{8,15},{9,8},{10,9... | collective-permute-start | bytes 393224 | tf_op jit(solution)/shard_map/ppermute | solution.py:472
  75.9 4.0 %all-to-all-done.1 = bf16[32,2,16,1536]{3,2,1,0:T(8,128)(2,1)} async-done(((bf16[32,2,16,1536]{3,2,1,0:T(8,128)(2,1)}), bf16[32,2,16,1536]{3,2,1,0:T(8,128)(2,1)}, u32[]{:S(2)}, u32[]{:S(2)}) %all-to-all-start.1) | async-done | bytes 3145760 | tf_op jit(solution)/shard_map/all_to_all | solution.py:503
  79.9 20.6 %attend.1 = (bf16[8,4,2,16,1024]{4,3,2,1,0:T(8,128)(2,1)}, bf16[8,4,16,128]{3,2,1,0:T(8,128)(2,1)}, bf16[8,4,16,128]{3,2,1,0:T(8,128)(2,1)}, bf16[8,4,16,128]{3,...) custom-call(s32[4,8]{1,0:T(4,128)} %add_add_fusion.t, ...), custom_call_target="tpu_custom_call" | custom-call | tf_op jit(solution)/shard_map/attend/pallas_call | solution.py:436
  100.5 5.6 %collective-permute-start.14 = (bf16[8,4,16,128]{3,2,1,0:T(8,128)(2,1)}, bf16[8,4,16,128]{3,2,1,0:T(8,128)(2,1)S(1)}, u32[]{:S(2)}, u32[]{:S(2)}) collective-permute-start(bf16[8,4,16,128]{3,2,1,0:T(8,128)(2,1)} %get-tuple-element.39), channel_id=1, source_target_pairs={{0,7},{1,0},{2,1},{3,2},{4,3},{5,4},{6,5},{7,6},{8,15},{9,8},{10,9... | collective-permute-start | bytes 393224 | tf_op jit(solution)/shard_map/ppermute | solution.py:472
  106.2 7.2 %all-to-all-start.2 = ((bf16[32,2,16,1024]{3,2,1,0:T(8,128)(2,1)}), bf16[32,2,16,1024]{3,2,1,0:T(8,128)(2,1)S(1)}, u32[]{:S(2)}, u32[]{:S(2)}) async-start(bf16[32,2,16,1024]{3,2,1,0:T(8,128)(2,1)} %bitcast.17), calls=%async_computation.2 | async-start | bytes 4194304 | tf_op jit(solution)/shard_map/all_to_all | solution.py:503
  113.6 2.7 %collective-permute-start.21 = (bf16[8,4,16,128]{3,2,1,0:T(8,128)(2,1)S(1)}, bf16[8,4,16,128]{3,2,1,0:T(8,128)(2,1)S(1)}, u32[]{:S(2)}, u32[]{:S(2)}) collective-permute-start(bf16[8,4,16,128]{3,2,1,0:T(8,128)(2,1)S(1)} %copy-done.34), channel_id=1, source_target_pairs={{0,7},{1,0},{2,1},{3,2},{4,3},{5,4},{6,5},{7,6},{8,15},{9,8},{10,9... | collective-permute-start | bytes 393224 | tf_op jit(solution)/shard_map/ppermute | solution.py:472
  116.3 2.7 %collective-permute-start.15 = (bf16[8,4,16,128]{3,2,1,0:T(8,128)(2,1)S(1)}, bf16[8,4,16,128]{3,2,1,0:T(8,128)(2,1)S(1)}, u32[]{:S(2)}, u32[]{:S(2)}) collective-permute-start(bf16[8,4,16,128]{3,2,1,0:T(8,128)(2,1)S(1)} %add_convert_fusion.9), channel_id=1, source_target_pairs={{0,7},{1,0},{2,1},{3,2},{4,3},{5,4},{6,5},{7,6},{8,15},{9,8},{10,9... | collective-permute-start | bytes 393224 | tf_op jit(solution)/shard_map/ppermute | solution.py:472
  119.9 2.7 %collective-permute-start.22 = (bf16[8,4,16,128]{3,2,1,0:T(8,128)(2,1)S(1)}, bf16[8,4,16,128]{3,2,1,0:T(8,128)(2,1)S(1)}, u32[]{:S(2)}, u32[]{:S(2)}) collective-permute-start(bf16[8,4,16,128]{3,2,1,0:T(8,128)(2,1)S(1)} %add_convert_fusion.4), channel_id=1, source_target_pairs={{0,7},{1,0},{2,1},{3,2},{4,3},{5,4},{6,5},{7,6},{8,15},{9,8},{10,9... | collective-permute-start | bytes 393224 | tf_op jit(solution)/shard_map/ppermute | solution.py:472
  122.8 2.7 %collective-permute-start.16 = (bf16[8,4,16,128]{3,2,1,0:T(8,128)(2,1)S(1)}, bf16[8,4,16,128]{3,2,1,0:T(8,128)(2,1)S(1)}, u32[]{:S(2)}, u32[]{:S(2)}) collective-permute-start(bf16[8,4,16,128]{3,2,1,0:T(8,128)(2,1)S(1)} %add_convert_fusion.8), channel_id=1, source_target_pairs={{0,7},{1,0},{2,1},{3,2},{4,3},{5,4},{6,5},{7,6},{8,15},{9,8},{10,9... | collective-permute-start | bytes 393224 | tf_op jit(solution)/shard_map/ppermute | solution.py:472
  125.7 2.7 %collective-permute-start.23 = (bf16[8,4,16,128]{3,2,1,0:T(8,128)(2,1)S(1)}, bf16[8,4,16,128]{3,2,1,0:T(8,128)(2,1)S(1)}, u32[]{:S(2)}, u32[]{:S(2)}) collective-permute-start(bf16[8,4,16,128]{3,2,1,0:T(8,128)(2,1)S(1)} %add_convert_fusion.3), channel_id=1, source_target_pairs={{0,7},{1,0},{2,1},{3,2},{4,3},{5,4},{6,5},{7,6},{8,15},{9,8},{10,9... | collective-permute-start | bytes 393224 | tf_op jit(solution)/shard_map/ppermute | solution.py:472
  128.7 2.7 %collective-permute-start.17 = (bf16[8,4,16,128]{3,2,1,0:T(8,128)(2,1)S(1)}, bf16[8,4,16,128]{3,2,1,0:T(8,128)(2,1)S(1)}, u32[]{:S(2)}, u32[]{:S(2)}) collective-permute-start(bf16[8,4,16,128]{3,2,1,0:T(8,128)(2,1)S(1)} %add_convert_fusion.7), channel_id=1, source_target_pairs={{0,7},{1,0},{2,1},{3,2},{4,3},{5,4},{6,5},{7,6},{8,15},{9,8},{10,9... | collective-permute-start | bytes 393224 | tf_op jit(solution)/shard_map/ppermute | solution.py:472
  131.4 3.3 %collective-permute-start.24 = (bf16[8,4,16,128]{3,2,1,0:T(8,128)(2,1)S(1)}, bf16[8,4,16,128]{3,2,1,0:T(8,128)(2,1)S(1)}, u32[]{:S(2)}, u32[]{:S(2)}) collective-permute-start(bf16[8,4,16,128]{3,2,1,0:T(8,128)(2,1)S(1)} %add_convert_fusion.2), channel_id=1, source_target_pairs={{0,7},{1,0},{2,1},{3,2},{4,3},{5,4},{6,5},{7,6},{8,15},{9,8},{10,9... | collective-permute-start | bytes 393224 | tf_op jit(solution)/shard_map/ppermute | solution.py:472
  135.1 2.7 %collective-permute-done.24.va = bf16[8,4,16,128]{3,2,1,0:T(8,128)(2,1)S(1)} collective-permute-done((bf16[8,4,16,128]{3,2,1,0:T(8,128)(2,1)S(1)}, bf16[8,4,16,128]{3,2,1,0:T(8,128)(2,1)S(1)}, u32[]{:S(2)}, u32[]{:S(2)}) %collective-permute-start.24) | collective-permute-done | bytes 131104 | tf_op jit(solution)/shard_map/ppermute | solution.py:472
  138.4 2.1 %place_pair.1 = bf16[8,4,2,16,256]{4,3,2,1,0:T(8,128)(2,1)} custom-call(s32[4,8]{1,0:T(4,128)} %add_add_fusion.t, bf16[8,4,16,128]{3,2,1,0:T(8,128)(2,1)} %copy-done.15, bf16[8,4,16,128]{3,2,1,0:T(8,128)(2,1)} %copy-done.12, bf16[8,4,16,128]{3,2,1,0:T(8,128)(2,1)} %get-tuple-element.46.kc, bf16[8,4,16,128]{3,2,1,0:T(8,128)(2,1)} %copy-done.16, ...), custom_call_target="tpu_custom_call" | custom-call | tf_op jit(solution)/shard_map/place_pair/pallas_call | solution.py:185
  140.6 10.6 %all-to-all-start.3 = ((bf16[32,2,16,256]{3,2,1,0:T(8,128)(2,1)}), bf16[32,2,16,256]{3,2,1,0:T(8,128)(2,1)S(1)}, u32[]{:S(2)}, u32[]{:S(2)}) async-start(bf16[32,2,16,256]{3,2,1,0:T(8,128)(2,1)} %bitcast.16), calls=%async_computation.3 | async-start | bytes 1048576 | tf_op jit(solution)/shard_map/all_to_all | solution.py:503
  151.1 3.1 %home_wide.1 = bf16[128,4096]{1,0:T(8,128)(2,1)} custom-call(s32[64]{0:T(128)} %dest.6, bf16[8,4,2,16,1024]{4,3,2,1,0:T(8,128)(2,1)} %bitcast.13), custom_call_target="tpu_custom_call" | custom-call | tf_op jit(solution)/shard_map/home_wide/pallas_call | solution.py:206
  154.2 7.9 %all-to-all-done.3 = bf16[32,2,16,256]{3,2,1,0:T(8,128)(2,1)S(1)} async-done(((bf16[32,2,16,256]{3,2,1,0:T(8,128)(2,1)}), bf16[32,2,16,256]{3,2,1,0:T(8,128)(2,1)S(1)}, u32[]{:S(2)}, u32[]{:S(2)}) %all-to-all-start.3) | async-done | bytes 524320 | tf_op jit(solution)/shard_map/all_to_all | solution.py:503
  163.0 1.8 %home_pair.1 = (bf16[128,512]{1,0:T(8,128)(2,1)}, bf16[128,512]{1,0:T(8,128)(2,1)}) custom-call(s32[64]{0:T(128)} %dest.6, bf16[8,4,2,16,256]{4,3,2,1,0:T(8,128)(2,1)} %bitcast.18), custom_call_target="tpu_custom_call" | custom-call | tf_op jit(solution)/shard_map/home_pair/pallas_call | solution.py:228
  (133 shorter events, 10.6 us)
Async XLA Ops:
  3.8 30.1 %all-to-all-start = ((bf16[32,2,16,768]{3,2,1,0:T(8,128)(2,1)}), bf16[32,2,16,768]{3,2,1,0:T(8,128)(2,1)S(1)}, u32[]{:S(2)}, u32[]{:S(2)}) async-start(bf16[32,2,16,768]{3,2,1,0:T(8,128)(2,1)} %bitcast.15), calls=%async_computation | async-start | bytes 3145728 | tf_op jit(solution)/shard_map/all_to_all | solution.py:503
  35.1 44.7 %all-to-all-start.1 = ((bf16[32,2,16,1536]{3,2,1,0:T(8,128)(2,1)}), bf16[32,2,16,1536]{3,2,1,0:T(8,128)(2,1)}, u32[]{:S(2)}, u32[]{:S(2)}) async-start(bf16[32,2,16,1536]{3,2,1,0:T(8,128)(2,1)} %bitcast.12), calls=%async_computation.1 | async-start | bytes 6291456 | tf_op jit(solution)/shard_map/all_to_all | solution.py:503
  45.3 8.5 %collective-permute-start = (bf16[8,4,16,128]{3,2,1,0:T(8,128)(2,1)}, bf16[8,4,16,128]{3,2,1,0:T(8,128)(2,1)S(1)}, u32[]{:S(2)}, u32[]{:S(2)}) collective-permute-start(bf16[8,4,16,128]{3,2,1,0:T(8,128)(2,1)} %get-tuple-element.36.refs_0_), channel_id=1, source_target_pairs={{0,7},{1,0},{2,1},{3,2},{4,3},{5,4},{6,5},{7,6},{8,15},{9,8},{10,9... | collective-permute-start | bytes 393224 | tf_op jit(solution)/shard_map/ppermute | solution.py:472
  51.0 6.2 %collective-permute-start.7 = (bf16[8,4,16,128]{3,2,1,0:T(8,128)(2,1)}, bf16[8,4,16,128]{3,2,1,0:T(8,128)(2,1)S(1)}, u32[]{:S(2)}, u32[]{:S(2)}) collective-permute-start(bf16[8,4,16,128]{3,2,1,0:T(8,128)(2,1)} %get-tuple-element.37.refs_8_), channel_id=1, source_target_pairs={{0,7},{1,0},{2,1},{3,2},{4,3},{5,4},{6,5},{7,6},{8,15},{9,8},{10,9... | collective-permute-start | bytes 393224 | tf_op jit(solution)/shard_map/ppermute | solution.py:472
  51.7 8.3 %collective-permute-start.4 = (bf16[8,4,16,128]{3,2,1,0:T(8,128)(2,1)}, bf16[8,4,16,128]{3,2,1,0:T(8,128)(2,1)S(1)}, u32[]{:S(2)}, u32[]{:S(2)}) collective-permute-start(bf16[8,4,16,128]{3,2,1,0:T(8,128)(2,1)} %get-tuple-element.36.refs_0_), channel_id=1, source_target_pairs={{0,1},{1,2},{2,3},{3,4},{4,5},{5,6},{6,7},{7,0},{8,9},{9,10},{10,1... | collective-permute-start | bytes 393224 | tf_op jit(solution)/shard_map/ppermute | solution.py:472
  52.4 7.6 %collective-permute-start.11 = (bf16[8,4,16,128]{3,2,1,0:T(8,128)(2,1)}, bf16[8,4,16,128]{3,2,1,0:T(8,128)(2,1)S(1)}, u32[]{:S(2)}, u32[]{:S(2)}) collective-permute-start(bf16[8,4,16,128]{3,2,1,0:T(8,128)(2,1)} %get-tuple-element.37.refs_8_), channel_id=1, source_target_pairs={{0,1},{1,2},{2,3},{3,4},{4,5},{5,6},{6,7},{7,0},{8,9},{9,10},{10,1... | collective-permute-start | bytes 393224 | tf_op jit(solution)/shard_map/ppermute | solution.py:472
  53.8 6.3 %collective-permute-start.1 = (bf16[8,4,16,128]{3,2,1,0:T(8,128)(2,1)S(1)}, bf16[8,4,16,128]{3,2,1,0:T(8,128)(2,1)S(1)}, u32[]{:S(2)}, u32[]{:S(2)}) collective-permute-start(bf16[8,4,16,128]{3,2,1,0:T(8,128)(2,1)S(1)} %collective-permute-done.refs_1_), channel_id=1, source_target_pairs={{0,7},{1,0},{2,1},{3,2},{4,3},{5,4},{6,5},{7,6},{8,15},{9,8},{10,9... | collective-permute-start | bytes 393224 | tf_op jit(solution)/shard_map/ppermute | solution.py:472
  57.2 6.0 %collective-permute-start.8 = (bf16[8,4,16,128]{3,2,1,0:T(8,128)(2,1)S(1)}, bf16[8,4,16,128]{3,2,1,0:T(8,128)(2,1)S(1)}, u32[]{:S(2)}, u32[]{:S(2)}) collective-permute-start(bf16[8,4,16,128]{3,2,1,0:T(8,128)(2,1)S(1)} %collective-permute-done.7.refs_9_), channel_id=1, source_target_pairs={{0,7},{1,0},{2,1},{3,2},{4,3},{5,4},{6,5},{7,6},{8,15},{9,8},{10,9... | collective-permute-start | bytes 393224 | tf_op jit(solution)/shard_map/ppermute | solution.py:472
  60.0 6.7 %collective-permute-start.5 = (bf16[8,4,16,128]{3,2,1,0:T(8,128)(2,1)S(1)}, bf16[8,4,16,128]{3,2,1,0:T(8,128)(2,1)S(1)}, u32[]{:S(2)}, u32[]{:S(2)}) collective-permute-start(bf16[8,4,16,128]{3,2,1,0:T(8,128)(2,1)S(1)} %collective-permute-done.4.refs_7_), channel_id=1, source_target_pairs={{0,1},{1,2},{2,3},{3,4},{4,5},{5,6},{6,7},{7,0},{8,9},{9,10},{10,1... | collective-permute-start | bytes 393224 | tf_op jit(solution)/shard_map/ppermute | solution.py:472
  60.1 7.6 %collective-permute-start.12 = (bf16[8,4,16,128]{3,2,1,0:T(8,128)(2,1)S(1)}, bf16[8,4,16,128]{3,2,1,0:T(8,128)(2,1)S(1)}, u32[]{:S(2)}, u32[]{:S(2)}) collective-permute-start(bf16[8,4,16,128]{3,2,1,0:T(8,128)(2,1)S(1)} %collective-permute-done.11.refs_15_), channel_id=1, source_target_pairs={{0,1},{1,2},{2,3},{3,4},{4,5},{5,6},{6,7},{7,0},{8,9},{9,10},{10,1... | collective-permute-start | bytes 393224 | tf_op jit(solution)/shard_map/ppermute | solution.py:472
  60.1 7.6 %collective-permute-start.2 = (bf16[8,4,16,128]{3,2,1,0:T(8,128)(2,1)S(1)}, bf16[8,4,16,128]{3,2,1,0:T(8,128)(2,1)S(1)}, u32[]{:S(2)}, u32[]{:S(2)}) collective-permute-start(bf16[8,4,16,128]{3,2,1,0:T(8,128)(2,1)S(1)} %collective-permute-done.1.refs_2_), channel_id=1, source_target_pairs={{0,7},{1,0},{2,1},{3,2},{4,3},{5,4},{6,5},{7,6},{8,15},{9,8},{10,9... | collective-permute-start | bytes 393224 | tf_op jit(solution)/shard_map/ppermute | solution.py:472
  63.2 7.2 %collective-permute-start.9 = (bf16[8,4,16,128]{3,2,1,0:T(8,128)(2,1)S(1)}, bf16[8,4,16,128]{3,2,1,0:T(8,128)(2,1)S(1)}, u32[]{:S(2)}, u32[]{:S(2)}) collective-permute-start(bf16[8,4,16,128]{3,2,1,0:T(8,128)(2,1)S(1)} %collective-permute-done.8.refs_10_), channel_id=1, source_target_pairs={{0,7},{1,0},{2,1},{3,2},{4,3},{5,4},{6,5},{7,6},{8,15},{9,8},{10,9... | collective-permute-start | bytes 393224 | tf_op jit(solution)/shard_map/ppermute | solution.py:472
  66.7 6.7 %collective-permute-start.6 = (bf16[8,4,16,128]{3,2,1,0:T(8,128)(2,1)S(1)}, bf16[8,4,16,128]{3,2,1,0:T(8,128)(2,1)S(1)}, u32[]{:S(2)}, u32[]{:S(2)}) collective-permute-start(bf16[8,4,16,128]{3,2,1,0:T(8,128)(2,1)S(1)} %collective-permute-done.5.refs_6_), channel_id=1, source_target_pairs={{0,1},{1,2},{2,3},{3,4},{4,5},{5,6},{6,7},{7,0},{8,9},{9,10},{10,1... | collective-permute-start | bytes 393224 | tf_op jit(solution)/shard_map/ppermute | solution.py:472
  67.7 5.9 %collective-permute-start.13 = (bf16[8,4,16,128]{3,2,1,0:T(8,128)(2,1)S(1)}, bf16[8,4,16,128]{3,2,1,0:T(8,128)(2,1)S(1)}, u32[]{:S(2)}, u32[]{:S(2)}) collective-permute-start(bf16[8,4,16,128]{3,2,1,0:T(8,128)(2,1)S(1)} %collective-permute-done.12.refs_14_), channel_id=1, source_target_pairs={{0,1},{1,2},{2,3},{3,4},{4,5},{5,6},{6,7},{7,0},{8,9},{9,10},{10,1... | collective-permute-start | bytes 393224 | tf_op jit(solution)/shard_map/ppermute | solution.py:472
  67.7 5.9 %collective-permute-start.3 = (bf16[8,4,16,128]{3,2,1,0:T(8,128)(2,1)S(1)}, bf16[8,4,16,128]{3,2,1,0:T(8,128)(2,1)S(1)}, u32[]{:S(2)}, u32[]{:S(2)}) collective-permute-start(bf16[8,4,16,128]{3,2,1,0:T(8,128)(2,1)S(1)} %collective-permute-done.2.refs_3_), channel_id=1, source_target_pairs={{0,7},{1,0},{2,1},{3,2},{4,3},{5,4},{6,5},{7,6},{8,15},{9,8},{10,9... | collective-permute-start | bytes 393224 | tf_op jit(solution)/shard_map/ppermute | solution.py:472
  70.4 5.5 %collective-permute-start.10 = (bf16[8,4,16,128]{3,2,1,0:T(8,128)(2,1)S(1)}, bf16[8,4,16,128]{3,2,1,0:T(8,128)(2,1)}, u32[]{:S(2)}, u32[]{:S(2)}) collective-permute-start(bf16[8,4,16,128]{3,2,1,0:T(8,128)(2,1)S(1)} %collective-permute-done.9.refs_11_), channel_id=1, source_target_pairs={{0,7},{1,0},{2,1},{3,2},{4,3},{5,4},{6,5},{7,6},{8,15},{9,8},{10,9... | collective-permute-start | bytes 393224 | tf_op jit(solution)/shard_map/ppermute | solution.py:472
  100.5 15.8 %collective-permute-start.14 = (bf16[8,4,16,128]{3,2,1,0:T(8,128)(2,1)}, bf16[8,4,16,128]{3,2,1,0:T(8,128)(2,1)S(1)}, u32[]{:S(2)}, u32[]{:S(2)}) collective-permute-start(bf16[8,4,16,128]{3,2,1,0:T(8,128)(2,1)} %get-tuple-element.39), channel_id=1, source_target_pairs={{0,7},{1,0},{2,1},{3,2},{4,3},{5,4},{6,5},{7,6},{8,15},{9,8},{10,9... | collective-permute-start | bytes 393224 | tf_op jit(solution)/shard_map/ppermute | solution.py:472
  106.2 34.4 %all-to-all-start.2 = ((bf16[32,2,16,1024]{3,2,1,0:T(8,128)(2,1)}), bf16[32,2,16,1024]{3,2,1,0:T(8,128)(2,1)S(1)}, u32[]{:S(2)}, u32[]{:S(2)}) async-start(bf16[32,2,16,1024]{3,2,1,0:T(8,128)(2,1)} %bitcast.17), calls=%async_computation.2 | async-start | bytes 4194304 | tf_op jit(solution)/shard_map/all_to_all | solution.py:503
  113.5 6.2 %collective-permute-start.18 = (bf16[8,4,16,128]{3,2,1,0:T(8,128)(2,1)S(1)}, bf16[8,4,16,128]{3,2,1,0:T(8,128)(2,1)S(1)}, u32[]{:S(2)}, u32[]{:S(2)}) collective-permute-start(bf16[8,4,16,128]{3,2,1,0:T(8,128)(2,1)S(1)} %copy-done.35), channel_id=1, source_target_pairs={{0,1},{1,2},{2,3},{3,4},{4,5},{5,6},{6,7},{7,0},{8,9},{9,10},{10,1... | collective-permute-start | bytes 393224 | tf_op jit(solution)/shard_map/ppermute | solution.py:472
  113.6 6.2 %collective-permute-start.21 = (bf16[8,4,16,128]{3,2,1,0:T(8,128)(2,1)S(1)}, bf16[8,4,16,128]{3,2,1,0:T(8,128)(2,1)S(1)}, u32[]{:S(2)}, u32[]{:S(2)}) collective-permute-start(bf16[8,4,16,128]{3,2,1,0:T(8,128)(2,1)S(1)} %copy-done.34), channel_id=1, source_target_pairs={{0,7},{1,0},{2,1},{3,2},{4,3},{5,4},{6,5},{7,6},{8,15},{9,8},{10,9... | collective-permute-start | bytes 393224 | tf_op jit(solution)/shard_map/ppermute | solution.py:472
  116.3 6.3 %collective-permute-start.25 = (bf16[8,4,16,128]{3,2,1,0:T(8,128)(2,1)S(1)}, bf16[8,4,16,128]{3,2,1,0:T(8,128)(2,1)S(1)}, u32[]{:S(2)}, u32[]{:S(2)}) collective-permute-start(bf16[8,4,16,128]{3,2,1,0:T(8,128)(2,1)S(1)} %copy-done.33), channel_id=1, source_target_pairs={{0,1},{1,2},{2,3},{3,4},{4,5},{5,6},{6,7},{7,0},{8,9},{9,10},{10,1... | collective-permute-start | bytes 393224 | tf_op jit(solution)/shard_map/ppermute | solution.py:472
  116.3 6.4 %collective-permute-start.15 = (bf16[8,4,16,128]{3,2,1,0:T(8,128)(2,1)S(1)}, bf16[8,4,16,128]{3,2,1,0:T(8,128)(2,1)S(1)}, u32[]{:S(2)}, u32[]{:S(2)}) collective-permute-start(bf16[8,4,16,128]{3,2,1,0:T(8,128)(2,1)S(1)} %add_convert_fusion.9), channel_id=1, source_target_pairs={{0,7},{1,0},{2,1},{3,2},{4,3},{5,4},{6,5},{7,6},{8,15},{9,8},{10,9... | collective-permute-start | bytes 393224 | tf_op jit(solution)/shard_map/ppermute | solution.py:472
  119.7 5.8 %collective-permute-start.19 = (bf16[8,4,16,128]{3,2,1,0:T(8,128)(2,1)S(1)}, bf16[8,4,16,128]{3,2,1,0:T(8,128)(2,1)S(1)}, u32[]{:S(2)}, u32[]{:S(2)}) collective-permute-start(bf16[8,4,16,128]{3,2,1,0:T(8,128)(2,1)S(1)} %add_convert_fusion.6), channel_id=1, source_target_pairs={{0,1},{1,2},{2,3},{3,4},{4,5},{5,6},{6,7},{7,0},{8,9},{9,10},{10,1... | collective-permute-start | bytes 393224 | tf_op jit(solution)/shard_map/ppermute | solution.py:472
  119.9 5.8 %collective-permute-start.22 = (bf16[8,4,16,128]{3,2,1,0:T(8,128)(2,1)S(1)}, bf16[8,4,16,128]{3,2,1,0:T(8,128)(2,1)S(1)}, u32[]{:S(2)}, u32[]{:S(2)}) collective-permute-start(bf16[8,4,16,128]{3,2,1,0:T(8,128)(2,1)S(1)} %add_convert_fusion.4), channel_id=1, source_target_pairs={{0,7},{1,0},{2,1},{3,2},{4,3},{5,4},{6,5},{7,6},{8,15},{9,8},{10,9... | collective-permute-start | bytes 393224 | tf_op jit(solution)/shard_map/ppermute | solution.py:472
  122.6 5.8 %collective-permute-start.26 = (bf16[8,4,16,128]{3,2,1,0:T(8,128)(2,1)S(1)}, bf16[8,4,16,128]{3,2,1,0:T(8,128)(2,1)S(1)}, u32[]{:S(2)}, u32[]{:S(2)}) collective-permute-start(bf16[8,4,16,128]{3,2,1,0:T(8,128)(2,1)S(1)} %add_convert_fusion.1), channel_id=1, source_target_pairs={{0,1},{1,2},{2,3},{3,4},{4,5},{5,6},{6,7},{7,0},{8,9},{9,10},{10,1... | collective-permute-start | bytes 393224 | tf_op jit(solution)/shard_map/ppermute | solution.py:472
  122.8 5.8 %collective-permute-start.16 = (bf16[8,4,16,128]{3,2,1,0:T(8,128)(2,1)S(1)}, bf16[8,4,16,128]{3,2,1,0:T(8,128)(2,1)S(1)}, u32[]{:S(2)}, u32[]{:S(2)}) collective-permute-start(bf16[8,4,16,128]{3,2,1,0:T(8,128)(2,1)S(1)} %add_convert_fusion.8), channel_id=1, source_target_pairs={{0,7},{1,0},{2,1},{3,2},{4,3},{5,4},{6,5},{7,6},{8,15},{9,8},{10,9... | collective-permute-start | bytes 393224 | tf_op jit(solution)/shard_map/ppermute | solution.py:472
  125.6 9.2 %collective-permute-start.20 = (bf16[8,4,16,128]{3,2,1,0:T(8,128)(2,1)S(1)}, bf16[8,4,16,128]{3,2,1,0:T(8,128)(2,1)S(1)}, u32[]{:S(2)}, u32[]{:S(2)}) collective-permute-start(bf16[8,4,16,128]{3,2,1,0:T(8,128)(2,1)S(1)} %add_convert_fusion.5), channel_id=1, source_target_pairs={{0,1},{1,2},{2,3},{3,4},{4,5},{5,6},{6,7},{7,0},{8,9},{9,10},{10,1... | collective-permute-start | bytes 393224 | tf_op jit(solution)/shard_map/ppermute | solution.py:472
  125.7 5.7 %collective-permute-start.23 = (bf16[8,4,16,128]{3,2,1,0:T(8,128)(2,1)S(1)}, bf16[8,4,16,128]{3,2,1,0:T(8,128)(2,1)S(1)}, u32[]{:S(2)}, u32[]{:S(2)}) collective-permute-start(bf16[8,4,16,128]{3,2,1,0:T(8,128)(2,1)S(1)} %add_convert_fusion.3), channel_id=1, source_target_pairs={{0,7},{1,0},{2,1},{3,2},{4,3},{5,4},{6,5},{7,6},{8,15},{9,8},{10,9... | collective-permute-start | bytes 393224 | tf_op jit(solution)/shard_map/ppermute | solution.py:472
  128.5 6.6 %collective-permute-start.27 = (bf16[8,4,16,128]{3,2,1,0:T(8,128)(2,1)S(1)}, bf16[8,4,16,128]{3,2,1,0:T(8,128)(2,1)S(1)}, u32[]{:S(2)}, u32[]{:S(2)}) collective-permute-start(bf16[8,4,16,128]{3,2,1,0:T(8,128)(2,1)S(1)} %add_convert_fusion), channel_id=1, source_target_pairs={{0,1},{1,2},{2,3},{3,4},{4,5},{5,6},{6,7},{7,0},{8,9},{9,10},{10,1... | collective-permute-start | bytes 393224 | tf_op jit(solution)/shard_map/ppermute | solution.py:472
  128.7 6.4 %collective-permute-start.17 = (bf16[8,4,16,128]{3,2,1,0:T(8,128)(2,1)S(1)}, bf16[8,4,16,128]{3,2,1,0:T(8,128)(2,1)S(1)}, u32[]{:S(2)}, u32[]{:S(2)}) collective-permute-start(bf16[8,4,16,128]{3,2,1,0:T(8,128)(2,1)S(1)} %add_convert_fusion.7), channel_id=1, source_target_pairs={{0,7},{1,0},{2,1},{3,2},{4,3},{5,4},{6,5},{7,6},{8,15},{9,8},{10,9... | collective-permute-start | bytes 393224 | tf_op jit(solution)/shard_map/ppermute | solution.py:472
  131.4 6.4 %collective-permute-start.24 = (bf16[8,4,16,128]{3,2,1,0:T(8,128)(2,1)S(1)}, bf16[8,4,16,128]{3,2,1,0:T(8,128)(2,1)S(1)}, u32[]{:S(2)}, u32[]{:S(2)}) collective-permute-start(bf16[8,4,16,128]{3,2,1,0:T(8,128)(2,1)S(1)} %add_convert_fusion.2), channel_id=1, source_target_pairs={{0,7},{1,0},{2,1},{3,2},{4,3},{5,4},{6,5},{7,6},{8,15},{9,8},{10,9... | collective-permute-start | bytes 393224 | tf_op jit(solution)/shard_map/ppermute | solution.py:472
  140.6 21.6 %all-to-all-start.3 = ((bf16[32,2,16,256]{3,2,1,0:T(8,128)(2,1)}), bf16[32,2,16,256]{3,2,1,0:T(8,128)(2,1)S(1)}, u32[]{:S(2)}, u32[]{:S(2)}) async-start(bf16[32,2,16,256]{3,2,1,0:T(8,128)(2,1)} %bitcast.16), calls=%async_computation.3 | async-start | bytes 1048576 | tf_op jit(solution)/shard_map/all_to_all | solution.py:503
  (36 other events, 373.3 us)

commit v4 on v3

--- a/solution.py
+++ b/solution.py
@@ -170,6 +170,7 @@
             pltpu.VMEM(late, BF16),
             pltpu.SemaphoreType.DMA((3,)),
         ],
+        compiler_params=params(8),
         name="pick_first",
     )(table, x)
 
@@ -187,6 +188,7 @@
         in_specs=[whole(pltpu.SMEM)] + [whole(pltpu.VMEM)] * 6,
         out_specs=whole(pltpu.VMEM),
         out_shape=jax.ShapeDtypeStruct((N_DP, N_Y, CAP, BR, 2 * HEAD), BF16),
+        compiler_params=params(8),
         name="place_pair",
     )(table, *dk, *dv)
 
@@ -230,6 +232,7 @@
         in_specs=[whole(pltpu.SMEM), whole(pltpu.VMEM)],
         out_specs=[whole(pltpu.VMEM), whole(pltpu.VMEM)],
         out_shape=[out, out],
+        compiler_params=params(8),
         name="home_pair",
     )(dest, x)
 
@@ -253,7 +256,7 @@
 def attend_body(t, soon_hbm, rest_hbm, *refs):
     ins, refs = refs[:2 * N_Z], refs[2 * N_Z:]
     dq_hbm, outs, refs = refs[0], refs[1:1 + 2 * N_Z], refs[1 + 2 * N_Z:]
-    (soon_buf, rest_buf, kv_buf, dq_buf, dkv_buf, ks, vs, kt, qm, gm, bias, sc, dp, acc_k, acc_v,
+    (soon_buf, rest_buf, dq_buf, dkv_buf, ks, vs, kt, qm, gm, bias, sc, dp, acc_k, acc_v,
      dqt, qg_in, kv_in, dq_out, dkv_out) = refs
     bands = (pl.ds(SPAN, SPAN), pl.ds(0, SPAN))
     z = t[3, 0]
@@ -267,8 +270,10 @@
                 rest_hbm.at[t[0, s], :, t[1, s]], rest_buf.at[s], qg_in.at[1, s]))
 
     def kv_copies(n):
-        return [pltpu.make_async_copy(ins[i].at[bands[n]], kv_buf.at[i, bands[n]], kv_in.at[n, i])
-                for i in range(2 * N_Z)]
+        return [pltpu.make_async_copy(ins[c * N_Z + r].at[bands[n]],
+                                      ref.at[bands[n], :, pl.ds(spots[r], BR), :],
+                                      kv_in.at[n, c * N_Z + r])
+                for c, ref in enumerate((ks, vs)) for r in range(N_Z)]
 
     def dkv_copies(n):
         return [pltpu.make_async_copy(dkv_buf.at[i, bands[n]], outs[i].at[bands[n]],
@@ -293,6 +298,30 @@
     bias[...] = jnp.where(key <= query, 0.0, NEG).astype(F32)
     halves = (slice(0, HALF), slice(HALF, BLOCK))
     own = SPAN - 1
+    acc_k[...] = jnp.zeros(acc_k.shape, F32)
+    acc_v[...] = jnp.zeros(acc_v.shape, F32)
+
+    def keys_of(ref, o, part):
+        rows = ref[o, part.start // HEAD:part.stop // HEAD]
+        return rows.reshape(part.stop - part.start, HEAD)
+
+    def fill(s, at):
+        for y in range(N_Y):
+            for h in range(PER_KEY):
+                rows = pl.ds(y * HEAD + h * BR, BR)
+                late = h * HEAD < LATER
+                buf, span = (rest_buf, LATER) if late else (soon_buf, SOON)
+                col = h * HEAD if late else h * HEAD - LATER
+                qm[at, rows, :] = buf[s, y, :, col:col + HEAD]
+                gm[at, rows, :] = buf[s, y, :, span + col:span + col + HEAD]
+
+    def finish(s, at):
+        dq = (dqt[at] * SCALE).astype(BF16).T
+        for y in range(N_Y):
+            for h in range(PER_KEY):
+                row = y * HEAD + h * BR
+                dq_buf[s, y, :, h * HEAD:(h + 1) * HEAD] = dq[row:row + BR]
+
 
     def lay(n, ready):
         o = ready - 1
@@ -302,26 +331,22 @@
             for copy in kv_copies(1):
                 copy.wait()
 
-        for y in range(N_Y):
-            for r in range(N_Z):
-                rows = pl.ds(y * HEAD + spots[r], BR)
-                ks[o, rows] = kv_buf[r, o, y]
-                vs[o, rows] = kv_buf[N_Z + r, o, y]
-        kt[o] = ks[o].T
-        acc_k[o] = jnp.zeros((BLOCK, HEAD), F32)
-        acc_v[o] = jnp.zeros((BLOCK, HEAD), F32)
+        kt[o] = ks[o].reshape(BLOCK, HEAD).T
         return o
 
     def work(s, first, count):
         low, high = halves
         full = slice(0, BLOCK)
         blocks = [(first + i, i) for i in range(count)]
+        now, other = lax.rem(s, 2), lax.rem(s + 1, 2)
+        finish(s + 1, other)
+        fill(jnp.maximum(s - 1, 0), other)
 
         def score_tile(o, at, keys, rows, masked):
             top = None
             for k0 in range(keys.start, keys.stop, TILE):
                 part = slice(k0, k0 + TILE)
-                x = dot_nt(ks[o, part], qm[rows])
+                x = dot_nt(keys_of(ks, o, part), qm[now, rows])
                 if masked:
                     x = x + bias[k0 - keys.start:k0 - keys.start + TILE]
                 sc[at, part, rows] = x
@@ -341,7 +366,7 @@
             total = moment = None
             for k0 in range(keys.start, keys.stop, TILE):
                 part = slice(k0, k0 + TILE)
-                d = dot_nt(vs[o, part], gm[rows])
+                d = dot_nt(keys_of(vs, o, part), gm[now, rows])
                 e = jnp.exp2((sc[at, part, rows] - top) * EXP_SCALE)
                 sc[at, part, rows] = e
                 dp[at, part, rows] = d
@@ -371,13 +396,13 @@
                 p = sc[at, part, rows] * inverse[:, rows]
                 w = p.astype(BF16)
                 ds = (p * (dp[at, part, rows] - delta[:, rows])).astype(BF16)
-                acc_v[o, part] += dot_nn(w, gm[rows])
-                acc_k[o, part] += dot_nn(ds, qm[rows])
+                acc_v[o, part] += dot_nn(w, gm[now, rows])
+                acc_k[o, part] += dot_nn(ds, qm[now, rows])
                 term = dot_nn(kt[o, :, part], ds)
                 if fresh and k0 == keys.start:
-                    dqt[:, rows] = term
+                    dqt[now, :, rows] = term
                 else:
-                    dqt[:, rows] += term
+                    dqt[now, :, rows] += term
 
         grad_tile(s, own, low, full, True)
         grad_tile(s, own, high, high, False)
@@ -388,30 +413,23 @@
                 dkv_buf[N_Z + r, s, y] = acc_v[s, rows].astype(BF16)
         for o, i in blocks:
             grad_tile(o, i, full, full, False)
-        dq = (dqt[...] * SCALE).T.astype(BF16)
-        for y in range(N_Y):
-            for h in range(PER_KEY):
-                at = y * HEAD + h * BR
-                dq_buf[s, y, :, h * HEAD:(h + 1) * HEAD] = dq[at:at + BR]
 
     def step(n, ready):
         s = SLOTS - 1 - n
         first = t[2, s]
         ready = lax.fori_loop(0, ready - first, lay, ready)
-        for copy in qg_copies(s):
-            copy.wait()
-        for y in range(N_Y):
-            for h in range(PER_KEY):
-                rows = pl.ds(y * HEAD + h * BR, BR)
-                late = h * HEAD < LATER
-                buf, span = (rest_buf, LATER) if late else (soon_buf, SOON)
-                at = h * HEAD if late else h * HEAD - LATER
-                qm[rows, :] = buf[s, y, :, at:at + HEAD]
-                gm[rows, :] = buf[s, y, :, span + at:span + at + HEAD]
+
+        @pl.when(s > 0)
+        def _():
+            for copy in qg_copies(s - 1):
+                copy.wait()
+
         for count in range(SPAN):
             pl.when(s - first == count)(functools.partial(work, s, first, count))
 
-        dq_copy(s).start()
+        @pl.when(s < SLOTS - 1)
+        def _():
+            dq_copy(s + 1).start()
 
         @pl.when(s == SPAN)
         def _():
@@ -420,9 +438,12 @@
 
         return ready
 
-    for copy in kv_copies(0):
+    for copy in qg_copies(SLOTS - 1) + tuple(kv_copies(0)):
         copy.wait()
+    fill(SLOTS - 1, (SLOTS - 1) % 2)
     lax.fori_loop(0, SLOTS, step, SLOTS)
+    finish(0, 0)
+    dq_copy(0).start()
     for copy in dkv_copies(1):
         copy.start()
     for n in range(2):
@@ -441,20 +462,19 @@
         scratch_shapes=[
             pltpu.VMEM((SLOTS, N_Y, BR, 2 * SOON), BF16),
             pltpu.VMEM((SLOTS, N_Y, BR, 2 * LATER), BF16),
+            pltpu.VMEM((SLOTS + 1, N_Y, BR, WIDE), BF16),
             pltpu.VMEM((2 * N_Z,) + CHUNK, BF16),
-            pltpu.VMEM((SLOTS, N_Y, BR, WIDE), BF16),
-            pltpu.VMEM((2 * N_Z,) + CHUNK, BF16),
-            pltpu.VMEM((SLOTS, BLOCK, HEAD), BF16),
-            pltpu.VMEM((SLOTS, BLOCK, HEAD), BF16),
+            pltpu.VMEM((SLOTS, N_Y, HEAD, HEAD), BF16),
+            pltpu.VMEM((SLOTS, N_Y, HEAD, HEAD), BF16),
             pltpu.VMEM((SLOTS, HEAD, BLOCK), BF16),
-            pltpu.VMEM((BLOCK, HEAD), BF16),
-            pltpu.VMEM((BLOCK, HEAD), BF16),
+            pltpu.VMEM((2, BLOCK, HEAD), BF16),
+            pltpu.VMEM((2, BLOCK, HEAD), BF16),
             pltpu.VMEM((HALF, HALF), F32),
             pltpu.VMEM((SPAN, BLOCK, BLOCK), F32),
             pltpu.VMEM((SPAN, BLOCK, BLOCK), F32),
             pltpu.VMEM((SLOTS, BLOCK, HEAD), F32),
             pltpu.VMEM((SLOTS, BLOCK, HEAD), F32),
-            pltpu.VMEM((HEAD, BLOCK), F32),
+            pltpu.VMEM((2, HEAD, BLOCK), F32),
             pltpu.SemaphoreType.DMA((2, SLOTS)),
             pltpu.SemaphoreType.DMA((2, 2 * N_Z)),
             pltpu.SemaphoreType.DMA((SLOTS,)),

time: 166 us -> 161 us (0.970)
  Pallas kernels: 36.4 us -> 33.8 us
  waiting for transfers between devices: 37.6 us -> 39.7 us
  local copies, waits for them, and re-layouts: 4.31 us -> 2.45 us
  starting transfers between devices: 83.3 us -> 81.6 us
    all_to_all x4, waiting for transfers between devices: 30.1 us -> 32.2 us  [swap(): return lax.all_to_all(flat, ('dp', 'y'), 0, 0, tiled=True).reshape(x.shape)]
    unnamed x72 -> x76, local copies, waits for them, and re-layouts: 4.08 us -> 2.22 us
    all_to_all x4, starting transfers between devices: 32.3 us -> 30.6 us  [swap(): return lax.all_to_all(flat, ('dp', 'y'), 0, 0, tiled=True).reshape(x.shape)]
  transfers between devices with their start and end apart: 32 -> 32, of which waited for: 12 -> 13; matrix products, arithmetic and copies ran while one was open for 1% -> 1% of each run, Pallas kernels for 7% -> 6%
where the time goes in v4:
time: 161 us; the launch traced here: 160 us
  starting transfers between devices  81.6 us (51%)
  waiting for transfers between devices  39.7 us (25%)
  Pallas kernels  33.8 us (21%)
  local copies, waits for them, and re-layouts  2.45 us (2%)
    ppermute x28, starting transfers between devices, hop(): return lax.ppermute(x, 'z', [(i, (i + step) % N_Z) for i in range(N_Z)])  51 us
    all_to_all x4, waiting for transfers between devices, swap(): return lax.all_to_all(flat, ('dp', 'y'), 0, 0, tiled=True).reshape(x.shape)  32.2 us
    all_to_all x4, starting transfers between devices, swap(): return lax.all_to_all(flat, ('dp', 'y'), 0, 0, tiled=True).reshape(x.shape)  30.6 us
    pallas_call x1, Pallas kernels, attend(): pl.pallas_call(attend_body, in_specs=[whole(pltpu.SMEM), whole(pl.ANY), w...  20.5 us
    ppermute x28, waiting for transfers between devices, hop(): return lax.ppermute(x, 'z', [(i, (i + step) % N_Z) for i in range(N_Z)])  7.5 us
    pallas_call x1, Pallas kernels, pack_rest(): pl.pallas_call(pack_rest_body, in_specs=[whole(pltpu.SMEM), whole(pltpu.V...  3.31 us
  transfers between devices with their start and end apart: 32, of which 13 were waited for; matrix products, arithmetic and copies ran while one was open for 1% of the time, Pallas kernels for 6%

profile of v4, /device:TPU:1, one launch (start us, length us, event | category | flops | bytes accessed | tf_op | source)
XLA Modules:
  0.0 160.3 jit_solution(1134850165668371720)
XLA Ops:
  0.6 3.1 %pack_first.1 = bf16[8,4,2,16,768]{4,3,2,1,0:T(8,128)(2,1)} custom-call(s32[64]{0:T(128)} %dest.6, bf16[128,512]{1,0:T(8,128)(2,1)} %k.1, bf16[128,512]{1,0:T(8,128)(2,1)} %v.1, bf16[128,4096]{1,0:T(8,128)(2,1)} %q.3, bf16[128,4096]{1,0:T(8,128)(2,1)} %g.3), custom_call_target="tpu_custom_call" | custom-call | tf_op jit(solution)/shard_map/pack_first/pallas_call | solution.py:109
  3.8 8.6 %all-to-all-start = ((bf16[32,2,16,768]{3,2,1,0:T(8,128)(2,1)}), bf16[32,2,16,768]{3,2,1,0:T(8,128)(2,1)S(1)}, u32[]{:S(2)}, u32[]{:S(2)}) async-start(bf16[32,2,16,768]{3,2,1,0:T(8,128)(2,1)} %bitcast.16), calls=%async_computation | async-start | bytes 3145728 | tf_op jit(solution)/shard_map/all_to_all | solution.py:523
  12.4 3.3 %pack_rest.1 = bf16[8,4,2,16,1536]{4,3,2,1,0:T(8,128)(2,1)} custom-call(s32[64]{0:T(128)} %dest.6, bf16[128,4096]{1,0:T(8,128)(2,1)} %q.3, bf16[128,4096]{1,0:T(8,128)(2,1)} %g.3), custom_call_target="tpu_custom_call" | custom-call | tf_op jit(solution)/shard_map/pack_rest/pallas_call | solution.py:138
  15.7 18.2 %all-to-all-done = bf16[32,2,16,768]{3,2,1,0:T(8,128)(2,1)S(1)} async-done(((bf16[32,2,16,768]{3,2,1,0:T(8,128)(2,1)}), bf16[32,2,16,768]{3,2,1,0:T(8,128)(2,1)S(1)}, u32[]{:S(2)}, u32[]{:S(2)}) %all-to-all-start) | async-done | bytes 1572896 | tf_op jit(solution)/shard_map/all_to_all | solution.py:523
  33.8 6.0 %all-to-all-start.1 = ((bf16[32,2,16,1536]{3,2,1,0:T(8,128)(2,1)}), bf16[32,2,16,1536]{3,2,1,0:T(8,128)(2,1)}, u32[]{:S(2)}, u32[]{:S(2)}) async-start(bf16[32,2,16,1536]{3,2,1,0:T(8,128)(2,1)} %bitcast.14), calls=%async_computation.1 | async-start | bytes 6291456 | tf_op jit(solution)/shard_map/all_to_all | solution.py:523
  41.2 1.1 pick_first.1
  43.1 5.6 %collective-permute-start = (bf16[8,4,16,128]{3,2,1,0:T(8,128)(2,1)S(1)}, bf16[8,4,16,128]{3,2,1,0:T(8,128)(2,1)S(1)}, u32[]{:S(2)}, u32[]{:S(2)}) collective-permute-start(bf16[8,4,16,128]{3,2,1,0:T(8,128)(2,1)S(1)} %get-tuple-element.36.refs_0_), channel_id=1, source_target_pairs={{0,7},{1,0},{2,1},{3,2},{4,3},{5,4},{6,5},{7,6},{8,15},{9,8},{10,9... | collective-permute-start | bytes 393224 | tf_op jit(solution)/shard_map/ppermute | solution.py:492
  51.2 3.5 %collective-permute-start.1 = (bf16[8,4,16,128]{3,2,1,0:T(8,128)(2,1)S(1)}, bf16[8,4,16,128]{3,2,1,0:T(8,128)(2,1)S(1)}, u32[]{:S(2)}, u32[]{:S(2)}) collective-permute-start(bf16[8,4,16,128]{3,2,1,0:T(8,128)(2,1)S(1)} %collective-permute-done.refs_1_), channel_id=1, source_target_pairs={{0,7},{1,0},{2,1},{3,2},{4,3},{5,4},{6,5},{7,6},{8,15},{9,8},{10,9... | collective-permute-start | bytes 393224 | tf_op jit(solution)/shard_map/ppermute | solution.py:492
  54.7 2.8 %collective-permute-start.8 = (bf16[8,4,16,128]{3,2,1,0:T(8,128)(2,1)S(1)}, bf16[8,4,16,128]{3,2,1,0:T(8,128)(2,1)S(1)}, u32[]{:S(2)}, u32[]{:S(2)}) collective-permute-start(bf16[8,4,16,128]{3,2,1,0:T(8,128)(2,1)S(1)} %collective-permute-done.7.refs_9_), channel_id=1, source_target_pairs={{0,7},{1,0},{2,1},{3,2},{4,3},{5,4},{6,5},{7,6},{8,15},{9,8},{10,9... | collective-permute-start | bytes 393224 | tf_op jit(solution)/shard_map/ppermute | solution.py:492
  57.6 2.6 %collective-permute-start.2 = (bf16[8,4,16,128]{3,2,1,0:T(8,128)(2,1)S(1)}, bf16[8,4,16,128]{3,2,1,0:T(8,128)(2,1)S(1)}, u32[]{:S(2)}, u32[]{:S(2)}) collective-permute-start(bf16[8,4,16,128]{3,2,1,0:T(8,128)(2,1)S(1)} %collective-permute-done.1.refs_2_), channel_id=1, source_target_pairs={{0,7},{1,0},{2,1},{3,2},{4,3},{5,4},{6,5},{7,6},{8,15},{9,8},{10,9... | collective-permute-start | bytes 393224 | tf_op jit(solution)/shard_map/ppermute | solution.py:492
  60.7 3.5 %collective-permute-start.9 = (bf16[8,4,16,128]{3,2,1,0:T(8,128)(2,1)S(1)}, bf16[8,4,16,128]{3,2,1,0:T(8,128)(2,1)S(1)}, u32[]{:S(2)}, u32[]{:S(2)}) collective-permute-start(bf16[8,4,16,128]{3,2,1,0:T(8,128)(2,1)S(1)} %collective-permute-done.8.refs_10_), channel_id=1, source_target_pairs={{0,7},{1,0},{2,1},{3,2},{4,3},{5,4},{6,5},{7,6},{8,15},{9,8},{10,9... | collective-permute-start | bytes 393224 | tf_op jit(solution)/shard_map/ppermute | solution.py:492
  65.2 2.9 %collective-permute-start.3 = (bf16[8,4,16,128]{3,2,1,0:T(8,128)(2,1)S(1)}, bf16[8,4,16,128]{3,2,1,0:T(8,128)(2,1)S(1)}, u32[]{:S(2)}, u32[]{:S(2)}) collective-permute-start(bf16[8,4,16,128]{3,2,1,0:T(8,128)(2,1)S(1)} %collective-permute-done.2.refs_3_), channel_id=1, source_target_pairs={{0,7},{1,0},{2,1},{3,2},{4,3},{5,4},{6,5},{7,6},{8,15},{9,8},{10,9... | collective-permute-start | bytes 393224 | tf_op jit(solution)/shard_map/ppermute | solution.py:492
  68.1 2.8 %collective-permute-start.10 = (bf16[8,4,16,128]{3,2,1,0:T(8,128)(2,1)S(1)}, bf16[8,4,16,128]{3,2,1,0:T(8,128)(2,1)}, u32[]{:S(2)}, u32[]{:S(2)}) collective-permute-start(bf16[8,4,16,128]{3,2,1,0:T(8,128)(2,1)S(1)} %collective-permute-done.9.refs_11_), channel_id=1, source_target_pairs={{0,7},{1,0},{2,1},{3,2},{4,3},{5,4},{6,5},{7,6},{8,15},{9,8},{10,9... | collective-permute-start | bytes 393224 | tf_op jit(solution)/shard_map/ppermute | solution.py:492
  72.4 1.3 collective-permute-done.10.refs_12_
  73.7 5.0 %all-to-all-done.1 = bf16[32,2,16,1536]{3,2,1,0:T(8,128)(2,1)} async-done(((bf16[32,2,16,1536]{3,2,1,0:T(8,128)(2,1)}), bf16[32,2,16,1536]{3,2,1,0:T(8,128)(2,1)}, u32[]{:S(2)}, u32[]{:S(2)}) %all-to-all-start.1) | async-done | bytes 3145760 | tf_op jit(solution)/shard_map/all_to_all | solution.py:523
  78.8 20.5 %attend.1 = (bf16[8,4,2,16,1024]{4,3,2,1,0:T(8,128)(2,1)}, bf16[8,4,16,128]{3,2,1,0:T(8,128)(2,1)}, bf16[8,4,16,128]{3,2,1,0:T(8,128)(2,1)}, bf16[8,4,16,128]{3,...) custom-call(s32[4,8]{1,0:T(4,128)} %copy-done.5, ...), custom_call_target="tpu_custom_call" | custom-call | tf_op jit(solution)/shard_map/attend/pallas_call | solution.py:457
  99.2 5.6 %collective-permute-start.14 = (bf16[8,4,16,128]{3,2,1,0:T(8,128)(2,1)}, bf16[8,4,16,128]{3,2,1,0:T(8,128)(2,1)S(1)}, u32[]{:S(2)}, u32[]{:S(2)}) collective-permute-start(bf16[8,4,16,128]{3,2,1,0:T(8,128)(2,1)} %get-tuple-element.39), channel_id=1, source_target_pairs={{0,7},{1,0},{2,1},{3,2},{4,3},{5,4},{6,5},{7,6},{8,15},{9,8},{10,9... | collective-permute-start | bytes 393224 | tf_op jit(solution)/shard_map/ppermute | solution.py:492
  104.9 6.4 %all-to-all-start.2 = ((bf16[32,2,16,1024]{3,2,1,0:T(8,128)(2,1)}), bf16[32,2,16,1024]{3,2,1,0:T(8,128)(2,1)S(1)}, u32[]{:S(2)}, u32[]{:S(2)}) async-start(bf16[32,2,16,1024]{3,2,1,0:T(8,128)(2,1)} %bitcast.17), calls=%async_computation.2 | async-start | bytes 4194304 | tf_op jit(solution)/shard_map/all_to_all | solution.py:523
  111.6 2.7 %collective-permute-start.21 = (bf16[8,4,16,128]{3,2,1,0:T(8,128)(2,1)S(1)}, bf16[8,4,16,128]{3,2,1,0:T(8,128)(2,1)S(1)}, u32[]{:S(2)}, u32[]{:S(2)}) collective-permute-start(bf16[8,4,16,128]{3,2,1,0:T(8,128)(2,1)S(1)} %copy-done.36), channel_id=1, source_target_pairs={{0,7},{1,0},{2,1},{3,2},{4,3},{5,4},{6,5},{7,6},{8,15},{9,8},{10,9... | collective-permute-start | bytes 393224 | tf_op jit(solution)/shard_map/ppermute | solution.py:492
  114.3 2.7 %collective-permute-start.15 = (bf16[8,4,16,128]{3,2,1,0:T(8,128)(2,1)S(1)}, bf16[8,4,16,128]{3,2,1,0:T(8,128)(2,1)S(1)}, u32[]{:S(2)}, u32[]{:S(2)}) collective-permute-start(bf16[8,4,16,128]{3,2,1,0:T(8,128)(2,1)S(1)} %add_convert_fusion.9), channel_id=1, source_target_pairs={{0,7},{1,0},{2,1},{3,2},{4,3},{5,4},{6,5},{7,6},{8,15},{9,8},{10,9... | collective-permute-start | bytes 393224 | tf_op jit(solution)/shard_map/ppermute | solution.py:492
  117.8 2.7 %collective-permute-start.22 = (bf16[8,4,16,128]{3,2,1,0:T(8,128)(2,1)S(1)}, bf16[8,4,16,128]{3,2,1,0:T(8,128)(2,1)S(1)}, u32[]{:S(2)}, u32[]{:S(2)}) collective-permute-start(bf16[8,4,16,128]{3,2,1,0:T(8,128)(2,1)S(1)} %add_convert_fusion.4), channel_id=1, source_target_pairs={{0,7},{1,0},{2,1},{3,2},{4,3},{5,4},{6,5},{7,6},{8,15},{9,8},{10,9... | collective-permute-start | bytes 393224 | tf_op jit(solution)/shard_map/ppermute | solution.py:492
  120.7 2.7 %collective-permute-start.16 = (bf16[8,4,16,128]{3,2,1,0:T(8,128)(2,1)S(1)}, bf16[8,4,16,128]{3,2,1,0:T(8,128)(2,1)S(1)}, u32[]{:S(2)}, u32[]{:S(2)}) collective-permute-start(bf16[8,4,16,128]{3,2,1,0:T(8,128)(2,1)S(1)} %add_convert_fusion.8), channel_id=1, source_target_pairs={{0,7},{1,0},{2,1},{3,2},{4,3},{5,4},{6,5},{7,6},{8,15},{9,8},{10,9... | collective-permute-start | bytes 393224 | tf_op jit(solution)/shard_map/ppermute | solution.py:492
  123.7 2.7 %collective-permute-start.23 = (bf16[8,4,16,128]{3,2,1,0:T(8,128)(2,1)S(1)}, bf16[8,4,16,128]{3,2,1,0:T(8,128)(2,1)S(1)}, u32[]{:S(2)}, u32[]{:S(2)}) collective-permute-start(bf16[8,4,16,128]{3,2,1,0:T(8,128)(2,1)S(1)} %add_convert_fusion.3), channel_id=1, source_target_pairs={{0,7},{1,0},{2,1},{3,2},{4,3},{5,4},{6,5},{7,6},{8,15},{9,8},{10,9... | collective-permute-start | bytes 393224 | tf_op jit(solution)/shard_map/ppermute | solution.py:492
  126.6 2.7 %collective-permute-start.17 = (bf16[8,4,16,128]{3,2,1,0:T(8,128)(2,1)S(1)}, bf16[8,4,16,128]{3,2,1,0:T(8,128)(2,1)S(1)}, u32[]{:S(2)}, u32[]{:S(2)}) collective-permute-start(bf16[8,4,16,128]{3,2,1,0:T(8,128)(2,1)S(1)} %add_convert_fusion.7), channel_id=1, source_target_pairs={{0,7},{1,0},{2,1},{3,2},{4,3},{5,4},{6,5},{7,6},{8,15},{9,8},{10,9... | collective-permute-start | bytes 393224 | tf_op jit(solution)/shard_map/ppermute | solution.py:492
  129.4 3.3 %collective-permute-start.24 = (bf16[8,4,16,128]{3,2,1,0:T(8,128)(2,1)S(1)}, bf16[8,4,16,128]{3,2,1,0:T(8,128)(2,1)S(1)}, u32[]{:S(2)}, u32[]{:S(2)}) collective-permute-start(bf16[8,4,16,128]{3,2,1,0:T(8,128)(2,1)S(1)} %add_convert_fusion.2), channel_id=1, source_target_pairs={{0,7},{1,0},{2,1},{3,2},{4,3},{5,4},{6,5},{7,6},{8,15},{9,8},{10,9... | collective-permute-start | bytes 393224 | tf_op jit(solution)/shard_map/ppermute | solution.py:492
  133.0 2.7 %collective-permute-done.24.va = bf16[8,4,16,128]{3,2,1,0:T(8,128)(2,1)S(1)} collective-permute-done((bf16[8,4,16,128]{3,2,1,0:T(8,128)(2,1)S(1)}, bf16[8,4,16,128]{3,2,1,0:T(8,128)(2,1)S(1)}, u32[]{:S(2)}, u32[]{:S(2)}) %collective-permute-start.24) | collective-permute-done | bytes 131104 | tf_op jit(solution)/shard_map/ppermute | solution.py:492
  135.7 1.5 place_pair.1
  137.2 1.1 all-to-all-done.2
  138.3 9.6 %all-to-all-start.3 = ((bf16[32,2,16,256]{3,2,1,0:T(8,128)(2,1)}), bf16[32,2,16,256]{3,2,1,0:T(8,128)(2,1)S(1)}, u32[]{:S(2)}, u32[]{:S(2)}) async-start(bf16[32,2,16,256]{3,2,1,0:T(8,128)(2,1)} %bitcast.9), calls=%async_computation.3 | async-start | bytes 1048576 | tf_op jit(solution)/shard_map/all_to_all | solution.py:523
  147.9 3.1 %home_wide.1 = bf16[128,4096]{1,0:T(8,128)(2,1)} custom-call(s32[64]{0:T(128)} %dest.6, bf16[8,4,2,16,1024]{4,3,2,1,0:T(8,128)(2,1)} %bitcast.15), custom_call_target="tpu_custom_call" | custom-call | tf_op jit(solution)/shard_map/home_wide/pallas_call | solution.py:208
  151.0 7.9 %all-to-all-done.3 = bf16[32,2,16,256]{3,2,1,0:T(8,128)(2,1)S(1)} async-done(((bf16[32,2,16,256]{3,2,1,0:T(8,128)(2,1)}), bf16[32,2,16,256]{3,2,1,0:T(8,128)(2,1)S(1)}, u32[]{:S(2)}, u32[]{:S(2)}) %all-to-all-start.3) | async-done | bytes 524320 | tf_op jit(solution)/shard_map/all_to_all | solution.py:523
  159.0 1.3 home_pair.1
  (137 shorter events, 9.4 us)
Async XLA Ops:
  3.8 30.1 %all-to-all-start = ((bf16[32,2,16,768]{3,2,1,0:T(8,128)(2,1)}), bf16[32,2,16,768]{3,2,1,0:T(8,128)(2,1)S(1)}, u32[]{:S(2)}, u32[]{:S(2)}) async-start(bf16[32,2,16,768]{3,2,1,0:T(8,128)(2,1)} %bitcast.16), calls=%async_computation | async-start | bytes 3145728 | tf_op jit(solution)/shard_map/all_to_all | solution.py:523
  33.8 44.9 %all-to-all-start.1 = ((bf16[32,2,16,1536]{3,2,1,0:T(8,128)(2,1)}), bf16[32,2,16,1536]{3,2,1,0:T(8,128)(2,1)}, u32[]{:S(2)}, u32[]{:S(2)}) async-start(bf16[32,2,16,1536]{3,2,1,0:T(8,128)(2,1)} %bitcast.14), calls=%async_computation.1 | async-start | bytes 6291456 | tf_op jit(solution)/shard_map/all_to_all | solution.py:523
  43.1 8.1 %collective-permute-start = (bf16[8,4,16,128]{3,2,1,0:T(8,128)(2,1)S(1)}, bf16[8,4,16,128]{3,2,1,0:T(8,128)(2,1)S(1)}, u32[]{:S(2)}, u32[]{:S(2)}) collective-permute-start(bf16[8,4,16,128]{3,2,1,0:T(8,128)(2,1)S(1)} %get-tuple-element.36.refs_0_), channel_id=1, source_target_pairs={{0,7},{1,0},{2,1},{3,2},{4,3},{5,4},{6,5},{7,6},{8,15},{9,8},{10,9... | collective-permute-start | bytes 393224 | tf_op jit(solution)/shard_map/ppermute | solution.py:492
  48.7 6.0 %collective-permute-start.7 = (bf16[8,4,16,128]{3,2,1,0:T(8,128)(2,1)S(1)}, bf16[8,4,16,128]{3,2,1,0:T(8,128)(2,1)S(1)}, u32[]{:S(2)}, u32[]{:S(2)}) collective-permute-start(bf16[8,4,16,128]{3,2,1,0:T(8,128)(2,1)S(1)} %get-tuple-element.37.refs_8_), channel_id=1, source_target_pairs={{0,7},{1,0},{2,1},{3,2},{4,3},{5,4},{6,5},{7,6},{8,15},{9,8},{10,9... | collective-permute-start | bytes 393224 | tf_op jit(solution)/shard_map/ppermute | solution.py:492
  49.4 8.1 %collective-permute-start.4 = (bf16[8,4,16,128]{3,2,1,0:T(8,128)(2,1)S(1)}, bf16[8,4,16,128]{3,2,1,0:T(8,128)(2,1)S(1)}, u32[]{:S(2)}, u32[]{:S(2)}) collective-permute-start(bf16[8,4,16,128]{3,2,1,0:T(8,128)(2,1)S(1)} %get-tuple-element.36.refs_0_), channel_id=1, source_target_pairs={{0,1},{1,2},{2,3},{3,4},{4,5},{5,6},{6,7},{7,0},{8,9},{9,10},{10,1... | collective-permute-start | bytes 393224 | tf_op jit(solution)/shard_map/ppermute | solution.py:492
  50.1 7.4 %collective-permute-start.11 = (bf16[8,4,16,128]{3,2,1,0:T(8,128)(2,1)S(1)}, bf16[8,4,16,128]{3,2,1,0:T(8,128)(2,1)S(1)}, u32[]{:S(2)}, u32[]{:S(2)}) collective-permute-start(bf16[8,4,16,128]{3,2,1,0:T(8,128)(2,1)S(1)} %get-tuple-element.37.refs_8_), channel_id=1, source_target_pairs={{0,1},{1,2},{2,3},{3,4},{4,5},{5,6},{6,7},{7,0},{8,9},{9,10},{10,1... | collective-permute-start | bytes 393224 | tf_op jit(solution)/shard_map/ppermute | solution.py:492
  51.2 6.5 %collective-permute-start.1 = (bf16[8,4,16,128]{3,2,1,0:T(8,128)(2,1)S(1)}, bf16[8,4,16,128]{3,2,1,0:T(8,128)(2,1)S(1)}, u32[]{:S(2)}, u32[]{:S(2)}) collective-permute-start(bf16[8,4,16,128]{3,2,1,0:T(8,128)(2,1)S(1)} %collective-permute-done.refs_1_), channel_id=1, source_target_pairs={{0,7},{1,0},{2,1},{3,2},{4,3},{5,4},{6,5},{7,6},{8,15},{9,8},{10,9... | collective-permute-start | bytes 393224 | tf_op jit(solution)/shard_map/ppermute | solution.py:492
  54.7 6.0 %collective-permute-start.8 = (bf16[8,4,16,128]{3,2,1,0:T(8,128)(2,1)S(1)}, bf16[8,4,16,128]{3,2,1,0:T(8,128)(2,1)S(1)}, u32[]{:S(2)}, u32[]{:S(2)}) collective-permute-start(bf16[8,4,16,128]{3,2,1,0:T(8,128)(2,1)S(1)} %collective-permute-done.7.refs_9_), channel_id=1, source_target_pairs={{0,7},{1,0},{2,1},{3,2},{4,3},{5,4},{6,5},{7,6},{8,15},{9,8},{10,9... | collective-permute-start | bytes 393224 | tf_op jit(solution)/shard_map/ppermute | solution.py:492
  57.5 6.7 %collective-permute-start.5 = (bf16[8,4,16,128]{3,2,1,0:T(8,128)(2,1)S(1)}, bf16[8,4,16,128]{3,2,1,0:T(8,128)(2,1)S(1)}, u32[]{:S(2)}, u32[]{:S(2)}) collective-permute-start(bf16[8,4,16,128]{3,2,1,0:T(8,128)(2,1)S(1)} %collective-permute-done.4.refs_7_), channel_id=1, source_target_pairs={{0,1},{1,2},{2,3},{3,4},{4,5},{5,6},{6,7},{7,0},{8,9},{9,10},{10,1... | collective-permute-start | bytes 393224 | tf_op jit(solution)/shard_map/ppermute | solution.py:492
  57.6 7.6 %collective-permute-start.12 = (bf16[8,4,16,128]{3,2,1,0:T(8,128)(2,1)S(1)}, bf16[8,4,16,128]{3,2,1,0:T(8,128)(2,1)S(1)}, u32[]{:S(2)}, u32[]{:S(2)}) collective-permute-start(bf16[8,4,16,128]{3,2,1,0:T(8,128)(2,1)S(1)} %collective-permute-done.11.refs_15_), channel_id=1, source_target_pairs={{0,1},{1,2},{2,3},{3,4},{4,5},{5,6},{6,7},{7,0},{8,9},{9,10},{10,1... | collective-permute-start | bytes 393224 | tf_op jit(solution)/shard_map/ppermute | solution.py:492
  57.6 7.6 %collective-permute-start.2 = (bf16[8,4,16,128]{3,2,1,0:T(8,128)(2,1)S(1)}, bf16[8,4,16,128]{3,2,1,0:T(8,128)(2,1)S(1)}, u32[]{:S(2)}, u32[]{:S(2)}) collective-permute-start(bf16[8,4,16,128]{3,2,1,0:T(8,128)(2,1)S(1)} %collective-permute-done.1.refs_2_), channel_id=1, source_target_pairs={{0,7},{1,0},{2,1},{3,2},{4,3},{5,4},{6,5},{7,6},{8,15},{9,8},{10,9... | collective-permute-start | bytes 393224 | tf_op jit(solution)/shard_map/ppermute | solution.py:492
  60.7 7.4 %collective-permute-start.9 = (bf16[8,4,16,128]{3,2,1,0:T(8,128)(2,1)S(1)}, bf16[8,4,16,128]{3,2,1,0:T(8,128)(2,1)S(1)}, u32[]{:S(2)}, u32[]{:S(2)}) collective-permute-start(bf16[8,4,16,128]{3,2,1,0:T(8,128)(2,1)S(1)} %collective-permute-done.8.refs_10_), channel_id=1, source_target_pairs={{0,7},{1,0},{2,1},{3,2},{4,3},{5,4},{6,5},{7,6},{8,15},{9,8},{10,9... | collective-permute-start | bytes 393224 | tf_op jit(solution)/shard_map/ppermute | solution.py:492
  64.2 6.7 %collective-permute-start.6 = (bf16[8,4,16,128]{3,2,1,0:T(8,128)(2,1)S(1)}, bf16[8,4,16,128]{3,2,1,0:T(8,128)(2,1)S(1)}, u32[]{:S(2)}, u32[]{:S(2)}) collective-permute-start(bf16[8,4,16,128]{3,2,1,0:T(8,128)(2,1)S(1)} %collective-permute-done.5.refs_6_), channel_id=1, source_target_pairs={{0,1},{1,2},{2,3},{3,4},{4,5},{5,6},{6,7},{7,0},{8,9},{9,10},{10,1... | collective-permute-start | bytes 393224 | tf_op jit(solution)/shard_map/ppermute | solution.py:492
  65.2 5.9 %collective-permute-start.13 = (bf16[8,4,16,128]{3,2,1,0:T(8,128)(2,1)S(1)}, bf16[8,4,16,128]{3,2,1,0:T(8,128)(2,1)S(1)}, u32[]{:S(2)}, u32[]{:S(2)}) collective-permute-start(bf16[8,4,16,128]{3,2,1,0:T(8,128)(2,1)S(1)} %collective-permute-done.12.refs_14_), channel_id=1, source_target_pairs={{0,1},{1,2},{2,3},{3,4},{4,5},{5,6},{6,7},{7,0},{8,9},{9,10},{10,1... | collective-permute-start | bytes 393224 | tf_op jit(solution)/shard_map/ppermute | solution.py:492
  65.2 5.8 %collective-permute-start.3 = (bf16[8,4,16,128]{3,2,1,0:T(8,128)(2,1)S(1)}, bf16[8,4,16,128]{3,2,1,0:T(8,128)(2,1)S(1)}, u32[]{:S(2)}, u32[]{:S(2)}) collective-permute-start(bf16[8,4,16,128]{3,2,1,0:T(8,128)(2,1)S(1)} %collective-permute-done.2.refs_3_), channel_id=1, source_target_pairs={{0,7},{1,0},{2,1},{3,2},{4,3},{5,4},{6,5},{7,6},{8,15},{9,8},{10,9... | collective-permute-start | bytes 393224 | tf_op jit(solution)/shard_map/ppermute | solution.py:492
  68.1 5.5 %collective-permute-start.10 = (bf16[8,4,16,128]{3,2,1,0:T(8,128)(2,1)S(1)}, bf16[8,4,16,128]{3,2,1,0:T(8,128)(2,1)}, u32[]{:S(2)}, u32[]{:S(2)}) collective-permute-start(bf16[8,4,16,128]{3,2,1,0:T(8,128)(2,1)S(1)} %collective-permute-done.9.refs_11_), channel_id=1, source_target_pairs={{0,7},{1,0},{2,1},{3,2},{4,3},{5,4},{6,5},{7,6},{8,15},{9,8},{10,9... | collective-permute-start | bytes 393224 | tf_op jit(solution)/shard_map/ppermute | solution.py:492
  99.2 15.0 %collective-permute-start.14 = (bf16[8,4,16,128]{3,2,1,0:T(8,128)(2,1)}, bf16[8,4,16,128]{3,2,1,0:T(8,128)(2,1)S(1)}, u32[]{:S(2)}, u32[]{:S(2)}) collective-permute-start(bf16[8,4,16,128]{3,2,1,0:T(8,128)(2,1)} %get-tuple-element.39), channel_id=1, source_target_pairs={{0,7},{1,0},{2,1},{3,2},{4,3},{5,4},{6,5},{7,6},{8,15},{9,8},{10,9... | collective-permute-start | bytes 393224 | tf_op jit(solution)/shard_map/ppermute | solution.py:492
  104.9 33.4 %all-to-all-start.2 = ((bf16[32,2,16,1024]{3,2,1,0:T(8,128)(2,1)}), bf16[32,2,16,1024]{3,2,1,0:T(8,128)(2,1)S(1)}, u32[]{:S(2)}, u32[]{:S(2)}) async-start(bf16[32,2,16,1024]{3,2,1,0:T(8,128)(2,1)} %bitcast.17), calls=%async_computation.2 | async-start | bytes 4194304 | tf_op jit(solution)/shard_map/all_to_all | solution.py:523
  111.5 6.2 %collective-permute-start.18 = (bf16[8,4,16,128]{3,2,1,0:T(8,128)(2,1)S(1)}, bf16[8,4,16,128]{3,2,1,0:T(8,128)(2,1)S(1)}, u32[]{:S(2)}, u32[]{:S(2)}) collective-permute-start(bf16[8,4,16,128]{3,2,1,0:T(8,128)(2,1)S(1)} %copy-done.37), channel_id=1, source_target_pairs={{0,1},{1,2},{2,3},{3,4},{4,5},{5,6},{6,7},{7,0},{8,9},{9,10},{10,1... | collective-permute-start | bytes 393224 | tf_op jit(solution)/shard_map/ppermute | solution.py:492
  111.6 6.2 %collective-permute-start.21 = (bf16[8,4,16,128]{3,2,1,0:T(8,128)(2,1)S(1)}, bf16[8,4,16,128]{3,2,1,0:T(8,128)(2,1)S(1)}, u32[]{:S(2)}, u32[]{:S(2)}) collective-permute-start(bf16[8,4,16,128]{3,2,1,0:T(8,128)(2,1)S(1)} %copy-done.36), channel_id=1, source_target_pairs={{0,7},{1,0},{2,1},{3,2},{4,3},{5,4},{6,5},{7,6},{8,15},{9,8},{10,9... | collective-permute-start | bytes 393224 | tf_op jit(solution)/shard_map/ppermute | solution.py:492
  114.2 6.3 %collective-permute-start.25 = (bf16[8,4,16,128]{3,2,1,0:T(8,128)(2,1)S(1)}, bf16[8,4,16,128]{3,2,1,0:T(8,128)(2,1)S(1)}, u32[]{:S(2)}, u32[]{:S(2)}) collective-permute-start(bf16[8,4,16,128]{3,2,1,0:T(8,128)(2,1)S(1)} %copy-done.35), channel_id=1, source_target_pairs={{0,1},{1,2},{2,3},{3,4},{4,5},{5,6},{6,7},{7,0},{8,9},{9,10},{10,1... | collective-permute-start | bytes 393224 | tf_op jit(solution)/shard_map/ppermute | solution.py:492
  114.3 6.4 %collective-permute-start.15 = (bf16[8,4,16,128]{3,2,1,0:T(8,128)(2,1)S(1)}, bf16[8,4,16,128]{3,2,1,0:T(8,128)(2,1)S(1)}, u32[]{:S(2)}, u32[]{:S(2)}) collective-permute-start(bf16[8,4,16,128]{3,2,1,0:T(8,128)(2,1)S(1)} %add_convert_fusion.9), channel_id=1, source_target_pairs={{0,7},{1,0},{2,1},{3,2},{4,3},{5,4},{6,5},{7,6},{8,15},{9,8},{10,9... | collective-permute-start | bytes 393224 | tf_op jit(solution)/shard_map/ppermute | solution.py:492
  117.7 5.8 %collective-permute-start.19 = (bf16[8,4,16,128]{3,2,1,0:T(8,128)(2,1)S(1)}, bf16[8,4,16,128]{3,2,1,0:T(8,128)(2,1)S(1)}, u32[]{:S(2)}, u32[]{:S(2)}) collective-permute-start(bf16[8,4,16,128]{3,2,1,0:T(8,128)(2,1)S(1)} %add_convert_fusion.6), channel_id=1, source_target_pairs={{0,1},{1,2},{2,3},{3,4},{4,5},{5,6},{6,7},{7,0},{8,9},{9,10},{10,1... | collective-permute-start | bytes 393224 | tf_op jit(solution)/shard_map/ppermute | solution.py:492
  117.8 5.8 %collective-permute-start.22 = (bf16[8,4,16,128]{3,2,1,0:T(8,128)(2,1)S(1)}, bf16[8,4,16,128]{3,2,1,0:T(8,128)(2,1)S(1)}, u32[]{:S(2)}, u32[]{:S(2)}) collective-permute-start(bf16[8,4,16,128]{3,2,1,0:T(8,128)(2,1)S(1)} %add_convert_fusion.4), channel_id=1, source_target_pairs={{0,7},{1,0},{2,1},{3,2},{4,3},{5,4},{6,5},{7,6},{8,15},{9,8},{10,9... | collective-permute-start | bytes 393224 | tf_op jit(solution)/shard_map/ppermute | solution.py:492
  120.6 5.8 %collective-permute-start.26 = (bf16[8,4,16,128]{3,2,1,0:T(8,128)(2,1)S(1)}, bf16[8,4,16,128]{3,2,1,0:T(8,128)(2,1)S(1)}, u32[]{:S(2)}, u32[]{:S(2)}) collective-permute-start(bf16[8,4,16,128]{3,2,1,0:T(8,128)(2,1)S(1)} %add_convert_fusion.1), channel_id=1, source_target_pairs={{0,1},{1,2},{2,3},{3,4},{4,5},{5,6},{6,7},{7,0},{8,9},{9,10},{10,1... | collective-permute-start | bytes 393224 | tf_op jit(solution)/shard_map/ppermute | solution.py:492
  120.7 5.8 %collective-permute-start.16 = (bf16[8,4,16,128]{3,2,1,0:T(8,128)(2,1)S(1)}, bf16[8,4,16,128]{3,2,1,0:T(8,128)(2,1)S(1)}, u32[]{:S(2)}, u32[]{:S(2)}) collective-permute-start(bf16[8,4,16,128]{3,2,1,0:T(8,128)(2,1)S(1)} %add_convert_fusion.8), channel_id=1, source_target_pairs={{0,7},{1,0},{2,1},{3,2},{4,3},{5,4},{6,5},{7,6},{8,15},{9,8},{10,9... | collective-permute-start | bytes 393224 | tf_op jit(solution)/shard_map/ppermute | solution.py:492
  123.5 9.2 %collective-permute-start.20 = (bf16[8,4,16,128]{3,2,1,0:T(8,128)(2,1)S(1)}, bf16[8,4,16,128]{3,2,1,0:T(8,128)(2,1)S(1)}, u32[]{:S(2)}, u32[]{:S(2)}) collective-permute-start(bf16[8,4,16,128]{3,2,1,0:T(8,128)(2,1)S(1)} %add_convert_fusion.5), channel_id=1, source_target_pairs={{0,1},{1,2},{2,3},{3,4},{4,5},{5,6},{6,7},{7,0},{8,9},{9,10},{10,1... | collective-permute-start | bytes 393224 | tf_op jit(solution)/shard_map/ppermute | solution.py:492
  123.7 5.7 %collective-permute-start.23 = (bf16[8,4,16,128]{3,2,1,0:T(8,128)(2,1)S(1)}, bf16[8,4,16,128]{3,2,1,0:T(8,128)(2,1)S(1)}, u32[]{:S(2)}, u32[]{:S(2)}) collective-permute-start(bf16[8,4,16,128]{3,2,1,0:T(8,128)(2,1)S(1)} %add_convert_fusion.3), channel_id=1, source_target_pairs={{0,7},{1,0},{2,1},{3,2},{4,3},{5,4},{6,5},{7,6},{8,15},{9,8},{10,9... | collective-permute-start | bytes 393224 | tf_op jit(solution)/shard_map/ppermute | solution.py:492
  126.5 6.6 %collective-permute-start.27 = (bf16[8,4,16,128]{3,2,1,0:T(8,128)(2,1)S(1)}, bf16[8,4,16,128]{3,2,1,0:T(8,128)(2,1)S(1)}, u32[]{:S(2)}, u32[]{:S(2)}) collective-permute-start(bf16[8,4,16,128]{3,2,1,0:T(8,128)(2,1)S(1)} %add_convert_fusion), channel_id=1, source_target_pairs={{0,1},{1,2},{2,3},{3,4},{4,5},{5,6},{6,7},{7,0},{8,9},{9,10},{10,1... | collective-permute-start | bytes 393224 | tf_op jit(solution)/shard_map/ppermute | solution.py:492
  126.6 6.4 %collective-permute-start.17 = (bf16[8,4,16,128]{3,2,1,0:T(8,128)(2,1)S(1)}, bf16[8,4,16,128]{3,2,1,0:T(8,128)(2,1)S(1)}, u32[]{:S(2)}, u32[]{:S(2)}) collective-permute-start(bf16[8,4,16,128]{3,2,1,0:T(8,128)(2,1)S(1)} %add_convert_fusion.7), channel_id=1, source_target_pairs={{0,7},{1,0},{2,1},{3,2},{4,3},{5,4},{6,5},{7,6},{8,15},{9,8},{10,9... | collective-permute-start | bytes 393224 | tf_op jit(solution)/shard_map/ppermute | solution.py:492
  129.4 6.4 %collective-permute-start.24 = (bf16[8,4,16,128]{3,2,1,0:T(8,128)(2,1)S(1)}, bf16[8,4,16,128]{3,2,1,0:T(8,128)(2,1)S(1)}, u32[]{:S(2)}, u32[]{:S(2)}) collective-permute-start(bf16[8,4,16,128]{3,2,1,0:T(8,128)(2,1)S(1)} %add_convert_fusion.2), channel_id=1, source_target_pairs={{0,7},{1,0},{2,1},{3,2},{4,3},{5,4},{6,5},{7,6},{8,15},{9,8},{10,9... | collective-permute-start | bytes 393224 | tf_op jit(solution)/shard_map/ppermute | solution.py:492
  138.3 20.6 %all-to-all-start.3 = ((bf16[32,2,16,256]{3,2,1,0:T(8,128)(2,1)}), bf16[32,2,16,256]{3,2,1,0:T(8,128)(2,1)S(1)}, u32[]{:S(2)}, u32[]{:S(2)}) async-start(bf16[32,2,16,256]{3,2,1,0:T(8,128)(2,1)} %bitcast.9), calls=%async_computation.3 | async-start | bytes 1048576 | tf_op jit(solution)/shard_map/all_to_all | solution.py:523
  (38 other events, 539.1 us)
